TPU v7x, 256 devices: a whole 4x4x8 slice. The times are simulated.
256 devices in a mesh: gx: 2 (over z_lo), gy: 2 (over core), gz: 64 (over y, z_hi, x).
Axes of the slice: x: 4, y: 4, z: 8 (z_hi: 4, z_lo: 2; z = z_hi * 2 + z_lo), core: 2. Of those that a mesh axis runs over, the one named last changes fastest.
Arguments:
- phase: float32 [256, 64, 256], P('gz', 'gx', 'gy'), may hold values from -2 to 2
- velocity: float32 [3, 256, 64, 256], P(None, 'gz', 'gx', 'gy'), may hold values from -3 to 3
- phase_obs: float32 [256, 64, 256], P('gz', 'gx', 'gy'), may hold values from -2 to 2
- velocity_obs: float32 [3, 256, 64, 256], P(None, 'gz', 'gx', 'gy'), may hold values from -3 to 3
- coefs: float32 [4], replicated, may hold values from 0.5 to 2
Outputs:
- phase_back: float32 [256, 64, 256], P('gz', 'gx', 'gy')
- velocity_back: float32 [3, 256, 64, 256], P(None, 'gz', 'gx', 'gy')
- param_grads: float32 [4], replicated
All inputs are finite; a program needn't handle non-finite values.
Results may differ from a plain program's by a relative error of at most 0.00045.
Values sent between devices are 32-bit elements; how exact they have to be, the bound alone decides.
No kernel may reach another device: no remote copies, remote signals or barrier semaphores. Data moves between devices by JAX's collectives and lax.ppermute only.
A program may use at most 64 MiB of HBM per device.

v0:
```python
import jax
import jax.numpy as jnp
from jax import lax
from jax.sharding import PartitionSpec as P

ITERS = 2


DT = 0.1
SHIFT = 0.01
FORWARD = ((1, 0, 0), (0, 1, 0), (0, 0, 1))
BACKWARD = ((-1, 0, 0), (0, -1, 0), (0, 0, -1))
CENTRE = (0, 0, 0)


def extended(block, sides, width):
    for axis, dim in sides:
        count = lax.axis_size(axis)
        forward = [(i, i + 1) for i in range(count - 1)]
        forward.append((count - 1, 0))
        backward = [(target, source) for source, target in forward]
        low = lax.ppermute(
            lax.slice_in_dim(block, block.shape[dim] - width, None, axis=dim), axis, forward
        )
        high = lax.ppermute(lax.slice_in_dim(block, 0, width, axis=dim), axis, backward)
        block = jnp.concatenate([low, block, high], axis=dim)
    return block


def offset_view(padded, shifts):
    index = [slice(None)] * (padded.ndim - 3)
    for place in range(3):
        extent = padded.shape[padded.ndim - 3 + place]
        index.append(slice(1 + shifts[place], extent - 1 + shifts[place]))
    return padded[tuple(index)]


def laplace(padded):
    total = -6.0 * offset_view(padded, CENTRE)
    for axis in range(3):
        total = total + offset_view(padded, FORWARD[axis]) + offset_view(padded, BACKWARD[axis])
    return total


def centred(padded, axis):
    return (offset_view(padded, FORWARD[axis]) - offset_view(padded, BACKWARD[axis])) * 0.5


def gradient(padded):
    return jnp.stack([centred(padded, axis) for axis in range(3)])


def divergence(padded):
    return centred(padded[0], 0) + centred(padded[1], 1) + centred(padded[2], 2)


def scalar_rim(field):
    return extended(field, (("gx", 1), ("gy", 2), ("gz", 0)), 1)


def global_sum(value):
    return lax.psum(value, ("gx", "gy", "gz"))


def norm_sum(value):
    return lax.psum(value, ("gx", "gy", "gz"))


def solve(source):
    solution = jnp.zeros_like(source)
    residual = source
    direction = source
    norm_now = norm_sum(jnp.sum(residual * residual))
    for step in range(ITERS):
        image = SHIFT * direction - laplace(scalar_rim(direction))
        alpha = norm_now / global_sum(jnp.sum(direction * image))
        solution = solution + alpha * direction
        residual = residual - alpha * image
        norm_next = norm_sum(jnp.sum(residual * residual))
        direction = residual + norm_next / norm_now * direction
        norm_now = norm_next
    return solution


def local(phase, velocity, phase_obs, velocity_obs, coefs):
    mobility = 0.1 * coefs[0]
    tension = 0.5 * coefs[1]
    viscosity = 0.1 * coefs[2]
    interface = 0.5 * coefs[3]
    vel_pad = extended(velocity, (("gx", 2), ("gy", 3), ("gz", 1)), 1)
    phase_pad = extended(phase, (("gx", 1), ("gy", 2), ("gz", 0)), 1)
    lap_phase = laplace(phase_pad)
    potential_here = phase * phase * phase - phase - interface * lap_phase
    potential_pad = extended(potential_here, (("gx", 1), ("gy", 2), ("gz", 0)), 1)
    potential = offset_view(potential_pad, CENTRE)
    lap_potential = laplace(potential_pad)
    phase_grad = gradient(phase_pad)
    vel_grad = jnp.stack([centred(vel_pad, axis) for axis in range(3)])
    advect = jnp.sum(velocity[:, None] * vel_grad, axis=0)
    lap_vel = laplace(vel_pad)
    provisional = (
        velocity - DT * advect + DT * viscosity * lap_vel + DT * tension * potential * phase_grad
    )
    prov_pad = extended(provisional, (("gx", 2), ("gy", 3), ("gz", 1)), 1)
    pressure = solve(-divergence(prov_pad))
    pressure_pad = extended(pressure, (("gx", 1), ("gy", 2), ("gz", 0)), 1)
    new_velocity = provisional - gradient(pressure_pad)
    new_phase = phase - DT * jnp.sum(velocity * phase_grad, axis=0) + DT * mobility * lap_potential
    misfit = jnp.concatenate([(new_phase - phase_obs)[None], new_velocity - velocity_obs], axis=0)
    misfit_pad = extended(misfit, (("gx", 2), ("gy", 3), ("gz", 1)), 1)
    phase_adj_pad = misfit_pad[0]
    phase_adj = offset_view(phase_adj_pad, CENTRE)
    velocity_adj = offset_view(misfit_pad[1:], CENTRE)
    source_adj = solve(divergence(misfit_pad[1:]))
    source_pad = extended(source_adj, (("gx", 1), ("gy", 2), ("gz", 0)), 1)
    prov_adj = velocity_adj + gradient(source_pad)
    prov_adj_pad = extended(prov_adj, (("gx", 2), ("gy", 3), ("gz", 1)), 1)
    potential_adj = DT * mobility * laplace(phase_adj_pad) + DT * tension * jnp.sum(
        prov_adj * phase_grad, axis=0
    )
    pot_adj_pad = extended(potential_adj, (("gx", 1), ("gy", 2), ("gz", 0)), 1)
    phase_back = (
        phase_adj
        + DT * divergence(vel_pad * phase_adj_pad[None])
        + (3.0 * phase * phase - 1.0) * potential_adj
        - interface * laplace(pot_adj_pad)
        - DT * tension * divergence(potential_pad[None] * prov_adj_pad)
    )
    transport = centred(vel_pad[0][None] * prov_adj_pad, 0)
    transport = transport + centred(vel_pad[1][None] * prov_adj_pad, 1)
    transport = transport + centred(vel_pad[2][None] * prov_adj_pad, 2)
    velocity_back = (
        prov_adj
        - DT * phase_adj[None] * phase_grad
        - DT * jnp.sum(prov_adj[None] * vel_grad, axis=1)
        + DT * transport
        + DT * viscosity * laplace(prov_adj_pad)
    )
    partial_value = jnp.stack(
        [
            DT * jnp.sum(phase_adj * lap_potential),
            DT * jnp.sum(prov_adj * potential * phase_grad),
            DT * jnp.sum(prov_adj * lap_vel),
            -jnp.sum(potential_adj * lap_phase),
        ]
    )
    totals = lax.psum(partial_value, ("gx", "gy", "gz"))
    cell_count = phase.size * lax.axis_size("gx") * lax.axis_size("gy") * lax.axis_size("gz")
    return (phase_back, velocity_back, totals / cell_count)


def solution(mesh):
    return jax.shard_map(
        local,
        mesh=mesh,
        in_specs=(
            P("gz", "gx", "gy"),
            P(None, "gz", "gx", "gy"),
            P("gz", "gx", "gy"),
            P(None, "gz", "gx", "gy"),
            P(),
        ),
        out_specs=(P("gz", "gx", "gy"), P(None, "gz", "gx", "gy"), P()),
        check_vma=False,
    )
```

profile of v0, /device:TPU:1, one launch (start us, length us, event | category | flops | bytes accessed | tf_op | source)
XLA Modules:
  0.0 788.5 jit_solution(6380719982318013957)
XLA Ops:
  13.5 9.0 %collective-permute-start.4 = (f32[1,34,130]{2,1,0:T(8,128)S(1)}, f32[1,34,130]{2,1,0:T(8,128)S(1)}, u32[]{:S(2)}, u32[]{:S(2)}) collective-permute-start(f32[1,34,130]{2,1,0:T(8,128)S(1)} %get-tuple-element.97), channel_id=1, source_target_pairs={{1,0},{2,1},{3,2},{4,3},{5,4},{6,5},{7,6},{8,7},{9,8},{10,9},{11,1... | collective-permute-start | bytes 53048 | tf_op jit(solution)/shard_map/ppermute | solution.py:25
  25.1 8.1 %collective-permute-start.16 = (f32[3,1,34,130]{3,2,1,0:T(8,128)S(1)}, f32[3,1,34,130]{3,2,1,0:T(8,128)S(1)}, u32[]{:S(2)}, u32[]{:S(2)}) collective-permute-start(f32[3,1,34,130]{3,2,1,0:T(8,128)S(1)} %get-tuple-element.65), channel_id=1, source_target_pairs={{1,0},{2,1},{3,2},{4,3},{5,4},{6,5},{7,6},{8,7},{9,8},{10,9},{11,1... | collective-permute-start | bytes 159128 | tf_op jit(solution)/shard_map/ppermute | solution.py:25
  34.4 4.1 collective-permute-done.16
  38.5 5.4 collective-permute-done.17
  57.2 7.8 collective-permute-start.23
  77.2 7.5 collective-permute-start.28
  85.8 8.1 %collective-permute-done.29 = f32[1,34,130]{2,1,0:T(8,128)S(1)} collective-permute-done((f32[1,34,130]{2,1,0:T(8,128)S(1)}, f32[1,34,130]{2,1,0:T(8,128)S(1)}, u32[]{:S(2)}, u32[]{:S(2)}) %collective-permute-start.29) | collective-permute-done | bytes 17712 | tf_op jit(solution)/shard_map/ppermute | solution.py:22
  94.7 72.9 %all-reduce.1 = (f32[]{:T(128)}, f32[]{:T(128)}) all-reduce(f32[]{:T(128)} %get-tuple-element.9, f32[]{:T(128)} %get-tuple-element.8), channel_id=1, replica_groups=mesh['gx'=2,'gy'=2,'gz'=64] {'gx','gy','gz'}, use_global_device_ids=true, to_apply=%region_3.0 | all-reduce | flops 2 | bytes 16 | tf_op jit(solution)/shard_map/psum | solution.py:66
  170.3 73.7 %psum.65 = f32[]{:T(128)} all-reduce(f32[]{:T(128)} %multiply_reduce_fusion.11), channel_id=1, replica_groups=mesh['gx'=2,'gy'=2,'gz'=64] {'gx','gy','gz'}, use_global_device_ids=true, to_apply=%region_7.0 | all-reduce | flops 1 | bytes 8 | tf_op jit(solution)/shard_map/psum | solution.py:66
  256.9 7.8 collective-permute-done.35
  267.4 72.5 %psum.66 = f32[]{:T(128)} all-reduce(f32[]{:T(128)} %fusion.74), channel_id=1, replica_groups=mesh['gx'=2,'gy'=2,'gz'=64] {'gx','gy','gz'}, use_global_device_ids=true, to_apply=%region_9.0 | all-reduce | flops 1 | bytes 8 | tf_op jit(solution)/shard_map/psum | solution.py:62
  348.0 6.7 collective-permute-done.11
  358.5 7.1 collective-permute-done.41
  370.3 4.6 collective-permute-start.44
  377.0 7.9 %collective-permute-start.47 = (f32[4,1,34,130]{3,2,1,0:T(8,128)S(1)}, f32[4,1,34,130]{3,2,1,0:T(8,128)S(1)}, u32[]{:S(2)}, u32[]{:S(2)}) collective-permute-start(f32[4,1,34,130]{3,2,1,0:T(8,128)S(1)} %get-tuple-element.47), channel_id=1, source_target_pairs={{1,0},{2,1},{3,2},{4,3},{5,4},{6,5},{7,6},{8,7},{9,8},{10,9},{11,1... | collective-permute-start | bytes 212168 | tf_op jit(solution)/shard_map/ppermute | solution.py:25
  399.5 7.5 collective-permute-start.52
  408.1 8.1 %collective-permute-done.53 = f32[1,34,130]{2,1,0:T(8,128)S(1)} collective-permute-done((f32[1,34,130]{2,1,0:T(8,128)S(1)}, f32[1,34,130]{2,1,0:T(8,128)S(1)}, u32[]{:S(2)}, u32[]{:S(2)}) %collective-permute-start.53) | collective-permute-done | bytes 17712 | tf_op jit(solution)/shard_map/ppermute | solution.py:22
  417.0 72.9 %all-reduce = (f32[]{:T(128)}, f32[]{:T(128)}) all-reduce(f32[]{:T(128)} %get-tuple-element.7, f32[]{:T(128)} %get-tuple-element.6), channel_id=1, replica_groups=mesh['gx'=2,'gy'=2,'gz'=64] {'gx','gy','gz'}, use_global_device_ids=true, to_apply=%region_11.0 | all-reduce | flops 2 | bytes 16 | tf_op jit(solution)/shard_map/psum | solution.py:66
  491.9 73.6 %psum.69 = f32[]{:T(128)} all-reduce(f32[]{:T(128)} %multiply_reduce_fusion.8), channel_id=1, replica_groups=mesh['gx'=2,'gy'=2,'gz'=64] {'gx','gy','gz'}, use_global_device_ids=true, to_apply=%region_15.0 | all-reduce | flops 1 | bytes 8 | tf_op jit(solution)/shard_map/psum | solution.py:66
  578.0 8.1 %collective-permute-done.59 = f32[1,34,130]{2,1,0:T(8,128)S(1)} collective-permute-done((f32[1,34,130]{2,1,0:T(8,128)S(1)}, f32[1,34,130]{2,1,0:T(8,128)S(1)}, u32[]{:S(2)}, u32[]{:S(2)}) %collective-permute-start.59) | collective-permute-done | bytes 17712 | tf_op jit(solution)/shard_map/ppermute | solution.py:22
  586.9 73.3 %psum.70 = f32[]{:T(128)} all-reduce(f32[]{:T(128)} %fusion.41), channel_id=1, replica_groups=mesh['gx'=2,'gy'=2,'gz'=64] {'gx','gy','gz'}, use_global_device_ids=true, to_apply=%region_17.0 | all-reduce | flops 1 | bytes 8 | tf_op jit(solution)/shard_map/psum | solution.py:62
  672.9 8.1 %collective-permute-done.65 = f32[1,34,130]{2,1,0:T(8,128)S(1)} collective-permute-done((f32[1,34,130]{2,1,0:T(8,128)S(1)}, f32[1,34,130]{2,1,0:T(8,128)S(1)}, u32[]{:S(2)}, u32[]{:S(2)}) %collective-permute-start.65) | collective-permute-done | bytes 17712 | tf_op jit(solution)/shard_map/ppermute | solution.py:22
  686.4 72.1 %psum.71 = f32[4]{0:T(128)S(1)} all-reduce(f32[4]{0:T(128)S(1)} %pad_maximum_fusion.286), channel_id=1, replica_groups=mesh['gx'=2,'gy'=2,'gz'=64] {'gx','gy','gz'}, use_global_device_ids=true, to_apply=%region_24.0 | all-reduce | flops 4 | bytes 32 | tf_op jit(solution)/shard_map/psum | solution.py:147
  771.0 6.6 collective-permute-start.77
  (266 shorter events, 139.6 us)
Async XLA Ops:
  4.8 17.7 %collective-permute-start.12 = (f32[3,4,1,128]{3,2,1,0:T(1,128)S(1)}, f32[3,4,1,128]{3,2,1,0:T(1,128)S(1)}, u32[]{:S(2)}, u32[]{:S(2)}) collective-permute-start(f32[3,4,1,128]{3,2,1,0:T(1,128)S(1)} %get-tuple-element.105), channel_id=1, source_target_pairs={{0,128},{128,0},{1,129},{129,1},{2,130},{130,2},{3,131},{131,3},{4... | collective-permute-start | bytes 18440 | tf_op jit(solution)/shard_map/ppermute | solution.py:22
  6.2 16.2 %collective-permute-start.13 = (f32[3,4,1,128]{3,2,1,0:T(1,128)S(1)}, f32[3,4,1,128]{3,2,1,0:T(1,128)S(1)}, u32[]{:S(2)}, u32[]{:S(2)}) collective-permute-start(f32[3,4,1,128]{3,2,1,0:T(1,128)S(1)} %get-tuple-element.106), channel_id=1, source_target_pairs={{128,0},{0,128},{129,1},{1,129},{130,2},{2,130},{131,3},{3,131},{1... | collective-permute-start | bytes 18440 | tf_op jit(solution)/shard_map/ppermute | solution.py:25
  13.5 19.8 %collective-permute-start.4 = (f32[1,34,130]{2,1,0:T(8,128)S(1)}, f32[1,34,130]{2,1,0:T(8,128)S(1)}, u32[]{:S(2)}, u32[]{:S(2)}) collective-permute-start(f32[1,34,130]{2,1,0:T(8,128)S(1)} %get-tuple-element.97), channel_id=1, source_target_pairs={{1,0},{2,1},{3,2},{4,3},{5,4},{6,5},{7,6},{8,7},{9,8},{10,9},{11,1... | collective-permute-start | bytes 53048 | tf_op jit(solution)/shard_map/ppermute | solution.py:25
  22.4 10.8 %collective-permute-start.5 = (f32[1,34,130]{2,1,0:T(8,128)S(1)}, f32[1,34,130]{2,1,0:T(8,128)S(1)}, u32[]{:S(2)}, u32[]{:S(2)}) collective-permute-start(f32[1,34,130]{2,1,0:T(8,128)S(1)} %get-tuple-element.96), channel_id=1, source_target_pairs={{0,1},{1,2},{2,3},{3,4},{4,5},{5,6},{6,7},{7,8},{8,9},{9,10},{10,1... | collective-permute-start | bytes 53048 | tf_op jit(solution)/shard_map/ppermute | solution.py:22
  25.1 13.4 %collective-permute-start.16 = (f32[3,1,34,130]{3,2,1,0:T(8,128)S(1)}, f32[3,1,34,130]{3,2,1,0:T(8,128)S(1)}, u32[]{:S(2)}, u32[]{:S(2)}) collective-permute-start(f32[3,1,34,130]{3,2,1,0:T(8,128)S(1)} %get-tuple-element.65), channel_id=1, source_target_pairs={{1,0},{2,1},{3,2},{4,3},{5,4},{6,5},{7,6},{8,7},{9,8},{10,9},{11,1... | collective-permute-start | bytes 159128 | tf_op jit(solution)/shard_map/ppermute | solution.py:25
  33.3 10.7 %collective-permute-start.17 = (f32[3,1,34,130]{3,2,1,0:T(8,128)S(1)}, f32[3,1,34,130]{3,2,1,0:T(8,128)S(1)}, u32[]{:S(2)}, u32[]{:S(2)}) collective-permute-start(f32[3,1,34,130]{3,2,1,0:T(8,128)S(1)} %get-tuple-element.64), channel_id=1, source_target_pairs={{0,1},{1,2},{2,3},{3,4},{4,5},{5,6},{6,7},{7,8},{8,9},{9,10},{10,1... | collective-permute-start | bytes 159128 | tf_op jit(solution)/shard_map/ppermute | solution.py:22
  56.9 11.2 %collective-permute-start.22 = (f32[3,1,34,130]{3,2,1,0:T(8,128)S(1)}, f32[3,1,34,130]{3,2,1,0:T(8,128)S(1)}, u32[]{:S(2)}, u32[]{:S(2)}) collective-permute-start(f32[3,1,34,130]{3,2,1,0:T(8,128)S(1)} %get-tuple-element.62), channel_id=1, source_target_pairs={{0,1},{1,2},{2,3},{3,4},{4,5},{5,6},{6,7},{7,8},{8,9},{9,10},{10,1... | collective-permute-start | bytes 159128 | tf_op jit(solution)/shard_map/ppermute | solution.py:22
  57.2 12.4 %collective-permute-start.23 = (f32[3,1,34,130]{3,2,1,0:T(8,128)S(1)}, f32[3,1,34,130]{3,2,1,0:T(8,128)S(1)}, u32[]{:S(2)}, u32[]{:S(2)}) collective-permute-start(f32[3,1,34,130]{3,2,1,0:T(8,128)S(1)} %get-tuple-element.63), channel_id=1, source_target_pairs={{1,0},{2,1},{3,2},{4,3},{5,4},{6,5},{7,6},{8,7},{9,8},{10,9},{11,1... | collective-permute-start | bytes 159128 | tf_op jit(solution)/shard_map/ppermute | solution.py:25
  84.7 9.2 %collective-permute-start.29 = (f32[1,34,130]{2,1,0:T(8,128)S(1)}, f32[1,34,130]{2,1,0:T(8,128)S(1)}, u32[]{:S(2)}, u32[]{:S(2)}) collective-permute-start(f32[1,34,130]{2,1,0:T(8,128)S(1)} %get-tuple-element.95), channel_id=1, source_target_pairs={{0,1},{1,2},{2,3},{3,4},{4,5},{5,6},{6,7},{7,8},{8,9},{9,10},{10,1... | collective-permute-start | bytes 53048 | tf_op jit(solution)/shard_map/ppermute | solution.py:22
  255.4 9.3 %collective-permute-start.35 = (f32[1,34,130]{2,1,0:T(8,128)S(1)}, f32[1,34,130]{2,1,0:T(8,128)S(1)}, u32[]{:S(2)}, u32[]{:S(2)}) collective-permute-start(f32[1,34,130]{2,1,0:T(8,128)S(1)} %get-tuple-element.93), channel_id=1, source_target_pairs={{0,1},{1,2},{2,3},{3,4},{4,5},{5,6},{6,7},{7,8},{8,9},{9,10},{10,1... | collective-permute-start | bytes 53048 | tf_op jit(solution)/shard_map/ppermute | solution.py:22
  255.5 87.8 %collective-permute-start.8 = (f32[4,34,1]{2,1,0:T(8,128)S(1)}, f32[4,34,1]{2,1,0:T(8,128)S(1)}, u32[]{:S(2)}, u32[]{:S(2)}) collective-permute-start(f32[4,34,1]{2,1,0:T(8,128)S(1)} %get-tuple-element.116), channel_id=1, source_target_pairs={{0,64},{64,0},{1,65},{65,1},{2,66},{66,2},{3,67},{67,3},{4,68},{68... | collective-permute-start | bytes 1640 | tf_op jit(solution)/shard_map/ppermute | solution.py:22
  265.5 77.7 %collective-permute-start.9 = (f32[4,34,1]{2,1,0:T(8,128)S(1)}, f32[4,34,1]{2,1,0:T(8,128)S(1)}, u32[]{:S(2)}, u32[]{:S(2)}) collective-permute-start(f32[4,34,1]{2,1,0:T(8,128)S(1)} %get-tuple-element.115), channel_id=1, source_target_pairs={{64,0},{0,64},{65,1},{1,65},{66,2},{2,66},{67,3},{3,67},{68,4},{4,... | collective-permute-start | bytes 1640 | tf_op jit(solution)/shard_map/ppermute | solution.py:25
  345.5 9.2 %collective-permute-start.11 = (f32[1,34,130]{2,1,0:T(8,128)S(1)}, f32[1,34,130]{2,1,0:T(8,128)S(1)}, u32[]{:S(2)}, u32[]{:S(2)}) collective-permute-start(f32[1,34,130]{2,1,0:T(8,128)S(1)} %get-tuple-element.89), channel_id=1, source_target_pairs={{0,1},{1,2},{2,3},{3,4},{4,5},{5,6},{6,7},{7,8},{8,9},{9,10},{10,1... | collective-permute-start | bytes 53048 | tf_op jit(solution)/shard_map/ppermute | solution.py:22
  345.7 9.8 %collective-permute-start.38 = (f32[4,34,1]{2,1,0:T(8,128)S(1)}, f32[4,34,1]{2,1,0:T(8,128)S(1)}, u32[]{:S(2)}, u32[]{:S(2)}) collective-permute-start(f32[4,34,1]{2,1,0:T(8,128)S(1)} %get-tuple-element.118), channel_id=1, source_target_pairs={{0,64},{64,0},{1,65},{65,1},{2,66},{66,2},{3,67},{67,3},{4,68},{68... | collective-permute-start | bytes 1640 | tf_op jit(solution)/shard_map/ppermute | solution.py:22
  356.5 9.2 %collective-permute-start.41 = (f32[1,34,130]{2,1,0:T(8,128)S(1)}, f32[1,34,130]{2,1,0:T(8,128)S(1)}, u32[]{:S(2)}, u32[]{:S(2)}) collective-permute-start(f32[1,34,130]{2,1,0:T(8,128)S(1)} %get-tuple-element.91), channel_id=1, source_target_pairs={{0,1},{1,2},{2,3},{3,4},{4,5},{5,6},{6,7},{7,8},{8,9},{9,10},{10,1... | collective-permute-start | bytes 53048 | tf_op jit(solution)/shard_map/ppermute | solution.py:22
  376.9 11.9 %collective-permute-start.46 = (f32[4,1,34,130]{3,2,1,0:T(8,128)S(1)}, f32[4,1,34,130]{3,2,1,0:T(8,128)S(1)}, u32[]{:S(2)}, u32[]{:S(2)}) collective-permute-start(f32[4,1,34,130]{3,2,1,0:T(8,128)S(1)} %get-tuple-element.46), channel_id=1, source_target_pairs={{0,1},{1,2},{2,3},{3,4},{4,5},{5,6},{6,7},{7,8},{8,9},{9,10},{10,1... | collective-permute-start | bytes 212168 | tf_op jit(solution)/shard_map/ppermute | solution.py:22
  377.0 14.9 %collective-permute-start.47 = (f32[4,1,34,130]{3,2,1,0:T(8,128)S(1)}, f32[4,1,34,130]{3,2,1,0:T(8,128)S(1)}, u32[]{:S(2)}, u32[]{:S(2)}) collective-permute-start(f32[4,1,34,130]{3,2,1,0:T(8,128)S(1)} %get-tuple-element.47), channel_id=1, source_target_pairs={{1,0},{2,1},{3,2},{4,3},{5,4},{6,5},{7,6},{8,7},{9,8},{10,9},{11,1... | collective-permute-start | bytes 212168 | tf_op jit(solution)/shard_map/ppermute | solution.py:25
  407.0 9.2 %collective-permute-start.53 = (f32[1,34,130]{2,1,0:T(8,128)S(1)}, f32[1,34,130]{2,1,0:T(8,128)S(1)}, u32[]{:S(2)}, u32[]{:S(2)}) collective-permute-start(f32[1,34,130]{2,1,0:T(8,128)S(1)} %get-tuple-element.87), channel_id=1, source_target_pairs={{0,1},{1,2},{2,3},{3,4},{4,5},{5,6},{6,7},{7,8},{8,9},{9,10},{10,1... | collective-permute-start | bytes 53048 | tf_op jit(solution)/shard_map/ppermute | solution.py:22
  576.9 9.2 %collective-permute-start.59 = (f32[1,34,130]{2,1,0:T(8,128)S(1)}, f32[1,34,130]{2,1,0:T(8,128)S(1)}, u32[]{:S(2)}, u32[]{:S(2)}) collective-permute-start(f32[1,34,130]{2,1,0:T(8,128)S(1)} %get-tuple-element.85), channel_id=1, source_target_pairs={{0,1},{1,2},{2,3},{3,4},{4,5},{5,6},{6,7},{7,8},{8,9},{9,10},{10,1... | collective-permute-start | bytes 53048 | tf_op jit(solution)/shard_map/ppermute | solution.py:22
  671.8 9.2 %collective-permute-start.65 = (f32[1,34,130]{2,1,0:T(8,128)S(1)}, f32[1,34,130]{2,1,0:T(8,128)S(1)}, u32[]{:S(2)}, u32[]{:S(2)}) collective-permute-start(f32[1,34,130]{2,1,0:T(8,128)S(1)} %get-tuple-element.83), channel_id=1, source_target_pairs={{0,1},{1,2},{2,3},{3,4},{4,5},{5,6},{6,7},{7,8},{8,9},{9,10},{10,1... | collective-permute-start | bytes 53048 | tf_op jit(solution)/shard_map/ppermute | solution.py:22
  768.2 9.4 %collective-permute-start.68 = (f32[4,34,1]{2,1,0:T(8,128)S(1)}, f32[4,34,1]{2,1,0:T(8,128)S(1)}, u32[]{:S(2)}, u32[]{:S(2)}) collective-permute-start(f32[4,34,1]{2,1,0:T(8,128)S(1)} %get-tuple-element.108), channel_id=1, source_target_pairs={{0,64},{64,0},{1,65},{65,1},{2,66},{66,2},{3,67},{67,3},{4,68},{68... | collective-permute-start | bytes 1640 | tf_op jit(solution)/shard_map/ppermute | solution.py:22
  769.7 12.7 %collective-permute-start.76 = (f32[3,1,34,130]{3,2,1,0:T(8,128)S(1)}, f32[3,1,34,130]{3,2,1,0:T(8,128)S(1)}, u32[]{:S(2)}, u32[]{:S(2)}) collective-permute-start(f32[3,1,34,130]{3,2,1,0:T(8,128)S(1)} %get-tuple-element.60), channel_id=1, source_target_pairs={{0,1},{1,2},{2,3},{3,4},{4,5},{5,6},{6,7},{7,8},{8,9},{9,10},{10,1... | collective-permute-start | bytes 159128 | tf_op jit(solution)/shard_map/ppermute | solution.py:22
  771.0 11.4 %collective-permute-start.77 = (f32[3,1,34,130]{3,2,1,0:T(8,128)S(1)}, f32[3,1,34,130]{3,2,1,0:T(8,128)S(1)}, u32[]{:S(2)}, u32[]{:S(2)}) collective-permute-start(f32[3,1,34,130]{3,2,1,0:T(8,128)S(1)} %get-tuple-element.61), channel_id=1, source_target_pairs={{1,0},{2,1},{3,2},{4,3},{5,4},{6,5},{7,6},{8,7},{9,8},{10,9},{11,1... | collective-permute-start | bytes 159128 | tf_op jit(solution)/shard_map/ppermute | solution.py:25
  777.8 9.3 %collective-permute-start.71 = (f32[1,34,130]{2,1,0:T(8,128)S(1)}, f32[1,34,130]{2,1,0:T(8,128)S(1)}, u32[]{:S(2)}, u32[]{:S(2)}) collective-permute-start(f32[1,34,130]{2,1,0:T(8,128)S(1)} %get-tuple-element.81), channel_id=1, source_target_pairs={{0,1},{1,2},{2,3},{3,4},{4,5},{5,6},{6,7},{7,8},{8,9},{9,10},{10,1... | collective-permute-start | bytes 53048 | tf_op jit(solution)/shard_map/ppermute | solution.py:22
  (70 other events, 277.9 us)
where the time goes:
time: 798 us; the launch traced here: 788 us
  blocking collectives  511 us (64%)
  starting transfers between devices  127 us (16%)
  waiting for transfers between devices  110 us (14%)
  other arithmetic  18.7 us (2%)
  between operations  15.2 us (2%)
    psum x4, blocking collectives, norm_sum(): return lax.psum(value, ('gx', 'gy', 'gz'))  293 us
    psum x2, blocking collectives, global_sum(): return lax.psum(value, ('gx', 'gy', 'gz'))  146 us
    ppermute x39, waiting for transfers between devices, extended(): lax.ppermute(lax.slice_in_dim(block, block.shape[dim] - width, None, axis...  83.4 us
    psum x1, blocking collectives, local(): totals = lax.psum(partial_value, ('gx', 'gy', 'gz'))  72.1 us
    ppermute x39, starting transfers between devices, extended(): lax.ppermute(lax.slice_in_dim(block, 0, width, axis=dim), axis, backward)  71.2 us
    ppermute x39, starting transfers between devices, extended(): lax.ppermute(lax.slice_in_dim(block, block.shape[dim] - width, None, axis...  56.3 us
    ppermute x39, waiting for transfers between devices, extended(): lax.ppermute(lax.slice_in_dim(block, 0, width, axis=dim), axis, backward)  26.4 us
  transfers between devices with their start and end apart: 78, of which 54 were waited for; matrix products, arithmetic and copies ran while one was open for 1% of the time, Pallas kernels for 0%

commit v1 on v0

v1 whole, which is shorter than its diff:
```python
import jax
import jax.numpy as jnp
from jax import lax
from jax.experimental import pallas as pl
from jax.experimental.pallas import tpu as pltpu
from jax.sharding import PartitionSpec as P

DT = 0.1
SHIFT = 0.01
CZ, CX, CY = 4, 32, 128
HX = 8
ROWS = CX + 2 * HX
LANES = 2 * CY
DEVICES = 256

V0, V1, V2, PH, PO, O0, O1, O2 = range(8)
HALO = (4, 3, 3, 4, 2, 1, 1, 1)
BASE = []
_at = 0
for _h in HALO:
    BASE.append(_at)
    _at += CZ + 2 * _h
TOTAL = _at
NUM_SUMS = 45


def x_up(a):
    return pltpu.roll(a, a.shape[0] - 1, 0)


def x_dn(a):
    return pltpu.roll(a, 1, 0)


def y_up(a):
    return pltpu.roll(a, a.shape[1] - 1, 1)


def y_dn(a):
    return pltpu.roll(a, 1, 1)


def dx(a):
    return 0.5 * (x_up(a) - x_dn(a))


def dy(a):
    return 0.5 * (y_up(a) - y_dn(a))


def own(a):
    return a[HX : HX + CX, :CY]


def loop(count, body):
    def step(t, carry):
        body(t)
        return carry

    lax.fori_loop(0, count, step, 0)


def first_kernel(coefs, e, b, u, q, adj, pot, lph, g, lv, p0, p1, p2):
    mobility = 0.1 * coefs[0]
    tension = 0.5 * coefs[1]
    viscosity = 0.1 * coefs[2]
    interface = 0.5 * coefs[3]

    def at(field, z):
        return e[BASE[field] + HALO[field] + z]

    def around(field, z):
        c = at(field, z)
        zu, zd = at(field, z + 1), at(field, z - 1)
        xu, xd, yu, yd = x_up(c), x_dn(c), y_up(c), y_dn(c)
        lap = (zu + zd) + (xu + xd) + (yu + yd) - 6.0 * c
        return c, 0.5 * (zu - zd), 0.5 * (xu - xd), 0.5 * (yu - yd), lap

    def potential(t):
        c = at(PH, t - 3)
        lap = at(PH, t - 2) + at(PH, t - 4) + (x_up(c) + x_dn(c)) + (y_up(c) + y_dn(c)) - 6.0 * c
        lph[t] = lap
        pot[t] = c * c * c - c - interface * lap

    loop(10, potential)

    def provisional(field, z, grad, potential_here):
        c, d0, d1, d2, lap = around(field, z)
        advect = at(V0, z) * d0 + at(V1, z) * d1 + at(V2, z) * d2
        value = c - DT * advect + (DT * viscosity) * lap + (DT * tension) * (potential_here * grad)
        return value, lap

    def along(t):
        z = t - 3
        grad = 0.5 * (at(PH, z + 1) - at(PH, z - 1))
        p0[t], lap = provisional(V0, z, grad, pot[t])
        lv[0, t] = lap

    loop(10, along)

    def across(t):
        z = t - 2
        c = at(PH, z)
        here = pot[t + 1]
        g0 = 0.5 * (at(PH, z + 1) - at(PH, z - 1))
        g1 = dx(c)
        g2 = dy(c)
        g[0, t] = g0
        g[1, t] = g1
        g[2, t] = g2
        p1[t], lap1 = provisional(V1, z, g1, here)
        p2[t], lap2 = provisional(V2, z, g2, here)
        lv[1, t + 1] = lap1
        lv[2, t + 1] = lap2
        lap_pot = pot[t + 2] + pot[t] + (x_up(here) + x_dn(here)) + (y_up(here) + y_dn(here)) - 6.0 * here
        flow = at(V0, z) * g0 + at(V1, z) * g1 + at(V2, z) * g2
        adj[t] = c - DT * flow + (DT * mobility) * lap_pot - at(PO, z)

    loop(8, across)

    def source(t):
        b[t] = -(0.5 * (p0[t + 2] - p0[t]) + dx(p1[t]) + dy(p2[t]))

    loop(8, source)

    def misfit(t):
        z = t - 1
        q[0, t] = p0[t + 2] - at(O0, z)
        q[1, t] = p1[t + 1] - at(O1, z)
        q[2, t] = p2[t + 1] - at(O2, z)

    loop(6, misfit)

    def second_source(t):
        u[t] = 0.5 * (q[0, t + 2] - q[0, t]) + dx(q[1, t + 1]) + dy(q[2, t + 1])

    loop(4, second_source)


def rows_of(a):
    return (a[0:8] + a[8:16]) + (a[16:24] + a[24:32])


def weight_kernel(q, adj, pot, lph, g, lv, w, part):
    zero = jnp.zeros((8, CY), jnp.float32)
    sums = [zero] * 5
    for t in range(CZ):
        here = pot[t + 3]
        lap = lph[t + 3]
        up, dn = pot[t + 4] * g[0, t + 3], pot[t + 2] * g[0, t + 1]
        w1 = 0.5 * (up - dn) + dx(here * g[1, t + 2]) + dy(here * g[2, t + 2])
        w2 = 0.5 * (lv[0, t + 4] - lv[0, t + 2]) + dx(lv[1, t + 3]) + dy(lv[2, t + 3])
        up, dn = lph[t + 4] * g[0, t + 3], lph[t + 2] * g[0, t + 1]
        w3 = 0.5 * (up - dn) + dx(lap * g[1, t + 2]) + dy(lap * g[2, t + 2])
        w[0, t] = own(w1)
        w[1, t] = own(w2)
        w[2, t] = own(w3)
        lap_pot = pot[t + 4] + pot[t + 2] + (x_up(here) + x_dn(here)) + (y_up(here) + y_dn(here)) - 6.0 * here
        c = adj[t + 2]
        lap_adj = adj[t + 3] + adj[t + 1] + (x_up(c) + x_dn(c)) + (y_up(c) + y_dn(c)) - 6.0 * c
        qg = q[0, t + 1] * g[0, t + 2] + q[1, t + 1] * g[1, t + 2] + q[2, t + 1] * g[2, t + 2]
        ql = q[0, t + 1] * lv[0, t + 3] + q[1, t + 1] * lv[1, t + 3] + q[2, t + 1] * lv[2, t + 3]
        terms = (own(c * lap_pot), own(here * qg), own(ql), own(lap * qg), own(lap_adj * lap))
        sums = [s + rows_of(a) for s, a in zip(sums, terms)]
    for k in range(5):
        part[k] = sums[k]


def shifted(c, zu, zd):
    return (6.0 + SHIFT) * c - ((zu + zd) + (x_up(c) + x_dn(c)) + (y_up(c) + y_dn(c)))


def moment_kernel(b8, u4, lo, hi, w, part, psi, out, bb, uu, f, af, a2f, a3f, ab, a2b, au, a2u):
    bb[0:4] = lo[0:4]
    bb[4:12] = b8[...]
    bb[12:16] = hi[0:4]
    uu[0:3] = lo[4:7]
    uu[3:7] = u4[...]
    uu[7:10] = hi[4:7]

    def wide(t):
        c = bb[t + 2]
        n = c.shape[0]
        across = (pltpu.roll(c, n - 2, 0) + pltpu.roll(c, 2, 0)) + (pltpu.roll(c, LANES - 2, 1) + pltpu.roll(c, 2, 1))
        f[t] = 0.25 * ((bb[t + 4] + bb[t]) + across) - 1.5 * c

    loop(12, wide)

    def apply(src, dst, count):
        def body(t):
            dst[t] = shifted(src[t + 1], src[t + 2], src[t])

        loop(count, body)

    apply(f, af, 10)
    apply(af, a2f, 8)
    apply(a2f.at[pl.ds(1, 6)], a3f, 4)
    apply(bb.at[pl.ds(3, 10)], ab, 8)
    apply(ab.at[pl.ds(1, 6)], a2b, 4)
    apply(uu, au, 8)
    apply(au.at[pl.ds(1, 6)], a2u, 4)

    def keep(t):
        psi[0, t] = uu[t + 1]
        psi[1, t] = au[t]
        psi[2, t] = f[t + 2]
        psi[3, t] = af[t + 1]
        psi[4, t] = a2f[t]
        psi[5, t] = bb[t + 4]
        psi[6, t] = ab[t]

    loop(8, keep)

    rows = pl.ds(HX, CX)
    lanes = pl.ds(0, CY)
    acc = [jnp.zeros((8, CY), jnp.float32)] * 40
    for t in range(CZ):
        vb, vab, va2b = bb[t + 6, rows, lanes], ab[t + 2, rows, lanes], a2b[t, rows, lanes]
        vu, vau, va2u = uu[t + 3, rows, lanes], au[t + 2, rows, lanes], a2u[t, rows, lanes]
        vf, vaf, va2f, va3f = (
            f[t + 4, rows, lanes], af[t + 3, rows, lanes], a2f[t + 2, rows, lanes], a3f[t, rows, lanes],
        )
        terms = [
            vb * vb, vb * vab, vab * vab, vab * va2b,
            vu * vu, vu * vau, vau * vau, vau * va2u,
            vu * vf, vu * vaf, vu * va2f, vau * va2f, va2u * va2f,
            vf * vf, vf * vaf, vaf * vaf, vaf * va2f, va2f * va2f, va2f * va3f,
        ]
        for k in range(3):
            wk = w[k, t]
            terms += [a * wk for a in (vu, vau, vf, vaf, va2f, vb, vab)]
        acc = [s + rows_of(a) for s, a in zip(acc, terms)]
    rows_list = [jnp.sum(a, axis=0, keepdims=True) for a in acc]
    rows_list += [jnp.sum(part[k], axis=0, keepdims=True) for k in range(5)]
    rows_list += [jnp.zeros((1, CY), jnp.float32)] * (48 - NUM_SUMS)
    table = jnp.concatenate(rows_list, axis=0)
    totals = jnp.sum(table, axis=1, keepdims=True)
    line = lax.broadcasted_iota(jnp.int32, (48, CY), 1)
    which = lax.broadcasted_iota(jnp.int32, (48, CY), 0)
    row = jnp.sum(jnp.where(line == which, totals, 0.0), axis=0, keepdims=True)
    out[...] = jnp.broadcast_to(row, (DEVICES, CY))


def steps(m0, m1, m2, m3):
    alpha = m0 / m1
    norm = m0 * ((m0 * m2) / (m1 * m1) - 1.0)
    beta = norm / m0
    one = 1.0 + beta
    curve = one * one * m1 - 2.0 * one * alpha * m2 + alpha * alpha * m3
    second = norm / curve
    return alpha + second * one, -second * alpha


def last_kernel(coefs, gathered, psi, e, q, adj, pot, g, phase_back, velocity_back, params, phi, pr, pa):
    mobility = 0.1 * coefs[0]
    tension = 0.5 * coefs[1]
    viscosity = 0.1 * coefs[2]
    interface = 0.5 * coefs[3]

    total = jnp.sum(gathered[...], axis=0, keepdims=True)
    line = lax.broadcasted_iota(jnp.int32, (1, CY), 1)

    def s(k):
        return jnp.sum(jnp.where(line == k, total, 0.0), axis=1, keepdims=True)

    c0, c1 = steps(s(0), s(1), s(2), s(3))
    uu = [s(4 + k) for k in range(4)]
    uf = [s(8 + k) for k in range(5)]
    ff = [s(13 + k) for k in range(6)]
    moments = [
        uu[k] - 2.0 * (c0 * uf[k] + c1 * uf[k + 1])
        + (c0 * c0) * ff[k] + (2.0 * c0 * c1) * ff[k + 1] + (c1 * c1) * ff[k + 2]
        for k in range(4)
    ]
    e0, e1 = steps(*moments)
    coef = (e0, e1, -e0 * c0, -(e0 * c1 + e1 * c0), -e1 * c1, -c0, -c1)

    def meet(k):
        value = coef[0] * s(19 + 7 * k)
        for j in range(1, 7):
            value = value + coef[j] * s(19 + 7 * k + j)
        return value

    scale = 1.0 / (256 * 64 * 256)
    g0 = DT * s(40)
    g1 = DT * (s(41) - meet(0))
    g2 = DT * (s(42) - meet(1))
    g3 = -((DT * mobility) * s(44) + (DT * tension) * (s(43) - meet(2)))
    place = lax.broadcasted_iota(jnp.int32, (1, CY), 1)
    packed = jnp.where(place == 0, g0, jnp.where(place == 1, g1, jnp.where(place == 2, g2, g3)))
    params[...] = packed * scale

    def combine(t):
        value = coef[0] * psi[0, t]
        for j in range(1, 7):
            value = value + coef[j] * psi[j, t]
        phi[t] = value

    loop(8, combine)

    def at(field, z):
        return e[BASE[field] + HALO[field] + z]

    def project(t):
        c = phi[t + 1]
        r0 = q[0, t] + 0.5 * (phi[t + 2] - phi[t])
        r1 = q[1, t] + dx(c)
        r2 = q[2, t] + dy(c)
        pr[0, t] = r0
        pr[1, t] = r1
        pr[2, t] = r2
        d = adj[t + 1]
        lap = adj[t + 2] + adj[t] + (x_up(d) + x_dn(d)) + (y_up(d) + y_dn(d)) - 6.0 * d
        pa[t] = (DT * mobility) * lap + (DT * tension) * (r0 * g[0, t + 1] + r1 * g[1, t + 1] + r2 * g[2, t + 1])

    loop(6, project)

    def finish(t):
        v0, v1, v2 = at(V0, t), at(V1, t), at(V2, t)
        v0u, v0d = at(V0, t + 1), at(V0, t - 1)
        c = adj[t + 2]
        here = pot[t + 3]
        ph = at(PH, t)
        lam = pa[t + 1]
        lap = pa[t + 2] + pa[t] + (x_up(lam) + x_dn(lam)) + (y_up(lam) + y_dn(lam)) - 6.0 * lam
        up = v0u * adj[t + 3] - tension * (pot[t + 4] * pr[0, t + 2])
        dn = v0d * adj[t + 1] - tension * (pot[t + 2] * pr[0, t])
        div = 0.5 * (up - dn)
        div = div + dx(v1 * c - tension * (here * pr[1, t + 1]))
        div = div + dy(v2 * c - tension * (here * pr[2, t + 1]))
        value = c + DT * div + (3.0 * ph * ph - 1.0) * lam - interface * lap
        phase_back[t] = own(value)
        r = [pr[i, t + 1] for i in range(3)]
        vel = (v0, v1, v2)
        grads = [[], [], []]
        for i, field in enumerate((V0, V1, V2)):
            grads[0].append(0.5 * (at(field, t + 1) - at(field, t - 1)))
            grads[1].append(dx(vel[i]))
            grads[2].append(dy(vel[i]))
        for k in range(3):
            mix = r[0] * grads[k][0] + r[1] * grads[k][1] + r[2] * grads[k][2]
            ru, rd = pr[k, t + 2], pr[k, t]
            moved = (viscosity + 0.5 * v0u) * ru + (viscosity - 0.5 * v0d) * rd
            moved = moved + x_up((viscosity + 0.5 * v1) * r[k]) + x_dn((viscosity - 0.5 * v1) * r[k])
            moved = moved + y_up((viscosity + 0.5 * v2) * r[k]) + y_dn((viscosity - 0.5 * v2) * r[k])
            moved = moved - (6.0 * viscosity) * r[k]
            value = r[k] + DT * (moved - mix - c * g[k, t + 2])
            velocity_back[k, t] = own(value)

    loop(4, finish)


def f32(*shape):
    return jax.ShapeDtypeStruct(shape, jnp.float32)


def layers(*lead):
    return f32(*lead, ROWS, LANES)


def scratch(*lead):
    return pltpu.VMEM((*lead, ROWS, LANES), jnp.float32)


VM = pl.BlockSpec(memory_space=pltpu.VMEM)
SM = pl.BlockSpec(memory_space=pltpu.SMEM)
PARAMS = pltpu.CompilerParams(vmem_limit_bytes=48 * 1024 * 1024)
SWAP = [(0, 1), (1, 0)]


def ring(value, step):
    count = lax.axis_size("gz")
    return lax.ppermute(value, "gz", [(i, (i + step) % count) for i in range(count)])


def extend(fields):
    lo = ring(jnp.concatenate([f[CZ - h :] for f, h in zip(fields, HALO)], 0), 1)
    hi = ring(jnp.concatenate([f[:h] for f, h in zip(fields, HALO)], 0), -1)
    parts = []
    at = 0
    for f, h in zip(fields, HALO):
        parts += [lo[at : at + h], f, hi[at : at + h]]
        at += h
    block = jnp.concatenate(parts, 0)
    got = lax.ppermute(jnp.concatenate([block[:, CX - HX :], block[:, :HX]], 1), "gx", SWAP)
    block = jnp.concatenate([got[:, :HX], block, got[:, HX:]], 1)
    other = lax.ppermute(block, "gy", SWAP)
    return jnp.concatenate([block, other], 2)


def local(phase, velocity, phase_obs, velocity_obs, coefs):
    fields = (
        velocity[0], velocity[1], velocity[2], phase, phase_obs,
        velocity_obs[0], velocity_obs[1], velocity_obs[2],
    )
    e = extend(fields)
    b, u, q, adj, pot, lph, g, lv = pl.pallas_call(
        first_kernel,
        out_shape=(layers(8), layers(4), layers(3, 6), layers(8), layers(10), layers(10), layers(3, 8), layers(3, 10)),
        in_specs=[SM, VM],
        out_specs=(VM,) * 8,
        scratch_shapes=[scratch(10), scratch(8), scratch(8)],
        compiler_params=PARAMS,
        name="first",
    )(coefs, e)
    lo = ring(jnp.concatenate([b[0:4], u[1:4]], 0), 1)
    hi = ring(jnp.concatenate([b[4:8], u[0:3]], 0), -1)
    w, part = pl.pallas_call(
        weight_kernel,
        out_shape=(f32(3, CZ, CX, CY), f32(5, 8, CY)),
        in_specs=[VM] * 6,
        out_specs=(VM, VM),
        compiler_params=PARAMS,
        name="weights",
    )(q, adj, pot, lph, g, lv)
    psi, sums = pl.pallas_call(
        moment_kernel,
        out_shape=(layers(7, 8), f32(DEVICES, CY)),
        in_specs=[VM] * 6,
        out_specs=(VM, VM),
        scratch_shapes=[
            scratch(16), scratch(10), scratch(12), scratch(10), scratch(8),
            scratch(4), scratch(8), scratch(4), scratch(8), scratch(4),
        ],
        compiler_params=PARAMS,
        name="moments",
    )(b, u, lo, hi, w, part)
    gathered = lax.all_to_all(sums.reshape(DEVICES, 1, CY), ("gx", "gy", "gz"), 0, 0).reshape(DEVICES, CY)
    phase_back, velocity_back, params = pl.pallas_call(
        last_kernel,
        out_shape=(f32(CZ, CX, CY), f32(3, CZ, CX, CY), f32(1, CY)),
        in_specs=[SM] + [VM] * 7,
        out_specs=(VM, VM, VM),
        scratch_shapes=[scratch(8), scratch(3, 6), scratch(6)],
        compiler_params=PARAMS,
        name="last",
    )(coefs, gathered, psi, e, q, adj, pot, g)
    return phase_back, velocity_back, params[0, :4]


def solution(mesh):
    return jax.shard_map(
        local,
        mesh=mesh,
        in_specs=(
            P("gz", "gx", "gy"),
            P(None, "gz", "gx", "gy"),
            P("gz", "gx", "gy"),
            P(None, "gz", "gx", "gy"),
            P(),
        ),
        out_specs=(P("gz", "gx", "gy"), P(None, "gz", "gx", "gy"), P()),
        check_vma=False,
    )
```

time: 798 us -> 117 us (0.15); the launches traced: 788 us -> 116 us
  blocking collectives: 511 us -> 23.6 us
  starting transfers between devices: 127 us -> 26.5 us
  waiting for transfers between devices: 110 us -> 40.1 us
  Pallas kernels: 0 us -> 18.5 us
  other arithmetic: 18.7 us -> 2.21 us
  between operations: 15.2 us -> 1 us
    psum x7 -> x0, blocking collectives: 511 us -> none  [the longest x4 293 us: norm_sum(): return lax.psum(value, ('gx', 'gy', 'gz'))]
    ppermute x78 -> x6, starting transfers between devices: 127 us -> 26.5 us  [the longest x4 20.3 us: ring(): lax.ppermute(value, 'gz', [(i, (i + step) % count) for i in range(count)])]
    ppermute x78 -> x6, waiting for transfers between devices: 110 us -> 40.1 us  [the longest x4 24.8 us: ring(): lax.ppermute(value, 'gz', [(i, (i + step) % count) for i in range(count)])]
    all_to_all x0 -> x1, blocking collectives: none -> 23.6 us  [local(): lax.all_to_all(sums.reshape(DEVICES, 1, CY), ('gx', 'gy', 'gz'), 0, 0)]
    pallas_call x0 -> x4, Pallas kernels: none -> 18.5 us  [the longest x1 7.1 us: local(): pl.pallas_call(first_kernel, out_shape=(layers(8), layers(4), layers(3, 6...]
  transfers between devices with their start and end apart: 78 -> 6, of which waited for: 54 -> 5; matrix products, arithmetic and copies ran while one was open for 1% -> 0% of each run, Pallas kernels for 0% -> 0%
where the time goes in v1:
time: 117 us; the launch traced here: 116 us
  waiting for transfers between devices  40.1 us (34%)
  starting transfers between devices  26.5 us (23%)
  blocking collectives  23.6 us (20%)
  Pallas kernels  18.5 us (16%)
  local copies, waits for them, and re-layouts  4.25 us (4%)
  other arithmetic  2.21 us (2%)
    ppermute x4, waiting for transfers between devices, ring(): lax.ppermute(value, 'gz', [(i, (i + step) % count) for i in range(count)])  24.8 us
    all_to_all x1, blocking collectives, local(): lax.all_to_all(sums.reshape(DEVICES, 1, CY), ('gx', 'gy', 'gz'), 0, 0)  23.6 us
    ppermute x4, starting transfers between devices, ring(): lax.ppermute(value, 'gz', [(i, (i + step) % count) for i in range(count)])  20.3 us
    ppermute x1, waiting for transfers between devices, extend(): lax.ppermute(jnp.concatenate([block[:, CX - HX:], block[:, :HX]], 1), 'gx...  12 us
    pallas_call x1, Pallas kernels, local(): pl.pallas_call(first_kernel, out_shape=(layers(8), layers(4), layers(3, 6...  7.1 us
    pallas_call x1, Pallas kernels, local(): pl.pallas_call(moment_kernel, out_shape=(layers(7, 8), f32(DEVICES, CY)),...  6.27 us
    pallas_call x1, Pallas kernels, local(): pl.pallas_call(last_kernel, out_shape=(f32(CZ, CX, CY), f32(3, CZ, CX, CY...  4.74 us
    ppermute x1, starting transfers between devices, extend(): lax.ppermute(jnp.concatenate([block[:, CX - HX:], block[:, :HX]], 1), 'gx...  4.23 us
  transfers between devices with their start and end apart: 6, of which 5 were waited for; matrix products, arithmetic and copies ran while one was open for 0% of the time, Pallas kernels for 0%

profile of v1, /device:TPU:1, one launch (start us, length us, event | category | flops | bytes accessed | tf_op | source)
XLA Modules:
  0.0 116.3 jit_solution(12870737456269061073)
XLA Ops:
  0.6 0.0 copy-start.1
  0.7 0.9 constant_dynamic-update-slice_fusion.7
  1.6 0.8 constant_dynamic-update-slice_fusion.14
  2.4 0.8 constant_dynamic-update-slice_fusion.6
  3.2 0.9 constant_dynamic-update-slice_fusion.13
  4.2 2.1 %collective-permute-start = (f32[19,32,128]{2,1,0:T(8,128)S(1)}, f32[19,32,128]{2,1,0:T(8,128)S(1)}, u32[]{:S(2)}, u32[]{:S(2)}) collective-permute-start(f32[19,32,128]{2,1,0:T(8,128)S(1)} %get-tuple-element.42), channel_id=1, source_target_pairs={{0,1},{1,2},{2,3},{3,4},{4,5},{5,6},{6,7},{7,8},{8,9},{9,10},{10,1... | collective-permute-start | bytes 933896 | tf_op jit(solution)/shard_map/ppermute | solution.py:373
  6.3 9.5 %collective-permute-start.1 = (f32[19,32,128]{2,1,0:T(8,128)S(1)}, f32[19,32,128]{2,1,0:T(8,128)S(1)}, u32[]{:S(2)}, u32[]{:S(2)}) collective-permute-start(f32[19,32,128]{2,1,0:T(8,128)S(1)} %get-tuple-element.41), channel_id=1, source_target_pairs={{0,63},{1,0},{2,1},{3,2},{4,3},{5,4},{6,5},{7,6},{8,7},{9,8},{10,9... | collective-permute-start | bytes 933896 | tf_op jit(solution)/shard_map/ppermute | solution.py:373
  15.9 9.0 %collective-permute-done = f32[19,32,128]{2,1,0:T(8,128)S(1)} collective-permute-done((f32[19,32,128]{2,1,0:T(8,128)S(1)}, f32[19,32,128]{2,1,0:T(8,128)S(1)}, u32[]{:S(2)}, u32[]{:S(2)}) %collective-permute-start) | collective-permute-done | bytes 311328 | tf_op jit(solution)/shard_map/ppermute | solution.py:373
  24.9 1.6 %collective-permute-done.1 = f32[19,32,128]{2,1,0:T(8,128)S(1)} collective-permute-done((f32[19,32,128]{2,1,0:T(8,128)S(1)}, f32[19,32,128]{2,1,0:T(8,128)S(1)}, u32[]{:S(2)}, u32[]{:S(2)}) %collective-permute-start.1) | collective-permute-done | bytes 311328 | tf_op jit(solution)/shard_map/ppermute | solution.py:373
  26.9 4.2 %collective-permute-start.2 = (f32[70,16,128]{2,1,0:T(8,128)S(1)}, f32[70,16,128]{2,1,0:T(8,128)S(1)}, u32[]{:S(2)}, u32[]{:S(2)}) collective-permute-start(f32[70,16,128]{2,1,0:T(8,128)S(1)} %pad_maximum_fusion.2), channel_id=1, source_target_pairs={{0,128},{128,0},{1,129},{129,1},{2,130},{130,2},{3,131},{131,3},{4... | collective-permute-start | bytes 1720328 | tf_op jit(solution)/shard_map/ppermute | solution.py:385
  31.1 12.0 %collective-permute-done.2 = f32[70,16,128]{2,1,0:T(8,128)S(1)} collective-permute-done((f32[70,16,128]{2,1,0:T(8,128)S(1)}, f32[70,16,128]{2,1,0:T(8,128)S(1)}, u32[]{:S(2)}, u32[]{:S(2)}) %collective-permute-start.2) | collective-permute-done | bytes 573472 | tf_op jit(solution)/shard_map/ppermute | solution.py:385
  43.2 0.1 pad_maximum_fusion.1
  43.3 2.0 %collective-permute-start.3 = (f32[70,48,128]{2,1,0:T(8,128)S(1)}, f32[70,48,128]{2,1,0:T(8,128)S(1)}, u32[]{:S(2)}, u32[]{:S(2)}) collective-permute-start(f32[70,48,128]{2,1,0:T(8,128)S(1)} %pad_maximum_fusion.1), channel_id=1, source_target_pairs={{0,64},{64,0},{1,65},{65,1},{2,66},{66,2},{3,67},{67,3},{4,68},{68... | collective-permute-start | bytes 5160968 | tf_op jit(solution)/shard_map/ppermute | solution.py:387
  45.3 3.2 %collective-permute-done.3 = f32[70,48,128]{2,1,0:T(8,128)S(1)} collective-permute-done((f32[70,48,128]{2,1,0:T(8,128)S(1)}, f32[70,48,128]{2,1,0:T(8,128)S(1)}, u32[]{:S(2)}, u32[]{:S(2)}) %collective-permute-start.3) | collective-permute-done | bytes 1720352 | tf_op jit(solution)/shard_map/ppermute | solution.py:387
  48.5 2.0 %pad_maximum_fusion.e = f32[70,48,256]{2,1,0:T(8,128)} fusion(f32[70,48,128]{2,1,0:T(8,128)S(1)} %collective-permute-done.3, f32[70,8,128]{2,1,0:T(8,128)S(1)} %get-tuple-element.36, f32[70,32,128]{2,1,0:T(8,128)S(1)} %constant_dynamic-update-slice_fusion.16, f32[70,8,128]{2,1,0:T(8,128)S(1)} %get-tuple-element.35), kind=kLoop, calls=%fused_computation | loop fusion | flops 2580480 | bytes 6881280 | tf_op jit(solution)/shard_map/concatenate | solution.py:388
  50.5 7.1 %first.1 = (f32[8,48,256]{2,1,0:T(8,128)S(1)}, f32[4,48,256]{2,1,0:T(8,128)S(1)}, f32[3,6,48,256]{3,2,1,0:T(8,128)S(1)}, f32[8,48,256]{2,1,0:T(8,128)S(1)}, f32[...) custom-call(f32[4]{0:T(128)S(1)} %copy-done, ...), custom_call_target="tpu_custom_call" | custom-call | tf_op jit(solution)/shard_map/first/pallas_call | solution.py:397
  57.8 0.1 collective-permute-start.4
  57.9 8.6 %collective-permute-start.5 = (f32[7,48,256]{2,1,0:T(8,128)S(1)}, f32[7,48,256]{2,1,0:T(8,128)S(1)}, u32[]{:S(2)}, u32[]{:S(2)}) collective-permute-start(f32[7,48,256]{2,1,0:T(8,128)S(1)} %pad_maximum_fusion.4), channel_id=1, source_target_pairs={{0,63},{1,0},{2,1},{3,2},{4,3},{5,4},{6,5},{7,6},{8,7},{9,8},{10,9... | collective-permute-start | bytes 1032200 | tf_op jit(solution)/shard_map/ppermute | solution.py:373
  66.5 0.4 weights.1
  66.9 14.2 %collective-permute-done.4.lo = f32[7,48,256]{2,1,0:T(8,128)S(1)} collective-permute-done((f32[7,48,256]{2,1,0:T(8,128)S(1)}, f32[7,48,256]{2,1,0:T(8,128)S(1)}, u32[]{:S(2)}, u32[]{:S(2)}) %collective-permute-start.4) | collective-permute-done | bytes 344096 | tf_op jit(solution)/shard_map/ppermute | solution.py:373
  81.1 6.3 %moments.1 = (f32[7,8,48,256]{3,2,1,0:T(8,128)S(1)}, f32[256,128]{1,0:T(8,128)S(1)}) custom-call(f32[8,48,256]{2,1,0:T(8,128)S(1)} %get-tuple-element.18.b8, f32[4,48,256]{2,1,0:T(8,128)S(1)} %get-tuple-element.19.u4, f32[7,48,256]{2,1,0:T(8,128)S(1)} %collective-permute-done.4.lo, f32[7,48,256]{2,1,0:T(8,128)S(1)} %collective-permute-done.5.hi, ...), custom_call_target="tpu_custom_call" | custom-call | tf_op jit(solution)/shard_map/moments/pallas_call | solution.py:416
  87.4 23.6 %all_to_all.5 = f32[256,1,128]{2,1,0:T(1,128)S(1)} all-to-all(f32[256,1,128]{2,1,0:T(1,128)S(1)} %bitcast.41), channel_id=1, replica_groups=mesh['gx'=2,'gy'=2,'gz'=64] {'gx','gy','gz'}, dimensions={0} | all-to-all | bytes 262144 | tf_op jit(solution)/shard_map/all_to_all | solution.py:428
  111.0 4.7 %last.1 = (f32[4,32,128]{2,1,0:T(8,128)}, f32[3,4,32,128]{3,2,1,0:T(8,128)}, f32[1,128]{1,0:T(1,128)S(1)}) custom-call(f32[4]{0:T(128)S(1)} %copy-done, f32[256,128]{1,0:T(8,128)S(1)} %bitcast.40, f32[7,8,48,256]{3,2,1,0:T(8,128)S(1)} %get-tuple-element.29.psi, f32[70,48,256]{2,1,0:T(8,128)} %pad_maximum_fusion.e, ...), custom_call_target="tpu_custom_call" | custom-call | tf_op jit(solution)/shard_map/last/pallas_call | solution.py:429
  115.8 0.5 slice_bitcast_fusion
  (47 shorter events, 0.4 us)
Async XLA Ops:
  0.6 24.2 %copy-start.1 = (f32[3,4,32,128]{3,2,1,0:T(8,128)S(1)}, f32[3,4,32,128]{3,2,1,0:T(8,128)}, u32[]{:S(2)}) copy-start(f32[3,4,32,128]{3,2,1,0:T(8,128)} %param.6) | copy-start | bytes 589828
  0.6 3.4 %copy-start.3 = (f32[4,32,128]{2,1,0:T(8,128)S(1)}, f32[4,32,128]{2,1,0:T(8,128)}, u32[]{:S(2)}) copy-start(f32[4,32,128]{2,1,0:T(8,128)} %param.5) | copy-start | bytes 196612
  0.7 3.5 %copy-start.4 = (f32[4,32,128]{2,1,0:T(8,128)S(1)}, f32[4,32,128]{2,1,0:T(8,128)}, u32[]{:S(2)}) copy-start(f32[4,32,128]{2,1,0:T(8,128)} %param.7) | copy-start | bytes 196612
  0.7 3.5 %copy-start.2 = (f32[3,4,32,128]{3,2,1,0:T(8,128)S(1)}, f32[3,4,32,128]{3,2,1,0:T(8,128)}, u32[]{:S(2)}) copy-start(f32[3,4,32,128]{3,2,1,0:T(8,128)} %param.8) | copy-start | bytes 589828
  4.2 20.7 %collective-permute-start = (f32[19,32,128]{2,1,0:T(8,128)S(1)}, f32[19,32,128]{2,1,0:T(8,128)S(1)}, u32[]{:S(2)}, u32[]{:S(2)}) collective-permute-start(f32[19,32,128]{2,1,0:T(8,128)S(1)} %get-tuple-element.42), channel_id=1, source_target_pairs={{0,1},{1,2},{2,3},{3,4},{4,5},{5,6},{6,7},{7,8},{8,9},{9,10},{10,1... | collective-permute-start | bytes 933896 | tf_op jit(solution)/shard_map/ppermute | solution.py:373
  6.3 20.2 %collective-permute-start.1 = (f32[19,32,128]{2,1,0:T(8,128)S(1)}, f32[19,32,128]{2,1,0:T(8,128)S(1)}, u32[]{:S(2)}, u32[]{:S(2)}) collective-permute-start(f32[19,32,128]{2,1,0:T(8,128)S(1)} %get-tuple-element.41), channel_id=1, source_target_pairs={{0,63},{1,0},{2,1},{3,2},{4,3},{5,4},{6,5},{7,6},{8,7},{9,8},{10,9... | collective-permute-start | bytes 933896 | tf_op jit(solution)/shard_map/ppermute | solution.py:373
  26.9 16.3 %collective-permute-start.2 = (f32[70,16,128]{2,1,0:T(8,128)S(1)}, f32[70,16,128]{2,1,0:T(8,128)S(1)}, u32[]{:S(2)}, u32[]{:S(2)}) collective-permute-start(f32[70,16,128]{2,1,0:T(8,128)S(1)} %pad_maximum_fusion.2), channel_id=1, source_target_pairs={{0,128},{128,0},{1,129},{129,1},{2,130},{130,2},{3,131},{131,3},{4... | collective-permute-start | bytes 1720328 | tf_op jit(solution)/shard_map/ppermute | solution.py:385
  43.3 7.2 %copy-start = (f32[4]{0:T(128)S(1)}, f32[4]{0:T(128)}, u32[]{:S(2)}) copy-start(f32[4]{0:T(128)} %coefs.3) | copy-start | bytes 52
  43.3 5.2 %collective-permute-start.3 = (f32[70,48,128]{2,1,0:T(8,128)S(1)}, f32[70,48,128]{2,1,0:T(8,128)S(1)}, u32[]{:S(2)}, u32[]{:S(2)}) collective-permute-start(f32[70,48,128]{2,1,0:T(8,128)S(1)} %pad_maximum_fusion.1), channel_id=1, source_target_pairs={{0,64},{64,0},{1,65},{65,1},{2,66},{66,2},{3,67},{67,3},{4,68},{68... | collective-permute-start | bytes 5160968 | tf_op jit(solution)/shard_map/ppermute | solution.py:387
  57.8 23.4 %collective-permute-start.4 = (f32[7,48,256]{2,1,0:T(8,128)S(1)}, f32[7,48,256]{2,1,0:T(8,128)S(1)}, u32[]{:S(2)}, u32[]{:S(2)}) collective-permute-start(f32[7,48,256]{2,1,0:T(8,128)S(1)} %pad_maximum_fusion.3), channel_id=1, source_target_pairs={{0,1},{1,2},{2,3},{3,4},{4,5},{5,6},{6,7},{7,8},{8,9},{9,10},{10,1... | collective-permute-start | bytes 1032200 | tf_op jit(solution)/shard_map/ppermute | solution.py:373
  57.9 23.2 %collective-permute-start.5 = (f32[7,48,256]{2,1,0:T(8,128)S(1)}, f32[7,48,256]{2,1,0:T(8,128)S(1)}, u32[]{:S(2)}, u32[]{:S(2)}) collective-permute-start(f32[7,48,256]{2,1,0:T(8,128)S(1)} %pad_maximum_fusion.4), channel_id=1, source_target_pairs={{0,63},{1,0},{2,1},{3,2},{4,3},{5,4},{6,5},{7,6},{8,7},{9,8},{10,9... | collective-permute-start | bytes 1032200 | tf_op jit(solution)/shard_map/ppermute | solution.py:373

commit v2 on v1

v2 whole, which is shorter than its diff:
```python
import jax
import jax.numpy as jnp
from jax import lax
from jax.experimental import pallas as pl
from jax.experimental.pallas import tpu as pltpu
from jax.sharding import PartitionSpec as P

DT = 0.1
SHIFT = 0.01
CZ, CX, CY = 4, 32, 128
HX = 8
NEAR = 4
ROWS = CX + 2 * HX
LANES = 2 * CY
DEVICES = 256

V0, V1, V2, PH, PO, O0, O1, O2 = range(8)
HALO = (3, 2, 2, 3, 0, 1, 0, 0)
BASE = []
_at = 0
for _h in HALO:
    BASE.append(_at)
    _at += CZ + 2 * _h
TOTAL = _at
SENT = sum(HALO)
NUM_SUMS = 45
SLOTS = 64


def x_up(a):
    return pltpu.roll(a, a.shape[0] - 1, 0)


def x_dn(a):
    return pltpu.roll(a, 1, 0)


def y_up(a):
    return pltpu.roll(a, a.shape[1] - 1, 1)


def y_dn(a):
    return pltpu.roll(a, 1, 1)


def dx(a):
    return 0.5 * (x_up(a) - x_dn(a))


def dy(a):
    return 0.5 * (y_up(a) - y_dn(a))


def own(a):
    return a[HX : HX + CX, :CY]


def lap_of(c, zu, zd):
    return (zu + zd) + (x_up(c) + x_dn(c)) + (y_up(c) + y_dn(c)) - 6.0 * c


def other_first(a):
    return jnp.concatenate([a[:, CY:], a[:, :CY]], 1)


def loop(count, body):
    def step(t, carry):
        body(t)
        return carry

    lax.fori_loop(0, count, step, 0)


def low_high(core, mine, theirs, j):
    a, b = mine[j], other_first(theirs[j])
    return jnp.where(core == 0, a, b), jnp.where(core == 0, b, a)


def load_kernel(vel, ph, po, vo, coefs, stack, out, coefs_out, sems):
    copies = [
        pltpu.make_async_copy(ph, stack.at[pl.ds(CZ * PH, CZ)], sems.at[6]),
        pltpu.make_async_copy(po, stack.at[pl.ds(CZ * PO, CZ)], sems.at[7]),
        pltpu.make_async_copy(coefs, coefs_out, sems.at[8]),
    ]
    for i in range(3):
        copies.append(pltpu.make_async_copy(vel.at[i], stack.at[pl.ds(CZ * (V0 + i), CZ)], sems.at[i]))
        copies.append(pltpu.make_async_copy(vo.at[i], stack.at[pl.ds(CZ * (O0 + i), CZ)], sems.at[3 + i]))
    for copy in copies:
        copy.start()
    for copy in copies:
        copy.wait()
    wide = CZ * PO
    out[0:wide, 0:HX] = stack[0:wide, CX - HX :]
    out[0:wide, HX:] = stack[0:wide, :HX]
    for n in range(wide):
        at, row = wide + n // 2, HX * (n % 2)
        out[at, row : row + NEAR] = stack[wide + n, CX - NEAR :]
        out[at, row + NEAR : row + HX] = stack[wide + n, :NEAR]


def pack_kernel(core, stack, vel_s, ph_s, vo_s, main, diag):
    c = core[0]
    n = 0
    for f, h in enumerate(HALO):
        for j in range(h):
            z = j + (CZ - h) * (1 - c)
            for half in range(2):
                if half == 0:
                    src = stack[CZ * f + z]
                else:
                    src = vel_s[f, z] if f < 3 else ph_s[z] if f == PH else vo_s[f - O0, z]
                lanes = pl.ds(CY * half, CY)
                main[n, :, lanes] = src
                diag[n, 0:HX, lanes] = src[CX - HX :]
                diag[n, HX:, lanes] = src[:HX]
            n += 1


def first_kernel(
    coefs, core, stack, vel_s, ph_s, po_s, vo_s, gxr, gxs, mr, ms, dr, ds,
    e, b, u, q, pot, lph, g, lv, send, p0, p1, p2,
):
    tension = 0.5 * coefs[1]
    viscosity = 0.1 * coefs[2]
    interface = 0.5 * coefs[3]
    c = core[0]

    n = 0
    for f, h in enumerate(HALO):
        mid = BASE[f] + h
        for z in range(CZ):
            for half, x in enumerate((gxr, gxs)):
                if half == 0:
                    src = stack[CZ * f + z]
                else:
                    src = vel_s[f, z] if f < 3 else ph_s[z] if f == PH else po_s[z] if f == PO else vo_s[f - O0, z]
                lanes = pl.ds(CY * half, CY)
                e[mid + z, HX : HX + CX, lanes] = src
                if f <= PH:
                    e[mid + z, 0:HX, lanes] = x[CZ * f + z, 0:HX]
                    e[mid + z, HX + CX :, lanes] = x[CZ * f + z, HX:]
                else:
                    k = CZ * (f - PO) + z
                    pair, row = CZ * PO + k // 2, HX * (k % 2)
                    e[mid + z, HX - NEAR : HX, lanes] = x[pair, row : row + NEAR]
                    e[mid + z, HX + CX : HX + CX + NEAR, lanes] = x[pair, row + NEAR : row + HX]
        for j in range(h):
            lo, hi = low_high(c, mr, ms, n)
            e[BASE[f] + j, HX : HX + CX] = lo
            e[mid + CZ + j, HX : HX + CX] = hi
            lo, hi = low_high(c, dr, ds, n)
            e[BASE[f] + j, 0:HX] = lo[0:HX]
            e[BASE[f] + j, HX + CX :] = lo[HX:]
            e[mid + CZ + j, 0:HX] = hi[0:HX]
            e[mid + CZ + j, HX + CX :] = hi[HX:]
            n += 1

    def at(field, z):
        return e[BASE[field] + HALO[field] + z]

    def potential(t):
        z = t - 2
        a = at(PH, z)
        lap = lap_of(a, at(PH, z + 1), at(PH, z - 1))
        lph[t] = lap
        pot[t] = a * a * a - a - interface * lap

    loop(8, potential)

    def provisional(field, z, grad, here):
        a = at(field, z)
        zu, zd = at(field, z + 1), at(field, z - 1)
        xu, xd, yu, yd = x_up(a), x_dn(a), y_up(a), y_dn(a)
        lap = (zu + zd) + (xu + xd) + (yu + yd) - 6.0 * a
        advect = at(V0, z) * (zu - zd) + at(V1, z) * (xu - xd) + at(V2, z) * (yu - yd)
        value = a - (0.5 * DT) * advect + (DT * viscosity) * lap + (DT * tension) * (here * grad)
        return value, lap

    def along(t):
        z = t - 2
        grad = 0.5 * (at(PH, z + 1) - at(PH, z - 1))
        p0[t], lv[0, t] = provisional(V0, z, grad, pot[t])

    loop(8, along)

    def across(t):
        z = t - 1
        a = at(PH, z)
        here = pot[t + 1]
        g0 = 0.5 * (at(PH, z + 1) - at(PH, z - 1))
        g1 = dx(a)
        g2 = dy(a)
        g[0, t] = g0
        g[1, t] = g1
        g[2, t] = g2
        p1[t], lv[1, t] = provisional(V1, z, g1, here)
        p2[t], lv[2, t] = provisional(V2, z, g2, here)

    loop(6, across)

    def source(t):
        b[t] = -(0.5 * (p0[t + 2] - p0[t]) + dx(p1[t]) + dy(p2[t]))
        q[0, t] = p0[t + 1] - at(O0, t - 1)

    loop(6, source)

    def second_source(t):
        q1 = p1[t + 1] - at(O1, t)
        q2 = p2[t + 1] - at(O2, t)
        q[1, t + 1] = q1
        q[2, t + 1] = q2
        u[t] = 0.5 * (q[0, t + 2] - q[0, t]) + dx(q1) + dy(q2)

    loop(4, second_source)

    for j in range(4):
        send[j] = b[j + 2 * c, NEAR : ROWS - NEAR]
    for j in range(2):
        send[4 + j] = u[j + 2 * (1 - c), NEAR : ROWS - NEAR]


def rows_of(a):
    return (a[0:8] + a[8:16]) + (a[16:24] + a[24:32])


def weight_kernel(coefs, e, q, pot, lph, g, lv, adj, w, part, edge):
    mobility = 0.1 * coefs[0]

    def at(field, z):
        return e[BASE[field] + HALO[field] + z]

    sums = [jnp.zeros((8, CY), jnp.float32)] * 5
    for t in range(CZ):
        here = pot[t + 2]
        lap = lph[t + 2]
        gs = [g[i, t + 1] for i in range(3)]
        up, dn = pot[t + 3] * g[0, t + 2], pot[t + 1] * g[0, t]
        w1 = 0.5 * (up - dn) + dx(here * gs[1]) + dy(here * gs[2])
        w2 = 0.5 * (lv[0, t + 3] - lv[0, t + 1]) + dx(lv[1, t + 1]) + dy(lv[2, t + 1])
        up, dn = lph[t + 3] * g[0, t + 2], lph[t + 1] * g[0, t]
        w3 = 0.5 * (up - dn) + dx(lap * gs[1]) + dy(lap * gs[2])
        w[0, t] = own(w1)
        w[1, t] = own(w2)
        w[2, t] = own(w3)
        lap_pot = lap_of(here, pot[t + 3], pot[t + 1])
        lap_lap = lap_of(lap, lph[t + 3], lph[t + 1])
        flow = at(V0, t) * gs[0] + at(V1, t) * gs[1] + at(V2, t) * gs[2]
        c = at(PH, t) - DT * flow + (DT * mobility) * lap_pot - at(PO, t)
        adj[t] = c
        qs = [q[i, t + 1] for i in range(3)]
        qg = qs[0] * gs[0] + qs[1] * gs[1] + qs[2] * gs[2]
        ql = qs[0] * lv[0, t + 2] + qs[1] * lv[1, t + 1] + qs[2] * lv[2, t + 1]
        terms = (own(c * lap_pot), own(here * qg), own(ql), own(lap * qg), own(c * lap_lap))
        sums = [s + rows_of(a) for s, a in zip(sums, terms)]
    for k in range(5):
        part[k] = sums[k]
    for k, z in ((0, CZ - 1), (1, 0)):
        edge[k, 0] = q[1, z + 1, NEAR : ROWS - NEAR]
        edge[k, 1] = q[2, z + 1, NEAR : ROWS - NEAR]
        for j in range(2):
            edge[k, 2 + j] = adj[2 * (1 - k) + j, NEAR : ROWS - NEAR]


def shifted(c, zu, zd):
    return (6.0 + SHIFT) * c - ((zu + zd) + (x_up(c) + x_dn(c)) + (y_up(c) + y_dn(c)))


def moment_kernel(core, b6, u4, r, s, w, part, edge, out, bb, uu, f, af, a2f, ab, au, send, a3f, a2b, a2u):
    c = core[0]
    near = pl.ds(NEAR, ROWS - 2 * NEAR)
    for j in range(4):
        lo, hi = low_high(c, r, s, j)
        bb[j, near] = lo
        bb[10 + j, near] = hi
    for j in range(2):
        lo, hi = low_high(c, r, s, 4 + j)
        uu[j, near] = lo
        uu[6 + j, near] = hi
    bb[4:10] = b6[...]
    uu[2:6] = u4[...]

    def wide(t):
        a = bb[t + 2]
        across = (pltpu.roll(a, ROWS - 2, 0) + pltpu.roll(a, 2, 0)) + (
            pltpu.roll(a, LANES - 2, 1) + pltpu.roll(a, 2, 1)
        )
        f[t] = 0.25 * ((bb[t + 4] + bb[t]) + across) - 1.5 * a

    loop(10, wide)

    def apply(src, dst, count):
        def body(t):
            dst[t] = shifted(src[t + 1], src[t + 2], src[t])

        loop(count, body)

    apply(f, af, 8)
    apply(af, a2f, 6)
    apply(a2f, a3f, 4)
    apply(bb.at[pl.ds(2, 10)], ab, 8)
    apply(ab.at[pl.ds(1, 6)], a2b, 4)
    apply(uu, au, 6)
    apply(au, a2u, 4)

    rows = pl.ds(HX, CX)
    lanes = pl.ds(0, CY)
    acc = [jnp.zeros((8, CY), jnp.float32)] * 40
    for t in range(CZ):
        vb, vab, va2b = bb[t + 5, rows, lanes], ab[t + 2, rows, lanes], a2b[t, rows, lanes]
        vu, vau, va2u = uu[t + 2, rows, lanes], au[t + 1, rows, lanes], a2u[t, rows, lanes]
        vf, vaf, va2f, va3f = (
            f[t + 3, rows, lanes], af[t + 2, rows, lanes], a2f[t + 1, rows, lanes], a3f[t, rows, lanes],
        )
        terms = [
            vb * vb, vb * vab, vab * vab, vab * va2b,
            vu * vu, vu * vau, vau * vau, vau * va2u,
            vu * vf, vu * vaf, vu * va2f, vau * va2f, va2u * va2f,
            vf * vf, vf * vaf, vaf * vaf, vaf * va2f, va2f * va2f, va2f * va3f,
        ]
        for k in range(3):
            wk = w[k, t]
            terms += [a * wk for a in (vu, vau, vf, vaf, va2f, vb, vab)]
        acc = [x + rows_of(a) for x, a in zip(acc, terms)]
    rows_list = [jnp.sum(a, axis=0, keepdims=True) for a in acc]
    rows_list += [jnp.sum(part[k], axis=0, keepdims=True) for k in range(5)]
    rows_list += [jnp.zeros((1, CY), jnp.float32)] * (48 - NUM_SUMS)
    table = jnp.concatenate(rows_list, axis=0)
    totals = jnp.sum(table, axis=1, keepdims=True)
    line = lax.broadcasted_iota(jnp.int32, (48, SLOTS), 1)
    which = lax.broadcasted_iota(jnp.int32, (48, SLOTS), 0)
    row = jnp.sum(jnp.where(line == which, totals, 0.0), axis=0, keepdims=True)
    out[...] = jnp.broadcast_to(row, (DEVICES, SLOTS))
    send[0:4] = edge[c]
    send[4] = a2f[3 - c, near]
    send[5] = au[3 - c, near]


def steps(m0, m1, m2, m3):
    alpha = m0 / m1
    norm = m0 * ((m0 * m2) / (m1 * m1) - 1.0)
    beta = norm / m0
    one = 1.0 + beta
    curve = one * one * m1 - 2.0 * one * alpha * m2 + alpha * alpha * m3
    second = norm / curve
    return alpha + second * one, -second * alpha


def last_kernel(
    coefs, core, gathered, bb, uu, f, af, a2f, ab, au, ri, si, e, q, adj4, pot, g,
    phase_back, velocity_back, params, phi, pr, pa, adj, qe,
):
    c = core[0]
    near = pl.ds(NEAR, ROWS - 2 * NEAR)
    for i in range(2):
        lo, hi = low_high(c, ri, si, i)
        qe[i, 0, near] = lo
        qe[i, 5, near] = hi
        qe[i, 1:5] = q[i + 1, 1:5]
        lo, hi = low_high(c, ri, si, 2 + i)
        adj[i, near] = lo
        adj[6 + i, near] = hi
    adj[2:6] = adj4[...]
    mobility = 0.1 * coefs[0]
    tension = 0.5 * coefs[1]
    viscosity = 0.1 * coefs[2]
    interface = 0.5 * coefs[3]

    total = jnp.sum(gathered[...], axis=0, keepdims=True)
    line = lax.broadcasted_iota(jnp.int32, (1, SLOTS), 1)

    def s(k):
        return jnp.sum(jnp.where(line == k, total, 0.0), axis=1, keepdims=True)

    c0, c1 = steps(s(0), s(1), s(2), s(3))
    m_uu = [s(4 + k) for k in range(4)]
    m_uf = [s(8 + k) for k in range(5)]
    m_ff = [s(13 + k) for k in range(6)]
    moments = [
        m_uu[k] - 2.0 * (c0 * m_uf[k] + c1 * m_uf[k + 1])
        + (c0 * c0) * m_ff[k] + (2.0 * c0 * c1) * m_ff[k + 1] + (c1 * c1) * m_ff[k + 2]
        for k in range(4)
    ]
    e0, e1 = steps(*moments)
    coef = (e0, e1, -e0 * c0, -(e0 * c1 + e1 * c0), -e1 * c1, -c0, -c1)

    def meet(k):
        value = coef[0] * s(19 + 7 * k)
        for j in range(1, 7):
            value = value + coef[j] * s(19 + 7 * k + j)
        return value

    scale = 1.0 / (256 * 64 * 256)
    g0 = DT * s(40)
    g1 = DT * (s(41) - meet(0))
    g2 = DT * (s(42) - meet(1))
    g3 = -((DT * mobility) * s(44) + (DT * tension) * (s(43) - meet(2)))
    place = lax.broadcasted_iota(jnp.int32, (1, CY), 1)
    packed = jnp.where(place == 0, g0, jnp.where(place == 1, g1, jnp.where(place == 2, g2, g3)))
    params[...] = packed * scale

    def combine(t):
        value = coef[0] * uu[t + 1] + coef[1] * au[t] + coef[2] * f[t + 2] + coef[3] * af[t + 1]
        phi[t + 1] = value + coef[4] * a2f[t] + coef[5] * bb[t + 4] + coef[6] * ab[t + 1]

    loop(6, combine)
    rows = near
    a_lo, a_hi = low_high(c, ri, si, 4)
    u_lo, u_hi = low_high(c, ri, si, 5)
    for t, a2, a1 in ((0, a_lo, u_lo), (7, a_hi, u_hi)):
        value = coef[0] * uu[t, rows] + coef[1] * a1 + coef[2] * f[t + 1, rows] + coef[3] * af[t, rows]
        phi[t, rows] = value + coef[4] * a2 + coef[5] * bb[t + 3, rows] + coef[6] * ab[t, rows]

    def at(field, z):
        return e[BASE[field] + HALO[field] + z]

    def project(t):
        c = phi[t + 1]
        r0 = q[0, t] + 0.5 * (phi[t + 2] - phi[t])
        r1 = qe[0, t] + dx(c)
        r2 = qe[1, t] + dy(c)
        pr[0, t] = r0
        pr[1, t] = r1
        pr[2, t] = r2
        d = adj[t + 1]
        lap = adj[t + 2] + adj[t] + (x_up(d) + x_dn(d)) + (y_up(d) + y_dn(d)) - 6.0 * d
        pa[t] = (DT * mobility) * lap + (DT * tension) * (r0 * g[0, t] + r1 * g[1, t] + r2 * g[2, t])

    loop(6, project)

    def finish(t):
        v0, v1, v2 = at(V0, t), at(V1, t), at(V2, t)
        v0u, v0d = at(V0, t + 1), at(V0, t - 1)
        c = adj[t + 2]
        here = pot[t + 2]
        ph = at(PH, t)
        lam = pa[t + 1]
        lap = pa[t + 2] + pa[t] + (x_up(lam) + x_dn(lam)) + (y_up(lam) + y_dn(lam)) - 6.0 * lam
        up = v0u * adj[t + 3] - tension * (pot[t + 3] * pr[0, t + 2])
        dn = v0d * adj[t + 1] - tension * (pot[t + 1] * pr[0, t])
        div = 0.5 * (up - dn)
        div = div + dx(v1 * c - tension * (here * pr[1, t + 1]))
        div = div + dy(v2 * c - tension * (here * pr[2, t + 1]))
        value = c + DT * div + (3.0 * ph * ph - 1.0) * lam - interface * lap
        phase_back[t] = own(value)
        r = [pr[i, t + 1] for i in range(3)]
        vel = (v0, v1, v2)
        grads = [[], [], []]
        for i, field in enumerate((V0, V1, V2)):
            grads[0].append(0.5 * (at(field, t + 1) - at(field, t - 1)))
            grads[1].append(dx(vel[i]))
            grads[2].append(dy(vel[i]))
        for k in range(3):
            mix = r[0] * grads[k][0] + r[1] * grads[k][1] + r[2] * grads[k][2]
            ru, rd = pr[k, t + 2], pr[k, t]
            moved = (viscosity + 0.5 * v0u) * ru + (viscosity - 0.5 * v0d) * rd
            moved = moved + x_up((viscosity + 0.5 * v1) * r[k]) + x_dn((viscosity - 0.5 * v1) * r[k])
            moved = moved + y_up((viscosity + 0.5 * v2) * r[k]) + y_dn((viscosity - 0.5 * v2) * r[k])
            moved = moved - (6.0 * viscosity) * r[k]
            value = r[k] + DT * (moved - mix - c * g[k, t + 1])
            velocity_back[k, t] = own(value)

    loop(4, finish)


def f32(*shape):
    return jax.ShapeDtypeStruct(shape, jnp.float32)


def layers(*lead):
    return f32(*lead, ROWS, LANES)


def scratch(*lead):
    return pltpu.VMEM((*lead, ROWS, LANES), jnp.float32)


VM = pl.BlockSpec(memory_space=pltpu.VMEM)
SM = pl.BlockSpec(memory_space=pltpu.SMEM)
PARAMS = pltpu.CompilerParams(vmem_limit_bytes=12 * 1024 * 1024)
SWAP = [(0, 1), (1, 0)]


def role_shift(value, cross):
    gx, gy, gz = (lax.axis_size(a) for a in ("gx", "gy", "gz"))
    pairs = []
    for x in range(gx):
        for y in range(gy):
            for i in range(gz):
                target = (1 - x if cross else x, y, (i + 1 - 2 * y) % gz)
                pairs.append(((x * gy + y) * gz + i, (target[0] * gy + y) * gz + target[2]))
    return lax.ppermute(value, ("gx", "gy", "gz"), pairs)


def ring(value, step):
    count = lax.axis_size("gz")
    return lax.ppermute(value, "gz", [(i, (i + step) % count) for i in range(count)])


def swap(value):
    return lax.ppermute(value, "gy", SWAP)


def call(kernel, outs, ins, scratches, name, smem):
    return pl.pallas_call(
        kernel,
        out_shape=outs,
        in_specs=[SM] * smem + [VM] * (len(ins) - smem),
        out_specs=jax.tree.map(lambda _: VM, outs),
        scratch_shapes=scratches,
        compiler_params=PARAMS,
        name=name,
    )(*ins)


def local(phase, velocity, phase_obs, velocity_obs, coefs):
    core = lax.axis_index("gy").astype(jnp.int32).reshape(1)
    mine = (velocity, phase, phase_obs, velocity_obs)
    theirs = lax.optimization_barrier(tuple(swap(a) for a in mine))
    stack, edges, coefs = pl.pallas_call(
        load_kernel,
        out_shape=(f32(8 * CZ, CX, CY), f32(6 * CZ, 2 * HX, CY), f32(4)),
        in_specs=[pl.BlockSpec(memory_space=pltpu.HBM)] * 5,
        out_specs=(VM, VM, VM),
        scratch_shapes=[pltpu.SemaphoreType.DMA((9,))],
        compiler_params=PARAMS,
        name="load",
    )(*mine, coefs)
    gxr = lax.ppermute(edges, "gx", SWAP)
    main, diag = call(
        pack_kernel,
        (f32(SENT, CX, LANES), f32(SENT, 2 * HX, LANES)),
        (core, stack, theirs[0], theirs[1], theirs[3]),
        [],
        "pack",
        1,
    )
    mr = role_shift(main, False)
    dr = role_shift(diag, True)
    gxs = swap(gxr)
    ms, ds = swap(mr), swap(dr)
    narrow = ROWS - 2 * NEAR
    e, b, u, q, pot, lph, g, lv, send = call(
        first_kernel,
        (layers(TOTAL), layers(6), layers(4), layers(3, 6), layers(8), layers(8), layers(3, 6), layers(3, 8),
         f32(6, narrow, LANES)),
        (coefs, core, stack, *theirs, gxr, gxs, mr, ms, dr, ds),
        [scratch(8), scratch(6), scratch(6)],
        "first",
        2,
    )
    r2 = role_shift(send, False)
    adj, w, part, edge = call(
        weight_kernel,
        (layers(4), f32(3, CZ, CX, CY), f32(5, 8, CY), f32(2, 4, narrow, LANES)),
        (coefs, e, q, pot, lph, g, lv),
        [],
        "weights",
        1,
    )
    r2, w, part, edge = lax.optimization_barrier((r2, w, part, edge))
    s2 = swap(r2)
    sums, bb, uu, f, af, a2f, ab, au, send = call(
        moment_kernel,
        (f32(DEVICES, SLOTS), layers(14), layers(8), layers(10), layers(8), layers(6), layers(8), layers(6),
         f32(6, narrow, LANES)),
        (core, b, u, r2, s2, w, part, edge),
        [scratch(4), scratch(4), scratch(4)],
        "moments",
        1,
    )
    ri = role_shift(send, False)
    gathered = lax.all_to_all(sums.reshape(DEVICES, 1, SLOTS), ("gx", "gy", "gz"), 0, 0).reshape(DEVICES, SLOTS)
    ri, gathered = lax.optimization_barrier((ri, gathered))
    si = swap(ri)
    phase_back, velocity_back, params = call(
        last_kernel,
        (f32(CZ, CX, CY), f32(3, CZ, CX, CY), f32(1, CY)),
        (coefs, core, gathered, bb, uu, f, af, a2f, ab, au, ri, si, e, q, adj, pot, g),
        [scratch(8), scratch(3, 6), scratch(6), scratch(8), scratch(2, 6)],
        "last",
        2,
    )
    return phase_back, velocity_back, params[0, :4]


def solution(mesh):
    return jax.shard_map(
        local,
        mesh=mesh,
        in_specs=(
            P("gz", "gx", "gy"),
            P(None, "gz", "gx", "gy"),
            P("gz", "gx", "gy"),
            P(None, "gz", "gx", "gy"),
            P(),
        ),
        out_specs=(P("gz", "gx", "gy"), P(None, "gz", "gx", "gy"), P()),
        check_vma=False,
    )
```

time: 117 us -> 93.1 us (0.80)
  waiting for transfers between devices: 40.1 us -> 17.5 us
  starting transfers between devices: 26.5 us -> 33.7 us
  Pallas kernels: 18.5 us -> 15.1 us
  blocking collectives: 23.6 us -> 21.3 us
  other arithmetic: 2.21 us -> 0 us
    ppermute x6 -> x14, waiting for transfers between devices: 40.1 us -> 17.5 us  [the longest x4 13.9 us: role_shift(): return lax.ppermute(value, ('gx', 'gy', 'gz'), pairs)]
    ppermute x6 -> x14, starting transfers between devices: 26.5 us -> 33.7 us  [the longest x4 23.4 us: role_shift(): return lax.ppermute(value, ('gx', 'gy', 'gz'), pairs)]
    pallas_call x4 -> x6, Pallas kernels: 18.5 us -> 15.1 us  [the longest x5 14.3 us: call(): pl.pallas_call(kernel, out_shape=outs, in_specs=[SM] * smem + [VM] * (len...]
    all_to_all x1, blocking collectives: 23.6 us -> 21.3 us  [local(): lax.all_to_all(sums.reshape(DEVICES, 1, SLOTS), ('gx', 'gy', 'gz'), 0, 0)]
    concatenate x5 -> x0, other arithmetic: 2.21 us -> none  [the longest x1 2 us: extend(): return jnp.concatenate([block, other], 2)]
    unnamed x42 -> x10, local copies, waits for them, and re-layouts: 3.61 us -> 4.19 us
  transfers between devices with their start and end apart: 6 -> 14, of which waited for: 5 -> 6; matrix products, arithmetic and copies ran while one was open for 0% -> 0% of each run, Pallas kernels for 0% -> 2%
where the time goes in v2:
time: 93.1 us; the launch traced here: 92.9 us
  starting transfers between devices  33.7 us (36%)
  blocking collectives  21.3 us (23%)
  waiting for transfers between devices  17.5 us (19%)
  Pallas kernels  15.1 us (16%)
  local copies, waits for them, and re-layouts  4.7 us (5%)
    ppermute x4, starting transfers between devices, role_shift(): return lax.ppermute(value, ('gx', 'gy', 'gz'), pairs)  23.4 us
    all_to_all x1, blocking collectives, local(): lax.all_to_all(sums.reshape(DEVICES, 1, SLOTS), ('gx', 'gy', 'gz'), 0, 0)  21.3 us
    pallas_call x5, Pallas kernels, call(): pl.pallas_call(kernel, out_shape=outs, in_specs=[SM] * smem + [VM] * (len...  14.3 us
    ppermute x4, waiting for transfers between devices, role_shift(): return lax.ppermute(value, ('gx', 'gy', 'gz'), pairs)  13.9 us
    ppermute x9, starting transfers between devices, swap(): return lax.ppermute(value, 'gy', SWAP)  9.49 us
    unnamed x10, local copies, waits for them, and re-layouts  4.19 us
    ppermute x9, waiting for transfers between devices, swap(): return lax.ppermute(value, 'gy', SWAP)  3.61 us
  transfers between devices with their start and end apart: 14, of which 6 were waited for; matrix products, arithmetic and copies ran while one was open for 0% of the time, Pallas kernels for 2%

profile of v2, /device:TPU:1, one launch (start us, length us, event | category | flops | bytes accessed | tf_op | source)
XLA Modules:
  0.0 92.9 jit_solution(18217338218699042780)
XLA Ops:
  0.6 3.3 %collective-permute-start = (f32[3,4,32,128]{3,2,1,0:T(8,128)}, f32[3,4,32,128]{3,2,1,0:T(8,128)S(1)}, u32[]{:S(2)}, u32[]{:S(2)}) collective-permute-start(f32[3,4,32,128]{3,2,1,0:T(8,128)} %vel.1), channel_id=1, source_target_pairs={{0,64},{64,0},{1,65},{65,1},{2,66},{66,2},{3,67},{67,3},{4,68},{68... | collective-permute-start | bytes 589832 | tf_op jit(solution)/shard_map/ppermute | solution.py:500
  4.6 0.9 copy-done
  5.5 0.9 copy-done.1
  6.4 0.8 copy-done.2
  7.3 0.8 copy-done.3
  8.1 0.7 copy-done.4
  8.8 0.8 load.1
  9.6 9.0 %collective-permute-start.6 = (f32[11,32,256]{2,1,0:T(8,128)S(1)}, f32[11,32,256]{2,1,0:T(8,128)S(1)}, u32[]{:S(2)}, u32[]{:S(2)}) collective-permute-start(f32[11,32,256]{2,1,0:T(8,128)S(1)} %get-tuple-element.50), channel_id=1, source_target_pairs={{0,1},{1,2},{2,3},{3,4},{4,5},{5,6},{6,7},{7,8},{8,9},{9,10},{10,1... | collective-permute-start | bytes 1081352 | tf_op jit(solution)/shard_map/ppermute | solution.py:491
  18.6 0.7 collective-permute-start.4
  19.5 9.2 %collective-permute-done.6.mr = f32[11,32,256]{2,1,0:T(8,128)S(1)} collective-permute-done((f32[11,32,256]{2,1,0:T(8,128)S(1)}, f32[11,32,256]{2,1,0:T(8,128)S(1)}, u32[]{:S(2)}, u32[]{:S(2)}) %collective-permute-start.6) | collective-permute-done | bytes 360480 | tf_op jit(solution)/shard_map/ppermute | solution.py:491
  28.6 3.2 %collective-permute-start.7 = (f32[11,32,256]{2,1,0:T(8,128)S(1)}, f32[11,32,256]{2,1,0:T(8,128)S(1)}, u32[]{:S(2)}, u32[]{:S(2)}) collective-permute-start(f32[11,32,256]{2,1,0:T(8,128)S(1)} %collective-permute-done.6.mr), channel_id=1, source_target_pairs={{0,64},{64,0},{1,65},{65,1},{2,66},{66,2},{3,67},{67,3},{4,68},{68... | collective-permute-start | bytes 1081352 | tf_op jit(solution)/shard_map/ppermute | solution.py:500
  32.3 1.1 %collective-permute-done.5.gxs = f32[24,16,128]{2,1,0:T(8,128)S(1)} collective-permute-done((f32[24,16,128]{2,1,0:T(8,128)S(1)}, f32[24,16,128]{2,1,0:T(8,128)S(1)}, u32[]{:S(2)}, u32[]{:S(2)}) %collective-permute-start.5) | collective-permute-done | bytes 196640 | tf_op jit(solution)/shard_map/ppermute | solution.py:500
  33.6 4.5 %first.1 = (f32[54,48,256]{2,1,0:T(8,128)S(1)}, f32[6,48,256]{2,1,0:T(8,128)S(1)}, f32[4,48,256]{2,1,0:T(8,128)S(1)}, f32[3,6,48,256]{3,2,1,0:T(8,128)S(1)}, f32...) custom-call(f32[4]{0:T(128)S(1)} %get-tuple-element.43.coefs, ...), custom_call_target="tpu_custom_call" | custom-call | tf_op jit(solution)/shard_map/first/pallas_call | solution.py:504
  38.2 6.4 %collective-permute-start.10 = (f32[6,40,256]{2,1,0:T(8,128)S(1)}, f32[6,40,256]{2,1,0:T(8,128)S(1)}, u32[]{:S(2)}, u32[]{:S(2)}) collective-permute-start(f32[6,40,256]{2,1,0:T(8,128)S(1)} %get-tuple-element.54), channel_id=1, source_target_pairs={{0,1},{1,2},{2,3},{3,4},{4,5},{5,6},{6,7},{7,8},{8,9},{9,10},{10,1... | collective-permute-start | bytes 737288 | tf_op jit(solution)/shard_map/ppermute | solution.py:491
  44.6 1.1 %weights.1 = (f32[4,48,256]{2,1,0:T(8,128)S(1)}, f32[3,4,32,128]{3,2,1,0:T(8,128)S(1)}, f32[5,8,128]{2,1,0:T(8,128)S(1)}, f32[2,4,40,256]{3,2,1,0:T(8,128)S(1)}) custom-call(f32[4]{0:T(128)S(1)} %get-tuple-element.43.coefs, f32[54,48,256]{2,1,0:T(8,128)S(1)} %get-tuple-element.55.e, f32[3,6,48,256]{3,2,1,0:T(8,128)S(1)} %get-tuple-element.56.q, ...), custom_call_target="tpu_custom_call" | custom-call | tf_op jit(solution)/shard_map/weights/pallas_call | solution.py:504
  45.7 4.7 %collective-permute-done.10.r = f32[6,40,256]{2,1,0:T(8,128)S(1)} collective-permute-done((f32[6,40,256]{2,1,0:T(8,128)S(1)}, f32[6,40,256]{2,1,0:T(8,128)S(1)}, u32[]{:S(2)}, u32[]{:S(2)}) %collective-permute-start.10) | collective-permute-done | bytes 245792 | tf_op jit(solution)/shard_map/ppermute | solution.py:491
  50.4 0.8 collective-permute-start.11
  51.2 1.1 %collective-permute-done.11.s = f32[6,40,256]{2,1,0:T(8,128)S(1)} collective-permute-done((f32[6,40,256]{2,1,0:T(8,128)S(1)}, f32[6,40,256]{2,1,0:T(8,128)S(1)}, u32[]{:S(2)}, u32[]{:S(2)}) %collective-permute-start.11) | collective-permute-done | bytes 245792 | tf_op jit(solution)/shard_map/ppermute | solution.py:500
  52.3 5.3 %moments.1 = (f32[256,64]{1,0:T(8,128)S(1)}, f32[14,48,256]{2,1,0:T(8,128)S(1)}, f32[8,48,256]{2,1,0:T(8,128)S(1)}, f32[10,48,256]{2,1,0:T(8,128)S(1)}, f32[8,48...) custom-call(s32[1]{0:T(128)} %bitcast.core, ...), custom_call_target="tpu_custom_call" | custom-call | tf_op jit(solution)/shard_map/moments/pallas_call | solution.py:504
  57.6 7.9 %collective-permute-start.12 = (f32[6,40,256]{2,1,0:T(8,128)S(1)}, f32[6,40,256]{2,1,0:T(8,128)S(1)}, u32[]{:S(2)}, u32[]{:S(2)}) collective-permute-start(f32[6,40,256]{2,1,0:T(8,128)S(1)} %get-tuple-element.68), channel_id=1, source_target_pairs={{0,1},{1,2},{2,3},{3,4},{4,5},{5,6},{6,7},{7,8},{8,9},{9,10},{10,1... | collective-permute-start | bytes 737288 | tf_op jit(solution)/shard_map/ppermute | solution.py:491
  65.5 21.3 %all_to_all.5 = f32[256,1,64]{2,1,0:T(1,128)S(1)} all-to-all(f32[256,1,64]{2,1,0:T(1,128)S(1)} %bitcast.8), channel_id=1, replica_groups=mesh['gx'=2,'gy'=2,'gz'=64] {'gx','gy','gz'}, dimensions={0} | all-to-all | bytes 131072 | tf_op jit(solution)/shard_map/all_to_all | solution.py:572
  86.8 1.1 %collective-permute-start.13 = (f32[6,40,256]{2,1,0:T(8,128)S(1)}, f32[6,40,256]{2,1,0:T(8,128)S(1)}, u32[]{:S(2)}, u32[]{:S(2)}) collective-permute-start(f32[6,40,256]{2,1,0:T(8,128)S(1)} %collective-permute-done.12.ri), channel_id=1, source_target_pairs={{0,64},{64,0},{1,65},{65,1},{2,66},{66,2},{3,67},{67,3},{4,68},{68... | collective-permute-start | bytes 737288 | tf_op jit(solution)/shard_map/ppermute | solution.py:500
  87.9 1.1 %collective-permute-done.13.si = f32[6,40,256]{2,1,0:T(8,128)S(1)} collective-permute-done((f32[6,40,256]{2,1,0:T(8,128)S(1)}, f32[6,40,256]{2,1,0:T(8,128)S(1)}, u32[]{:S(2)}, u32[]{:S(2)}) %collective-permute-start.13) | collective-permute-done | bytes 245792 | tf_op jit(solution)/shard_map/ppermute | solution.py:500
  89.0 3.4 %last.1 = (f32[4,32,128]{2,1,0:T(8,128)}, f32[3,4,32,128]{3,2,1,0:T(8,128)}, f32[1,128]{1,0:T(1,128)S(1)}) custom-call(f32[4]{0:T(128)S(1)} %get-tuple-element.43.coefs, s32[1]{0:T(128)} %bitcast.core, f32[256,64]{1,0:T(8,128)S(1)} %bitcast.7, f32[14,48,256]{2,1,0:T(8,128)S(1)} %get-tuple-element.71.bb, f32[8,48,256]{2,1,0:T(8,128)S(1)} %get-tuple-element.72.uu, ...), custom_call_target="tpu_custom_call" | custom-call | tf_op jit(solution)/shard_map/last/pallas_call | solution.py:504
  (22 shorter events, 2.1 us)
Async XLA Ops:
  0.6 8.9 %collective-permute-start = (f32[3,4,32,128]{3,2,1,0:T(8,128)}, f32[3,4,32,128]{3,2,1,0:T(8,128)S(1)}, u32[]{:S(2)}, u32[]{:S(2)}) collective-permute-start(f32[3,4,32,128]{3,2,1,0:T(8,128)} %vel.1), channel_id=1, source_target_pairs={{0,64},{64,0},{1,65},{65,1},{2,66},{66,2},{3,67},{67,3},{4,68},{68... | collective-permute-start | bytes 589832 | tf_op jit(solution)/shard_map/ppermute | solution.py:500
  4.0 5.6 %collective-permute-start.3 = (f32[3,4,32,128]{3,2,1,0:T(8,128)}, f32[3,4,32,128]{3,2,1,0:T(8,128)S(1)}, u32[]{:S(2)}, u32[]{:S(2)}) collective-permute-start(f32[3,4,32,128]{3,2,1,0:T(8,128)} %vo.1), channel_id=1, source_target_pairs={{0,64},{64,0},{1,65},{65,1},{2,66},{66,2},{3,67},{67,3},{4,68},{68... | collective-permute-start | bytes 589832 | tf_op jit(solution)/shard_map/ppermute | solution.py:500
  4.1 5.5 %collective-permute-start.1 = (f32[4,32,128]{2,1,0:T(8,128)}, f32[4,32,128]{2,1,0:T(8,128)S(1)}, u32[]{:S(2)}, u32[]{:S(2)}) collective-permute-start(f32[4,32,128]{2,1,0:T(8,128)} %ph.1), channel_id=1, source_target_pairs={{0,64},{64,0},{1,65},{65,1},{2,66},{66,2},{3,67},{67,3},{4,68},{68... | collective-permute-start | bytes 196616 | tf_op jit(solution)/shard_map/ppermute | solution.py:500
  4.5 5.1 %collective-permute-start.2 = (f32[4,32,128]{2,1,0:T(8,128)}, f32[4,32,128]{2,1,0:T(8,128)S(1)}, u32[]{:S(2)}, u32[]{:S(2)}) collective-permute-start(f32[4,32,128]{2,1,0:T(8,128)} %po.1), channel_id=1, source_target_pairs={{0,64},{64,0},{1,65},{65,1},{2,66},{66,2},{3,67},{67,3},{4,68},{68... | collective-permute-start | bytes 196616 | tf_op jit(solution)/shard_map/ppermute | solution.py:500
  4.6 0.9 copy-start
  5.5 0.9 copy-start.1
  6.4 0.8 copy-start.2
  7.3 0.8 copy-start.3
  8.1 0.7 copy-start.4
  9.6 19.0 %collective-permute-start.6 = (f32[11,32,256]{2,1,0:T(8,128)S(1)}, f32[11,32,256]{2,1,0:T(8,128)S(1)}, u32[]{:S(2)}, u32[]{:S(2)}) collective-permute-start(f32[11,32,256]{2,1,0:T(8,128)S(1)} %get-tuple-element.50), channel_id=1, source_target_pairs={{0,1},{1,2},{2,3},{3,4},{4,5},{5,6},{6,7},{7,8},{8,9},{9,10},{10,1... | collective-permute-start | bytes 1081352 | tf_op jit(solution)/shard_map/ppermute | solution.py:491
  18.6 13.2 %collective-permute-start.4 = (f32[24,16,128]{2,1,0:T(8,128)S(1)}, f32[24,16,128]{2,1,0:T(8,128)S(1)}, u32[]{:S(2)}, u32[]{:S(2)}) collective-permute-start(f32[24,16,128]{2,1,0:T(8,128)S(1)} %get-tuple-element.49), channel_id=1, source_target_pairs={{0,128},{128,0},{1,129},{129,1},{2,130},{130,2},{3,131},{131,3},{4... | collective-permute-start | bytes 589832 | tf_op jit(solution)/shard_map/ppermute | solution.py:528
  19.4 12.4 %collective-permute-start.8 = (f32[11,16,256]{2,1,0:T(8,128)S(1)}, f32[11,16,256]{2,1,0:T(8,128)S(1)}, u32[]{:S(2)}, u32[]{:S(2)}) collective-permute-start(f32[11,16,256]{2,1,0:T(8,128)S(1)} %get-tuple-element.51), channel_id=1, source_target_pairs={{0,129},{1,130},{2,131},{3,132},{4,133},{5,134},{6,135},{7,136},{8... | collective-permute-start | bytes 540680 | tf_op jit(solution)/shard_map/ppermute | solution.py:491
  28.6 5.0 %collective-permute-start.7 = (f32[11,32,256]{2,1,0:T(8,128)S(1)}, f32[11,32,256]{2,1,0:T(8,128)S(1)}, u32[]{:S(2)}, u32[]{:S(2)}) collective-permute-start(f32[11,32,256]{2,1,0:T(8,128)S(1)} %collective-permute-done.6.mr), channel_id=1, source_target_pairs={{0,64},{64,0},{1,65},{65,1},{2,66},{66,2},{3,67},{67,3},{4,68},{68... | collective-permute-start | bytes 1081352 | tf_op jit(solution)/shard_map/ppermute | solution.py:500
  31.8 1.6 %collective-permute-start.5 = (f32[24,16,128]{2,1,0:T(8,128)S(1)}, f32[24,16,128]{2,1,0:T(8,128)S(1)}, u32[]{:S(2)}, u32[]{:S(2)}) collective-permute-start(f32[24,16,128]{2,1,0:T(8,128)S(1)} %collective-permute-done.4.gxr), channel_id=1, source_target_pairs={{0,64},{64,0},{1,65},{65,1},{2,66},{66,2},{3,67},{67,3},{4,68},{68... | collective-permute-start | bytes 589832 | tf_op jit(solution)/shard_map/ppermute | solution.py:500
  31.8 1.8 %collective-permute-start.9 = (f32[11,16,256]{2,1,0:T(8,128)S(1)}, f32[11,16,256]{2,1,0:T(8,128)S(1)}, u32[]{:S(2)}, u32[]{:S(2)}) collective-permute-start(f32[11,16,256]{2,1,0:T(8,128)S(1)} %collective-permute-done.8.dr), channel_id=1, source_target_pairs={{0,64},{64,0},{1,65},{65,1},{2,66},{66,2},{3,67},{67,3},{4,68},{68... | collective-permute-start | bytes 540680 | tf_op jit(solution)/shard_map/ppermute | solution.py:500
  38.2 12.2 %collective-permute-start.10 = (f32[6,40,256]{2,1,0:T(8,128)S(1)}, f32[6,40,256]{2,1,0:T(8,128)S(1)}, u32[]{:S(2)}, u32[]{:S(2)}) collective-permute-start(f32[6,40,256]{2,1,0:T(8,128)S(1)} %get-tuple-element.54), channel_id=1, source_target_pairs={{0,1},{1,2},{2,3},{3,4},{4,5},{5,6},{6,7},{7,8},{8,9},{9,10},{10,1... | collective-permute-start | bytes 737288 | tf_op jit(solution)/shard_map/ppermute | solution.py:491
  50.4 1.9 %collective-permute-start.11 = (f32[6,40,256]{2,1,0:T(8,128)S(1)}, f32[6,40,256]{2,1,0:T(8,128)S(1)}, u32[]{:S(2)}, u32[]{:S(2)}) collective-permute-start(f32[6,40,256]{2,1,0:T(8,128)S(1)} %collective-permute-done.10.r), channel_id=1, source_target_pairs={{0,64},{64,0},{1,65},{65,1},{2,66},{66,2},{3,67},{67,3},{4,68},{68... | collective-permute-start | bytes 737288 | tf_op jit(solution)/shard_map/ppermute | solution.py:500
  57.6 29.2 %collective-permute-start.12 = (f32[6,40,256]{2,1,0:T(8,128)S(1)}, f32[6,40,256]{2,1,0:T(8,128)S(1)}, u32[]{:S(2)}, u32[]{:S(2)}) collective-permute-start(f32[6,40,256]{2,1,0:T(8,128)S(1)} %get-tuple-element.68), channel_id=1, source_target_pairs={{0,1},{1,2},{2,3},{3,4},{4,5},{5,6},{6,7},{7,8},{8,9},{9,10},{10,1... | collective-permute-start | bytes 737288 | tf_op jit(solution)/shard_map/ppermute | solution.py:491
  86.8 2.2 %collective-permute-start.13 = (f32[6,40,256]{2,1,0:T(8,128)S(1)}, f32[6,40,256]{2,1,0:T(8,128)S(1)}, u32[]{:S(2)}, u32[]{:S(2)}) collective-permute-start(f32[6,40,256]{2,1,0:T(8,128)S(1)} %collective-permute-done.12.ri), channel_id=1, source_target_pairs={{0,64},{64,0},{1,65},{65,1},{2,66},{66,2},{3,67},{67,3},{4,68},{68... | collective-permute-start | bytes 737288 | tf_op jit(solution)/shard_map/ppermute | solution.py:500

commit v3 on v2

--- a/solution.py
+++ b/solution.py
@@ -10,12 +10,13 @@
 CZ, CX, CY = 4, 32, 128
 HX = 8
 NEAR = 4
+NARROW = (CX + 2 * HX) - 2 * NEAR
 ROWS = CX + 2 * HX
 LANES = 2 * CY
 DEVICES = 256
 
 V0, V1, V2, PH, PO, O0, O1, O2 = range(8)
-HALO = (3, 2, 2, 3, 0, 1, 0, 0)
+HALO = (2, 1, 1, 2, 0, 1, 0, 0)
 BASE = []
 _at = 0
 for _h in HALO:
@@ -68,7 +69,7 @@
         body(t)
         return carry
 
-    lax.fori_loop(0, count, step, 0)
+    lax.fori_loop(0, count, step, 0, unroll=2)
 
 
 def low_high(core, mine, theirs, j):
@@ -98,17 +99,14 @@
         out[at, row + NEAR : row + HX] = stack[wide + n, :NEAR]
 
 
-def pack_kernel(core, stack, vel_s, ph_s, vo_s, main, diag):
+def pack_kernel(core, stack, peer, main, diag):
     c = core[0]
     n = 0
     for f, h in enumerate(HALO):
         for j in range(h):
             z = j + (CZ - h) * (1 - c)
             for half in range(2):
-                if half == 0:
-                    src = stack[CZ * f + z]
-                else:
-                    src = vel_s[f, z] if f < 3 else ph_s[z] if f == PH else vo_s[f - O0, z]
+                src = (stack, peer)[half][CZ * f + z]
                 lanes = pl.ds(CY * half, CY)
                 main[n, :, lanes] = src
                 diag[n, 0:HX, lanes] = src[CX - HX :]
@@ -116,24 +114,12 @@
             n += 1
 
 
-def first_kernel(
-    coefs, core, stack, vel_s, ph_s, po_s, vo_s, gxr, gxs, mr, ms, dr, ds,
-    e, b, u, q, pot, lph, g, lv, send, p0, p1, p2,
-):
-    tension = 0.5 * coefs[1]
-    viscosity = 0.1 * coefs[2]
-    interface = 0.5 * coefs[3]
-    c = core[0]
-
-    n = 0
+def inner_kernel(stack, peer, gxr, gxs, e):
     for f, h in enumerate(HALO):
         mid = BASE[f] + h
         for z in range(CZ):
             for half, x in enumerate((gxr, gxs)):
-                if half == 0:
-                    src = stack[CZ * f + z]
-                else:
-                    src = vel_s[f, z] if f < 3 else ph_s[z] if f == PH else po_s[z] if f == PO else vo_s[f - O0, z]
+                src = (stack, peer)[half][CZ * f + z]
                 lanes = pl.ds(CY * half, CY)
                 e[mid + z, HX : HX + CX, lanes] = src
                 if f <= PH:
@@ -144,28 +130,41 @@
                     pair, row = CZ * PO + k // 2, HX * (k % 2)
                     e[mid + z, HX - NEAR : HX, lanes] = x[pair, row : row + NEAR]
                     e[mid + z, HX + CX : HX + CX + NEAR, lanes] = x[pair, row + NEAR : row + HX]
+
+
+def first_kernel(
+    coefs, core, inner, mr, ms, dr, ds, e, b, u, q, pot, lph, g, lv, send, far, p0,
+):
+    tension = 0.5 * coefs[1]
+    viscosity = 0.1 * coefs[2]
+    interface = 0.5 * coefs[3]
+    c = core[0]
+
+    n = 0
+    for f, h in enumerate(HALO):
+        high = BASE[f] + h + CZ
         for j in range(h):
             lo, hi = low_high(c, mr, ms, n)
             e[BASE[f] + j, HX : HX + CX] = lo
-            e[mid + CZ + j, HX : HX + CX] = hi
+            e[high + j, HX : HX + CX] = hi
             lo, hi = low_high(c, dr, ds, n)
             e[BASE[f] + j, 0:HX] = lo[0:HX]
             e[BASE[f] + j, HX + CX :] = lo[HX:]
-            e[mid + CZ + j, 0:HX] = hi[0:HX]
-            e[mid + CZ + j, HX + CX :] = hi[HX:]
+            e[high + j, 0:HX] = hi[0:HX]
+            e[high + j, HX + CX :] = hi[HX:]
             n += 1
 
     def at(field, z):
         return e[BASE[field] + HALO[field] + z]
 
     def potential(t):
-        z = t - 2
+        z = t - 1
         a = at(PH, z)
         lap = lap_of(a, at(PH, z + 1), at(PH, z - 1))
         lph[t] = lap
         pot[t] = a * a * a - a - interface * lap
 
-    loop(8, potential)
+    loop(6, potential)
 
     def provisional(field, z, grad, here):
         a = at(field, z)
@@ -177,46 +176,44 @@
         return value, lap
 
     def along(t):
-        z = t - 2
+        z = t - 1
         grad = 0.5 * (at(PH, z + 1) - at(PH, z - 1))
         p0[t], lv[0, t] = provisional(V0, z, grad, pot[t])
 
-    loop(8, along)
-
-    def across(t):
+    loop(6, along)
+
+    def slopes(t):
         z = t - 1
         a = at(PH, z)
-        here = pot[t + 1]
-        g0 = 0.5 * (at(PH, z + 1) - at(PH, z - 1))
-        g1 = dx(a)
-        g2 = dy(a)
-        g[0, t] = g0
-        g[1, t] = g1
-        g[2, t] = g2
-        p1[t], lv[1, t] = provisional(V1, z, g1, here)
-        p2[t], lv[2, t] = provisional(V2, z, g2, here)
-
-    loop(6, across)
-
-    def source(t):
-        b[t] = -(0.5 * (p0[t + 2] - p0[t]) + dx(p1[t]) + dy(p2[t]))
-        q[0, t] = p0[t + 1] - at(O0, t - 1)
-
-    loop(6, source)
-
-    def second_source(t):
-        q1 = p1[t + 1] - at(O1, t)
-        q2 = p2[t + 1] - at(O2, t)
-        q[1, t + 1] = q1
-        q[2, t + 1] = q2
-        u[t] = 0.5 * (q[0, t + 2] - q[0, t]) + dx(q1) + dy(q2)
-
-    loop(4, second_source)
-
+        g[0, t] = 0.5 * (at(PH, z + 1) - at(PH, z - 1))
+        g[1, t] = dx(a)
+        g[2, t] = dy(a)
+        q[0, t] = p0[t] - at(O0, z)
+
+    loop(6, slopes)
+
+    def across(z):
+        here = pot[z + 1]
+        p1, lv[1, z] = provisional(V1, z, g[1, z + 1], here)
+        p2, lv[2, z] = provisional(V2, z, g[2, z + 1], here)
+        b[z] = -(0.5 * (p0[z + 2] - p0[z]) + dx(p1) + dy(p2))
+        q1 = p1 - at(O1, z)
+        q2 = p2 - at(O2, z)
+        q[1, z + 1] = q1
+        q[2, z + 1] = q2
+        u[z] = 0.5 * (q[0, z + 2] - q[0, z]) + dx(q1) + dy(q2)
+
+    loop(4, across)
+
+    inside = pl.ds(NEAR, NARROW)
     for j in range(4):
-        send[j] = b[j + 2 * c, NEAR : ROWS - NEAR]
+        send[NARROW * j : NARROW * (j + 1)] = b[j, inside]
     for j in range(2):
-        send[4 + j] = u[j + 2 * (1 - c), NEAR : ROWS - NEAR]
+        send[NARROW * (4 + j) : NARROW * (5 + j)] = u[j + 2 * (1 - c), inside]
+    edge = 3 * (1 - c)
+    send[NARROW * 6 : NARROW * 6 + 1] = b[edge, NEAR - 1 : NEAR]
+    send[NARROW * 6 + 1 : NARROW * 6 + 2] = b[edge, ROWS - NEAR : ROWS - NEAR + 1]
+    far[...] = b[0, HX : HX + CX, :CY]
 
 
 def rows_of(a):
@@ -231,25 +228,25 @@
 
     sums = [jnp.zeros((8, CY), jnp.float32)] * 5
     for t in range(CZ):
-        here = pot[t + 2]
-        lap = lph[t + 2]
+        here = pot[t + 1]
+        lap = lph[t + 1]
         gs = [g[i, t + 1] for i in range(3)]
-        up, dn = pot[t + 3] * g[0, t + 2], pot[t + 1] * g[0, t]
+        up, dn = pot[t + 2] * g[0, t + 2], pot[t] * g[0, t]
         w1 = 0.5 * (up - dn) + dx(here * gs[1]) + dy(here * gs[2])
-        w2 = 0.5 * (lv[0, t + 3] - lv[0, t + 1]) + dx(lv[1, t + 1]) + dy(lv[2, t + 1])
-        up, dn = lph[t + 3] * g[0, t + 2], lph[t + 1] * g[0, t]
+        w2 = 0.5 * (lv[0, t + 2] - lv[0, t]) + dx(lv[1, t]) + dy(lv[2, t])
+        up, dn = lph[t + 2] * g[0, t + 2], lph[t] * g[0, t]
         w3 = 0.5 * (up - dn) + dx(lap * gs[1]) + dy(lap * gs[2])
         w[0, t] = own(w1)
         w[1, t] = own(w2)
         w[2, t] = own(w3)
-        lap_pot = lap_of(here, pot[t + 3], pot[t + 1])
-        lap_lap = lap_of(lap, lph[t + 3], lph[t + 1])
+        lap_pot = lap_of(here, pot[t + 2], pot[t])
+        lap_lap = lap_of(lap, lph[t + 2], lph[t])
         flow = at(V0, t) * gs[0] + at(V1, t) * gs[1] + at(V2, t) * gs[2]
         c = at(PH, t) - DT * flow + (DT * mobility) * lap_pot - at(PO, t)
         adj[t] = c
         qs = [q[i, t + 1] for i in range(3)]
         qg = qs[0] * gs[0] + qs[1] * gs[1] + qs[2] * gs[2]
-        ql = qs[0] * lv[0, t + 2] + qs[1] * lv[1, t + 1] + qs[2] * lv[2, t + 1]
+        ql = qs[0] * lv[0, t + 1] + qs[1] * lv[1, t] + qs[2] * lv[2, t]
         terms = (own(c * lap_pot), own(here * qg), own(ql), own(lap * qg), own(c * lap_lap))
         sums = [s + rows_of(a) for s, a in zip(sums, terms)]
     for k in range(5):
@@ -265,18 +262,28 @@
     return (6.0 + SHIFT) * c - ((zu + zd) + (x_up(c) + x_dn(c)) + (y_up(c) + y_dn(c)))
 
 
-def moment_kernel(core, b6, u4, r, s, w, part, edge, out, bb, uu, f, af, a2f, ab, au, send, a3f, a2b, a2u):
+def moment_kernel(core, b4, u4, r, s, far, w, part, edge, out, bb, uu, f, af, a2f, ab, au, send, a2b, a2u):
     c = core[0]
-    near = pl.ds(NEAR, ROWS - 2 * NEAR)
+    near = pl.ds(NEAR, NARROW)
+
+    def got(first, count):
+        mine, theirs = r[first : first + count], other_first(s[first : first + count])
+        return jnp.where(c == 0, mine, theirs), jnp.where(c == 0, theirs, mine)
+
     for j in range(4):
-        lo, hi = low_high(c, r, s, j)
+        lo, hi = got(NARROW * j, NARROW)
         bb[j, near] = lo
-        bb[10 + j, near] = hi
+        bb[8 + j, near] = hi
     for j in range(2):
-        lo, hi = low_high(c, r, s, 4 + j)
+        lo, hi = got(NARROW * (4 + j), NARROW)
         uu[j, near] = lo
         uu[6 + j, near] = hi
-    bb[4:10] = b6[...]
+    lo, hi = got(NARROW * 6, 8)
+    for z, rim in ((3, lo), (8, hi)):
+        bb[z, NEAR - 1 : NEAR] = rim[0:1]
+        bb[z, ROWS - NEAR : ROWS - NEAR + 1] = rim[1:2]
+    bb[12, HX : HX + CX, :CY] = far[...]
+    bb[4:8] = b4[...]
     uu[2:6] = u4[...]
 
     def wide(t):
@@ -286,7 +293,7 @@
         )
         f[t] = 0.25 * ((bb[t + 4] + bb[t]) + across) - 1.5 * a
 
-    loop(10, wide)
+    loop(9, wide)
 
     def apply(src, dst, count):
         def body(t):
@@ -294,10 +301,9 @@
 
         loop(count, body)
 
-    apply(f, af, 8)
-    apply(af, a2f, 6)
-    apply(a2f, a3f, 4)
-    apply(bb.at[pl.ds(2, 10)], ab, 8)
+    apply(f, af, 7)
+    apply(af, a2f, 5)
+    apply(bb.at[pl.ds(1, 10)], ab, 8)
     apply(ab.at[pl.ds(1, 6)], a2b, 4)
     apply(uu, au, 6)
     apply(au, a2u, 4)
@@ -306,11 +312,12 @@
     lanes = pl.ds(0, CY)
     acc = [jnp.zeros((8, CY), jnp.float32)] * 40
     for t in range(CZ):
-        vb, vab, va2b = bb[t + 5, rows, lanes], ab[t + 2, rows, lanes], a2b[t, rows, lanes]
+        vb, vab, va2b = bb[t + 4, rows, lanes], ab[t + 2, rows, lanes], a2b[t, rows, lanes]
         vu, vau, va2u = uu[t + 2, rows, lanes], au[t + 1, rows, lanes], a2u[t, rows, lanes]
-        vf, vaf, va2f, va3f = (
-            f[t + 3, rows, lanes], af[t + 2, rows, lanes], a2f[t + 1, rows, lanes], a3f[t, rows, lanes],
-        )
+        vf, vaf, va2f = f[t + 2, rows, lanes], af[t + 1, rows, lanes], a2f[t, rows, lanes]
+        a = a2f[t]
+        across = (x_up(a) + x_dn(a)) + (y_up(a) + y_dn(a))
+        va3f = (6.0 + SHIFT) * va2f - (2.0 * a2f[t + 1, rows, lanes] + own(across))
         terms = [
             vb * vb, vb * vab, vab * vab, vab * va2b,
             vu * vu, vu * vau, vau * vau, vau * va2u,
@@ -331,8 +338,11 @@
     row = jnp.sum(jnp.where(line == which, totals, 0.0), axis=0, keepdims=True)
     out[...] = jnp.broadcast_to(row, (DEVICES, SLOTS))
     send[0:4] = edge[c]
-    send[4] = a2f[3 - c, near]
-    send[5] = au[3 - c, near]
+    first = 2 * (1 - c)
+    send[4] = a2f[first, near]
+    send[5] = a2f[first + 1, near]
+    send[6] = af[3 - c, near]
+    send[7] = au[3 - c, near]
 
 
 def steps(m0, m1, m2, m3):
@@ -347,7 +357,7 @@
 
 def last_kernel(
     coefs, core, gathered, bb, uu, f, af, a2f, ab, au, ri, si, e, q, adj4, pot, g,
-    phase_back, velocity_back, params, phi, pr, pa, adj, qe,
+    phase_back, velocity_back, params, phi, pr, pa, adj, qe, a2e, afe, aue,
 ):
     c = core[0]
     near = pl.ds(NEAR, ROWS - 2 * NEAR)
@@ -396,19 +406,24 @@
     g3 = -((DT * mobility) * s(44) + (DT * tension) * (s(43) - meet(2)))
     place = lax.broadcasted_iota(jnp.int32, (1, CY), 1)
     packed = jnp.where(place == 0, g0, jnp.where(place == 1, g1, jnp.where(place == 2, g2, g3)))
-    params[...] = packed * scale
+    params[...] = (packed * scale)[0, 0:4]
+
+    for j in range(2):
+        lo, hi = low_high(c, ri, si, 4 + j)
+        a2e[j, near] = lo
+        a2e[6 + j, near] = hi
+    a2e[2:6] = a2f[0:4]
+    for j, (src, dst) in enumerate(((af, afe), (au, aue))):
+        lo, hi = low_high(c, ri, si, 6 + j)
+        dst[0, near] = lo
+        dst[7, near] = hi
+        dst[1:7] = src[0:6]
 
     def combine(t):
-        value = coef[0] * uu[t + 1] + coef[1] * au[t] + coef[2] * f[t + 2] + coef[3] * af[t + 1]
-        phi[t + 1] = value + coef[4] * a2f[t] + coef[5] * bb[t + 4] + coef[6] * ab[t + 1]
-
-    loop(6, combine)
-    rows = near
-    a_lo, a_hi = low_high(c, ri, si, 4)
-    u_lo, u_hi = low_high(c, ri, si, 5)
-    for t, a2, a1 in ((0, a_lo, u_lo), (7, a_hi, u_hi)):
-        value = coef[0] * uu[t, rows] + coef[1] * a1 + coef[2] * f[t + 1, rows] + coef[3] * af[t, rows]
-        phi[t, rows] = value + coef[4] * a2 + coef[5] * bb[t + 3, rows] + coef[6] * ab[t, rows]
+        value = coef[0] * uu[t] + coef[1] * aue[t] + coef[2] * f[t] + coef[3] * afe[t]
+        phi[t] = value + coef[4] * a2e[t] + coef[5] * bb[t + 2] + coef[6] * ab[t]
+
+    loop(8, combine)
 
     def at(field, z):
         return e[BASE[field] + HALO[field] + z]
@@ -431,12 +446,12 @@
         v0, v1, v2 = at(V0, t), at(V1, t), at(V2, t)
         v0u, v0d = at(V0, t + 1), at(V0, t - 1)
         c = adj[t + 2]
-        here = pot[t + 2]
+        here = pot[t + 1]
         ph = at(PH, t)
         lam = pa[t + 1]
         lap = pa[t + 2] + pa[t] + (x_up(lam) + x_dn(lam)) + (y_up(lam) + y_dn(lam)) - 6.0 * lam
-        up = v0u * adj[t + 3] - tension * (pot[t + 3] * pr[0, t + 2])
-        dn = v0d * adj[t + 1] - tension * (pot[t + 1] * pr[0, t])
+        up = v0u * adj[t + 3] - tension * (pot[t + 2] * pr[0, t + 2])
+        dn = v0d * adj[t + 1] - tension * (pot[t] * pr[0, t])
         div = 0.5 * (up - dn)
         div = div + dx(v1 * c - tension * (here * pr[1, t + 1]))
         div = div + dy(v2 * c - tension * (here * pr[2, t + 1]))
@@ -500,13 +515,14 @@
     return lax.ppermute(value, "gy", SWAP)
 
 
-def call(kernel, outs, ins, scratches, name, smem):
+def call(kernel, outs, ins, scratches, name, smem, aliases={}):
     return pl.pallas_call(
         kernel,
         out_shape=outs,
         in_specs=[SM] * smem + [VM] * (len(ins) - smem),
         out_specs=jax.tree.map(lambda _: VM, outs),
         scratch_shapes=scratches,
+        input_output_aliases=aliases,
         compiler_params=PARAMS,
         name=name,
     )(*ins)
@@ -515,7 +531,6 @@
 def local(phase, velocity, phase_obs, velocity_obs, coefs):
     core = lax.axis_index("gy").astype(jnp.int32).reshape(1)
     mine = (velocity, phase, phase_obs, velocity_obs)
-    theirs = lax.optimization_barrier(tuple(swap(a) for a in mine))
     stack, edges, coefs = pl.pallas_call(
         load_kernel,
         out_shape=(f32(8 * CZ, CX, CY), f32(6 * CZ, 2 * HX, CY), f32(4)),
@@ -524,12 +539,13 @@
         scratch_shapes=[pltpu.SemaphoreType.DMA((9,))],
         compiler_params=PARAMS,
         name="load",
-    )(*mine, coefs)
+    )(*(pltpu.with_memory_space_constraint(a, pltpu.HBM) for a in (*mine, coefs)))
+    peer = swap(stack)
     gxr = lax.ppermute(edges, "gx", SWAP)
     main, diag = call(
         pack_kernel,
         (f32(SENT, CX, LANES), f32(SENT, 2 * HX, LANES)),
-        (core, stack, theirs[0], theirs[1], theirs[3]),
+        (core, stack, peer),
         [],
         "pack",
         1,
@@ -537,34 +553,38 @@
     mr = role_shift(main, False)
     dr = role_shift(diag, True)
     gxs = swap(gxr)
-    ms, ds = swap(mr), swap(dr)
-    narrow = ROWS - 2 * NEAR
-    e, b, u, q, pot, lph, g, lv, send = call(
+    inner = call(inner_kernel, layers(TOTAL), (stack, peer, gxr, gxs), [], "inner", 0)
+    mr, inner = lax.optimization_barrier((mr, inner))
+    ms = swap(mr)
+    ds = swap(dr)
+    e, b, u, q, pot, lph, g, lv, send, far = call(
         first_kernel,
-        (layers(TOTAL), layers(6), layers(4), layers(3, 6), layers(8), layers(8), layers(3, 6), layers(3, 8),
-         f32(6, narrow, LANES)),
-        (coefs, core, stack, *theirs, gxr, gxs, mr, ms, dr, ds),
-        [scratch(8), scratch(6), scratch(6)],
+        (layers(TOTAL), layers(4), layers(4), layers(3, 6), layers(6), layers(6), layers(3, 6), layers(3, 6),
+         f32(6 * NARROW + 8, LANES), f32(CX, CY)),
+        (coefs, core, inner, mr, ms, dr, ds),
+        [scratch(6)],
         "first",
         2,
+        {2: 0},
     )
     r2 = role_shift(send, False)
+    far = ring(far, -2)
     adj, w, part, edge = call(
         weight_kernel,
-        (layers(4), f32(3, CZ, CX, CY), f32(5, 8, CY), f32(2, 4, narrow, LANES)),
+        (layers(4), f32(3, CZ, CX, CY), f32(5, 8, CY), f32(2, 4, NARROW, LANES)),
         (coefs, e, q, pot, lph, g, lv),
         [],
         "weights",
         1,
     )
-    r2, w, part, edge = lax.optimization_barrier((r2, w, part, edge))
+    r2, far, w, part, edge = lax.optimization_barrier((r2, far, w, part, edge))
     s2 = swap(r2)
     sums, bb, uu, f, af, a2f, ab, au, send = call(
         moment_kernel,
-        (f32(DEVICES, SLOTS), layers(14), layers(8), layers(10), layers(8), layers(6), layers(8), layers(6),
-         f32(6, narrow, LANES)),
-        (core, b, u, r2, s2, w, part, edge),
-        [scratch(4), scratch(4), scratch(4)],
+        (f32(DEVICES, SLOTS), layers(13), layers(8), layers(9), layers(7), layers(5), layers(8), layers(6),
+         f32(8, NARROW, LANES)),
+        (core, b, u, r2, s2, far, w, part, edge),
+        [scratch(4), scratch(4)],
         "moments",
         1,
     )
@@ -574,13 +594,13 @@
     si = swap(ri)
     phase_back, velocity_back, params = call(
         last_kernel,
-        (f32(CZ, CX, CY), f32(3, CZ, CX, CY), f32(1, CY)),
+        (f32(CZ, CX, CY), f32(3, CZ, CX, CY), f32(4)),
         (coefs, core, gathered, bb, uu, f, af, a2f, ab, au, ri, si, e, q, adj, pot, g),
-        [scratch(8), scratch(3, 6), scratch(6), scratch(8), scratch(2, 6)],
+        [scratch(8), scratch(3, 6), scratch(6), scratch(8), scratch(2, 6), scratch(8), scratch(8), scratch(8)],
         "last",
         2,
     )
-    return phase_back, velocity_back, params[0, :4]
+    return phase_back, velocity_back, params
 
 
 def solution(mesh):

time: 93.1 us -> 81.9 us (0.88)
  waiting for transfers between devices: 17.5 us -> 10.5 us
  starting transfers between devices: 33.7 us -> 39.9 us
  local copies, waits for them, and re-layouts: 4.7 us -> 0 us
  Pallas kernels: 15.1 us -> 11.5 us
  blocking collectives: 21.3 us -> 19.2 us
    ppermute x4, waiting for transfers between devices: 13.9 us -> 0.01 us  [role_shift(): return lax.ppermute(value, ('gx', 'gy', 'gz'), pairs)]
    ppermute x0 -> x1, waiting for transfers between devices: none -> 5.57 us  [ring(): lax.ppermute(value, 'gz', [(i, (i + step) % count) for i in range(count)])]
    ppermute x4, starting transfers between devices: 23.4 us -> 27.9 us  [role_shift(): return lax.ppermute(value, ('gx', 'gy', 'gz'), pairs)]
    unnamed x10 -> x0, local copies, waits for them, and re-layouts: 4.19 us -> none
    pallas_call x5 -> x6, Pallas kernels: 14.3 us -> 10.3 us  [call(): pl.pallas_call(kernel, out_shape=outs, in_specs=[SM] * smem + [VM] * (len...]
    ppermute x9 -> x6, starting transfers between devices: 9.49 us -> 12 us  [swap(): return lax.ppermute(value, 'gy', SWAP)]
    all_to_all x1, blocking collectives: 21.3 us -> 19.2 us  [local(): lax.all_to_all(sums.reshape(DEVICES, 1, SLOTS), ('gx', 'gy', 'gz'), 0, 0)]
    ppermute x9 -> x6, waiting for transfers between devices: 3.61 us -> 4.91 us  [swap(): return lax.ppermute(value, 'gy', SWAP)]
  transfers between devices with their start and end apart: 14 -> 12, of which waited for: 6 -> 5; matrix products, arithmetic and copies ran while one was open for 0% -> 0% of each run, Pallas kernels for 2% -> 1%
where the time goes in v3:
time: 81.9 us; the launch traced here: 81.8 us
  starting transfers between devices  39.9 us (49%)
  blocking collectives  19.2 us (23%)
  Pallas kernels  11.5 us (14%)
  waiting for transfers between devices  10.5 us (13%)
    ppermute x4, starting transfers between devices, role_shift(): return lax.ppermute(value, ('gx', 'gy', 'gz'), pairs)  27.9 us
    all_to_all x1, blocking collectives, local(): lax.all_to_all(sums.reshape(DEVICES, 1, SLOTS), ('gx', 'gy', 'gz'), 0, 0)  19.2 us
    ppermute x6, starting transfers between devices, swap(): return lax.ppermute(value, 'gy', SWAP)  12 us
    pallas_call x6, Pallas kernels, call(): pl.pallas_call(kernel, out_shape=outs, in_specs=[SM] * smem + [VM] * (len...  10.3 us
    ppermute x1, waiting for transfers between devices, ring(): lax.ppermute(value, 'gz', [(i, (i + step) % count) for i in range(count)])  5.57 us
    ppermute x6, waiting for transfers between devices, swap(): return lax.ppermute(value, 'gy', SWAP)  4.91 us
  transfers between devices with their start and end apart: 12, of which 5 were waited for; matrix products, arithmetic and copies ran while one was open for 0% of the time, Pallas kernels for 1%

profile of v3, /device:TPU:1, one launch (start us, length us, event | category | flops | bytes accessed | tf_op | source)
XLA Modules:
  0.0 81.8 jit_solution(317964392632932899)
XLA Ops:
  0.6 1.2 %load.1 = (f32[32,32,128]{2,1,0:T(8,128)S(1)}, f32[24,16,128]{2,1,0:T(8,128)S(1)}, f32[4]{0:T(128)S(1)}) custom-call(f32[3,4,32,128]{3,2,1,0:T(8,128)} %vel.1, f32[4,32,128]{2,1,0:T(8,128)} %ph.1, f32[4,32,128]{2,1,0:T(8,128)} %po.1, f32[3,4,32,128]{3,2,1,0:T(8,128)} %vo.1, f32[4]{0:T(128)} %coefs.1), custom_call_target="tpu_custom_call" | custom-call | tf_op jit(solution)/shard_map/load/pallas_call | solution.py:534
  1.8 3.3 %collective-permute-start = (f32[32,32,128]{2,1,0:T(8,128)S(1)}, f32[32,32,128]{2,1,0:T(8,128)S(1)}, u32[]{:S(2)}, u32[]{:S(2)}) collective-permute-start(f32[32,32,128]{2,1,0:T(8,128)S(1)} %get-tuple-element.41.stack), channel_id=1, source_target_pairs={{0,64},{64,0},{1,65},{65,1},{2,66},{66,2},{3,67},{67,3},{4,68},{68... | collective-permute-start | bytes 1572872 | tf_op jit(solution)/shard_map/ppermute | solution.py:515
  5.1 0.0 collective-permute-start.2
  5.1 1.5 %collective-permute-done.peer = f32[32,32,128]{2,1,0:T(8,128)S(1)} collective-permute-done((f32[32,32,128]{2,1,0:T(8,128)S(1)}, f32[32,32,128]{2,1,0:T(8,128)S(1)}, u32[]{:S(2)}, u32[]{:S(2)}) %collective-permute-start) | collective-permute-done | bytes 524320 | tf_op jit(solution)/shard_map/ppermute | solution.py:515
  6.7 9.0 %collective-permute-start.1 = (f32[7,32,256]{2,1,0:T(8,128)S(1)}, f32[7,32,256]{2,1,0:T(8,128)S(1)}, u32[]{:S(2)}, u32[]{:S(2)}) collective-permute-start(f32[7,32,256]{2,1,0:T(8,128)S(1)} %get-tuple-element.42), channel_id=1, source_target_pairs={{0,1},{1,2},{2,3},{3,4},{4,5},{5,6},{6,7},{7,8},{8,9},{9,10},{10,1... | collective-permute-start | bytes 688136 | tf_op jit(solution)/shard_map/ppermute | solution.py:506
  15.7 0.0 collective-permute-start.3
  15.7 7.7 %collective-permute-start.5 = (f32[7,16,256]{2,1,0:T(8,128)S(1)}, f32[7,16,256]{2,1,0:T(8,128)S(1)}, u32[]{:S(2)}, u32[]{:S(2)}) collective-permute-start(f32[7,16,256]{2,1,0:T(8,128)S(1)} %get-tuple-element.46), channel_id=1, source_target_pairs={{0,129},{1,130},{2,131},{3,132},{4,133},{5,134},{6,135},{7,136},{8... | collective-permute-start | bytes 344072 | tf_op jit(solution)/shard_map/ppermute | solution.py:506
  23.4 0.1 inner.1
  23.5 0.0 collective-permute-done.1.mr
  23.5 3.4 %collective-permute-start.4 = (f32[7,32,256]{2,1,0:T(8,128)S(1)}, f32[7,32,256]{2,1,0:T(8,128)S(1)}, u32[]{:S(2)}, u32[]{:S(2)}) collective-permute-start(f32[7,32,256]{2,1,0:T(8,128)S(1)} %collective-permute-done.1.mr), channel_id=1, source_target_pairs={{0,64},{64,0},{1,65},{65,1},{2,66},{66,2},{3,67},{67,3},{4,68},{68... | collective-permute-start | bytes 688136 | tf_op jit(solution)/shard_map/ppermute | solution.py:515
  26.9 1.4 %collective-permute-start.6 = (f32[7,16,256]{2,1,0:T(8,128)S(1)}, f32[7,16,256]{2,1,0:T(8,128)S(1)}, u32[]{:S(2)}, u32[]{:S(2)}) collective-permute-start(f32[7,16,256]{2,1,0:T(8,128)S(1)} %collective-permute-done.5.dr), channel_id=1, source_target_pairs={{0,64},{64,0},{1,65},{65,1},{2,66},{66,2},{3,67},{67,3},{4,68},{68... | collective-permute-start | bytes 344072 | tf_op jit(solution)/shard_map/ppermute | solution.py:515
  28.3 1.0 %collective-permute-done.6.ds = f32[7,16,256]{2,1,0:T(8,128)S(1)} collective-permute-done((f32[7,16,256]{2,1,0:T(8,128)S(1)}, f32[7,16,256]{2,1,0:T(8,128)S(1)}, u32[]{:S(2)}, u32[]{:S(2)}) %collective-permute-start.6) | collective-permute-done | bytes 114720 | tf_op jit(solution)/shard_map/ppermute | solution.py:515
  29.3 2.8 %first.1 = (f32[46,48,256]{2,1,0:T(8,128)S(1)}, f32[4,48,256]{2,1,0:T(8,128)S(1)}, f32[4,48,256]{2,1,0:T(8,128)S(1)}, f32[3,6,48,256]{3,2,1,0:T(8,128)S(1)}, f32...) custom-call(f32[4]{0:T(128)S(1)} %get-tuple-element.40.coefs, ...), custom_call_target="tpu_custom_call", output_to_operand_aliasing={{0}: (2, {})} | custom-call | tf_op jit(solution)/shard_map/first/pallas_call | solution.py:519
  32.1 5.5 %collective-permute-start.7 = (f32[248,256]{1,0:T(8,128)S(1)}, f32[248,256]{1,0:T(8,128)S(1)}, u32[]{:S(2)}, u32[]{:S(2)}) collective-permute-start(f32[248,256]{1,0:T(8,128)S(1)} %get-tuple-element.49), channel_id=1, source_target_pairs={{0,1},{1,2},{2,3},{3,4},{4,5},{5,6},{6,7},{7,8},{8,9},{9,10},{10,1... | collective-permute-start | bytes 761864 | tf_op jit(solution)/shard_map/ppermute | solution.py:506
  37.6 1.1 %weights.1 = (f32[4,48,256]{2,1,0:T(8,128)S(1)}, f32[3,4,32,128]{3,2,1,0:T(8,128)S(1)}, f32[5,8,128]{2,1,0:T(8,128)S(1)}, f32[2,4,40,256]{3,2,1,0:T(8,128)S(1)}) custom-call(f32[4]{0:T(128)S(1)} %get-tuple-element.40.coefs, f32[46,48,256]{2,1,0:T(8,128)S(1)} %get-tuple-element.51.e, f32[3,6,48,256]{3,2,1,0:T(8,128)S(1)} %get-tuple-element.52.q, ...), custom_call_target="tpu_custom_call" | custom-call | tf_op jit(solution)/shard_map/weights/pallas_call | solution.py:519
  38.7 5.6 %collective-permute-done.8.far = f32[32,128]{1,0:T(8,128)S(1)} collective-permute-done((f32[32,128]{1,0:T(8,128)S(1)}, f32[32,128]{1,0:T(8,128)S(1)}, u32[]{:S(2)}, u32[]{:S(2)}) %collective-permute-start.8) | collective-permute-done | bytes 16416 | tf_op jit(solution)/shard_map/ppermute | solution.py:511
  44.3 2.8 %collective-permute-start.9 = (f32[248,256]{1,0:T(8,128)S(1)}, f32[248,256]{1,0:T(8,128)S(1)}, u32[]{:S(2)}, u32[]{:S(2)}) collective-permute-start(f32[248,256]{1,0:T(8,128)S(1)} %collective-permute-done.7.r), channel_id=1, source_target_pairs={{0,64},{64,0},{1,65},{65,1},{2,66},{66,2},{3,67},{67,3},{4,68},{68... | collective-permute-start | bytes 761864 | tf_op jit(solution)/shard_map/ppermute | solution.py:515
  47.1 1.2 %collective-permute-done.9.s = f32[248,256]{1,0:T(8,128)S(1)} collective-permute-done((f32[248,256]{1,0:T(8,128)S(1)}, f32[248,256]{1,0:T(8,128)S(1)}, u32[]{:S(2)}, u32[]{:S(2)}) %collective-permute-start.9) | collective-permute-done | bytes 253984 | tf_op jit(solution)/shard_map/ppermute | solution.py:515
  48.2 3.3 %moments.1 = (f32[256,64]{1,0:T(8,128)S(1)}, f32[13,48,256]{2,1,0:T(8,128)S(1)}, f32[8,48,256]{2,1,0:T(8,128)S(1)}, f32[9,48,256]{2,1,0:T(8,128)S(1)}, f32[7,48,...) custom-call(s32[1]{0:T(128)} %bitcast.core, ...), custom_call_target="tpu_custom_call" | custom-call | tf_op jit(solution)/shard_map/moments/pallas_call | solution.py:519
  51.5 5.7 %collective-permute-start.10 = (f32[8,40,256]{2,1,0:T(8,128)S(1)}, f32[8,40,256]{2,1,0:T(8,128)S(1)}, u32[]{:S(2)}, u32[]{:S(2)}) collective-permute-start(f32[8,40,256]{2,1,0:T(8,128)S(1)} %get-tuple-element.65), channel_id=1, source_target_pairs={{0,1},{1,2},{2,3},{3,4},{4,5},{5,6},{6,7},{7,8},{8,9},{9,10},{10,1... | collective-permute-start | bytes 983048 | tf_op jit(solution)/shard_map/ppermute | solution.py:506
  57.2 19.2 %all_to_all.5 = f32[256,1,64]{2,1,0:T(1,128)S(1)} all-to-all(f32[256,1,64]{2,1,0:T(1,128)S(1)} %bitcast.6), channel_id=1, replica_groups=mesh['gx'=2,'gy'=2,'gz'=64] {'gx','gy','gz'}, dimensions={0} | all-to-all | bytes 131072 | tf_op jit(solution)/shard_map/all_to_all | solution.py:592
  76.4 1.1 %collective-permute-start.11 = (f32[8,40,256]{2,1,0:T(8,128)S(1)}, f32[8,40,256]{2,1,0:T(8,128)S(1)}, u32[]{:S(2)}, u32[]{:S(2)}) collective-permute-start(f32[8,40,256]{2,1,0:T(8,128)S(1)} %collective-permute-done.10.ri), channel_id=1, source_target_pairs={{0,64},{64,0},{1,65},{65,1},{2,66},{66,2},{3,67},{67,3},{4,68},{68... | collective-permute-start | bytes 983048 | tf_op jit(solution)/shard_map/ppermute | solution.py:515
  77.5 1.3 %collective-permute-done.11.si = f32[8,40,256]{2,1,0:T(8,128)S(1)} collective-permute-done((f32[8,40,256]{2,1,0:T(8,128)S(1)}, f32[8,40,256]{2,1,0:T(8,128)S(1)}, u32[]{:S(2)}, u32[]{:S(2)}) %collective-permute-start.11) | collective-permute-done | bytes 327712 | tf_op jit(solution)/shard_map/ppermute | solution.py:515
  78.7 3.1 %last.1 = (f32[4,32,128]{2,1,0:T(8,128)}, f32[3,4,32,128]{3,2,1,0:T(8,128)}, f32[4]{0:T(128)}) custom-call(f32[4]{0:T(128)S(1)} %get-tuple-element.40.coefs, s32[1]{0:T(128)} %bitcast.core, f32[256,64]{1,0:T(8,128)S(1)} %bitcast.5, f32[13,48,256]{2,1,0:T(8,128)S(1)} %get-tuple-element.68.bb, f32[8,48,256]{2,1,0:T(8,128)S(1)} %get-tuple-element.69.uu, ...), custom_call_target="tpu_custom_call" | custom-call | tf_op jit(solution)/shard_map/last/pallas_call | solution.py:519
  (8 shorter events, 0.0 us)
Async XLA Ops:
  1.8 4.9 %collective-permute-start = (f32[32,32,128]{2,1,0:T(8,128)S(1)}, f32[32,32,128]{2,1,0:T(8,128)S(1)}, u32[]{:S(2)}, u32[]{:S(2)}) collective-permute-start(f32[32,32,128]{2,1,0:T(8,128)S(1)} %get-tuple-element.41.stack), channel_id=1, source_target_pairs={{0,64},{64,0},{1,65},{65,1},{2,66},{66,2},{3,67},{67,3},{4,68},{68... | collective-permute-start | bytes 1572872 | tf_op jit(solution)/shard_map/ppermute | solution.py:515
  5.1 10.6 %collective-permute-start.2 = (f32[24,16,128]{2,1,0:T(8,128)S(1)}, f32[24,16,128]{2,1,0:T(8,128)S(1)}, u32[]{:S(2)}, u32[]{:S(2)}) collective-permute-start(f32[24,16,128]{2,1,0:T(8,128)S(1)} %get-tuple-element.43), channel_id=1, source_target_pairs={{0,128},{128,0},{1,129},{129,1},{2,130},{130,2},{3,131},{131,3},{4... | collective-permute-start | bytes 589832 | tf_op jit(solution)/shard_map/ppermute | solution.py:544
  6.7 16.8 %collective-permute-start.1 = (f32[7,32,256]{2,1,0:T(8,128)S(1)}, f32[7,32,256]{2,1,0:T(8,128)S(1)}, u32[]{:S(2)}, u32[]{:S(2)}) collective-permute-start(f32[7,32,256]{2,1,0:T(8,128)S(1)} %get-tuple-element.42), channel_id=1, source_target_pairs={{0,1},{1,2},{2,3},{3,4},{4,5},{5,6},{6,7},{7,8},{8,9},{9,10},{10,1... | collective-permute-start | bytes 688136 | tf_op jit(solution)/shard_map/ppermute | solution.py:506
  15.7 7.7 %collective-permute-start.3 = (f32[24,16,128]{2,1,0:T(8,128)S(1)}, f32[24,16,128]{2,1,0:T(8,128)S(1)}, u32[]{:S(2)}, u32[]{:S(2)}) collective-permute-start(f32[24,16,128]{2,1,0:T(8,128)S(1)} %collective-permute-done.2.gxr), channel_id=1, source_target_pairs={{0,64},{64,0},{1,65},{65,1},{2,66},{66,2},{3,67},{67,3},{4,68},{68... | collective-permute-start | bytes 589832 | tf_op jit(solution)/shard_map/ppermute | solution.py:515
  15.7 11.2 %collective-permute-start.5 = (f32[7,16,256]{2,1,0:T(8,128)S(1)}, f32[7,16,256]{2,1,0:T(8,128)S(1)}, u32[]{:S(2)}, u32[]{:S(2)}) collective-permute-start(f32[7,16,256]{2,1,0:T(8,128)S(1)} %get-tuple-element.46), channel_id=1, source_target_pairs={{0,129},{1,130},{2,131},{3,132},{4,133},{5,134},{6,135},{7,136},{8... | collective-permute-start | bytes 344072 | tf_op jit(solution)/shard_map/ppermute | solution.py:506
  23.5 5.7 %collective-permute-start.4 = (f32[7,32,256]{2,1,0:T(8,128)S(1)}, f32[7,32,256]{2,1,0:T(8,128)S(1)}, u32[]{:S(2)}, u32[]{:S(2)}) collective-permute-start(f32[7,32,256]{2,1,0:T(8,128)S(1)} %collective-permute-done.1.mr), channel_id=1, source_target_pairs={{0,64},{64,0},{1,65},{65,1},{2,66},{66,2},{3,67},{67,3},{4,68},{68... | collective-permute-start | bytes 688136 | tf_op jit(solution)/shard_map/ppermute | solution.py:515
  26.9 2.4 %collective-permute-start.6 = (f32[7,16,256]{2,1,0:T(8,128)S(1)}, f32[7,16,256]{2,1,0:T(8,128)S(1)}, u32[]{:S(2)}, u32[]{:S(2)}) collective-permute-start(f32[7,16,256]{2,1,0:T(8,128)S(1)} %collective-permute-done.5.dr), channel_id=1, source_target_pairs={{0,64},{64,0},{1,65},{65,1},{2,66},{66,2},{3,67},{67,3},{4,68},{68... | collective-permute-start | bytes 344072 | tf_op jit(solution)/shard_map/ppermute | solution.py:515
  32.1 12.2 %collective-permute-start.7 = (f32[248,256]{1,0:T(8,128)S(1)}, f32[248,256]{1,0:T(8,128)S(1)}, u32[]{:S(2)}, u32[]{:S(2)}) collective-permute-start(f32[248,256]{1,0:T(8,128)S(1)} %get-tuple-element.49), channel_id=1, source_target_pairs={{0,1},{1,2},{2,3},{3,4},{4,5},{5,6},{6,7},{7,8},{8,9},{9,10},{10,1... | collective-permute-start | bytes 761864 | tf_op jit(solution)/shard_map/ppermute | solution.py:506
  37.6 6.7 %collective-permute-start.8 = (f32[32,128]{1,0:T(8,128)S(1)}, f32[32,128]{1,0:T(8,128)S(1)}, u32[]{:S(2)}, u32[]{:S(2)}) collective-permute-start(f32[32,128]{1,0:T(8,128)S(1)} %get-tuple-element.50), channel_id=1, source_target_pairs={{0,62},{1,63},{2,0},{3,1},{4,2},{5,3},{6,4},{7,5},{8,6},{9,7},{10,... | collective-permute-start | bytes 49160 | tf_op jit(solution)/shard_map/ppermute | solution.py:511
  44.3 4.0 %collective-permute-start.9 = (f32[248,256]{1,0:T(8,128)S(1)}, f32[248,256]{1,0:T(8,128)S(1)}, u32[]{:S(2)}, u32[]{:S(2)}) collective-permute-start(f32[248,256]{1,0:T(8,128)S(1)} %collective-permute-done.7.r), channel_id=1, source_target_pairs={{0,64},{64,0},{1,65},{65,1},{2,66},{66,2},{3,67},{67,3},{4,68},{68... | collective-permute-start | bytes 761864 | tf_op jit(solution)/shard_map/ppermute | solution.py:515
  51.5 24.9 %collective-permute-start.10 = (f32[8,40,256]{2,1,0:T(8,128)S(1)}, f32[8,40,256]{2,1,0:T(8,128)S(1)}, u32[]{:S(2)}, u32[]{:S(2)}) collective-permute-start(f32[8,40,256]{2,1,0:T(8,128)S(1)} %get-tuple-element.65), channel_id=1, source_target_pairs={{0,1},{1,2},{2,3},{3,4},{4,5},{5,6},{6,7},{7,8},{8,9},{9,10},{10,1... | collective-permute-start | bytes 983048 | tf_op jit(solution)/shard_map/ppermute | solution.py:506
  76.4 2.3 %collective-permute-start.11 = (f32[8,40,256]{2,1,0:T(8,128)S(1)}, f32[8,40,256]{2,1,0:T(8,128)S(1)}, u32[]{:S(2)}, u32[]{:S(2)}) collective-permute-start(f32[8,40,256]{2,1,0:T(8,128)S(1)} %collective-permute-done.10.ri), channel_id=1, source_target_pairs={{0,64},{64,0},{1,65},{65,1},{2,66},{66,2},{3,67},{67,3},{4,68},{68... | collective-permute-start | bytes 983048 | tf_op jit(solution)/shard_map/ppermute | solution.py:515

commit v4 on v3

--- a/solution.py
+++ b/solution.py
@@ -10,10 +10,11 @@
 CZ, CX, CY = 4, 32, 128
 HX = 8
 NEAR = 4
+UNROLL = 4
 NARROW = (CX + 2 * HX) - 2 * NEAR
 ROWS = CX + 2 * HX
 LANES = 2 * CY
-DEVICES = 256
+PARTNERS = 128
 
 V0, V1, V2, PH, PO, O0, O1, O2 = range(8)
 HALO = (2, 1, 1, 2, 0, 1, 0, 0)
@@ -23,7 +24,11 @@
     BASE.append(_at)
     _at += CZ + 2 * _h
 TOTAL = _at
-SENT = sum(HALO)
+SENT = [(f, k) for f, h in enumerate(HALO) for k in range(1, h + 1)]
+CORNER = [3 if f == O0 else 8 - k for f, k in SENT]
+CORNER_ROWS = -(-2 * sum(CORNER) // 8) * 8
+AGAIN = [("b", k, 6 - k) for k in (1, 2, 3, 4)] + [("u", k, 3 - k) for k in (1, 2)]
+AGAIN_ROWS = -(-sum(CX + 2 * w for _, _, w in AGAIN) // 8) * 8
 NUM_SUMS = 45
 SLOTS = 64
 
@@ -62,6 +67,10 @@
 
 def other_first(a):
     return jnp.concatenate([a[:, CY:], a[:, :CY]], 1)
+
+
+def outgoing(core, k):
+    return (CZ - k) * (1 - core) + (k - 1) * core
 
 
 def loop(count, body):
@@ -69,15 +78,15 @@
         body(t)
         return carry
 
-    lax.fori_loop(0, count, step, 0, unroll=2)
-
-
-def low_high(core, mine, theirs, j):
-    a, b = mine[j], other_first(theirs[j])
-    return jnp.where(core == 0, a, b), jnp.where(core == 0, b, a)
-
-
-def load_kernel(vel, ph, po, vo, coefs, stack, out, coefs_out, sems):
+    lax.fori_loop(0, count, step, 0, unroll=UNROLL)
+
+
+def low_high(core, mine, theirs):
+    theirs = other_first(theirs)
+    return jnp.where(core == 0, mine, theirs), jnp.where(core == 0, theirs, mine)
+
+
+def load_kernel(vel, ph, po, vo, coefs, stack, out, coefs_out, give, sems):
     copies = [
         pltpu.make_async_copy(ph, stack.at[pl.ds(CZ * PH, CZ)], sems.at[6]),
         pltpu.make_async_copy(po, stack.at[pl.ds(CZ * PO, CZ)], sems.at[7]),
@@ -90,6 +99,9 @@
         copy.start()
     for copy in copies:
         copy.wait()
+    other = 1 - lax.axis_index("gy")
+    for n, (f, k) in enumerate(SENT):
+        give[n] = stack[CZ * f + outgoing(other, k)]
     wide = CZ * PO
     out[0:wide, 0:HX] = stack[0:wide, CX - HX :]
     out[0:wide, HX:] = stack[0:wide, :HX]
@@ -99,19 +111,16 @@
         out[at, row + NEAR : row + HX] = stack[wide + n, :NEAR]
 
 
-def pack_kernel(core, stack, peer, main, diag):
-    c = core[0]
-    n = 0
-    for f, h in enumerate(HALO):
-        for j in range(h):
-            z = j + (CZ - h) * (1 - c)
-            for half in range(2):
-                src = (stack, peer)[half][CZ * f + z]
-                lanes = pl.ds(CY * half, CY)
-                main[n, :, lanes] = src
-                diag[n, 0:HX, lanes] = src[CX - HX :]
-                diag[n, HX:, lanes] = src[:HX]
-            n += 1
+def pack_kernel(stack, got, main, diag):
+    c = lax.axis_index("gy")
+    row = 0
+    for n, (f, k) in enumerate(SENT):
+        src = jnp.concatenate([stack[CZ * f + outgoing(c, k)], got[n]], 1)
+        main[n] = src
+        w = CORNER[n]
+        diag[row : row + w] = src[CX - w :]
+        diag[row + w : row + 2 * w] = src[:w]
+        row += 2 * w
 
 
 def inner_kernel(stack, peer, gxr, gxs, e):
@@ -132,27 +141,24 @@
                     e[mid + z, HX + CX : HX + CX + NEAR, lanes] = x[pair, row + NEAR : row + HX]
 
 
-def first_kernel(
-    coefs, core, inner, mr, ms, dr, ds, e, b, u, q, pot, lph, g, lv, send, far, p0,
-):
+def first_kernel(coefs, inner, mr, ms, dr, ds, e, b, u, q, pot, lph, g, lv, send, far, p0):
     tension = 0.5 * coefs[1]
     viscosity = 0.1 * coefs[2]
     interface = 0.5 * coefs[3]
-    c = core[0]
-
-    n = 0
-    for f, h in enumerate(HALO):
-        high = BASE[f] + h + CZ
-        for j in range(h):
-            lo, hi = low_high(c, mr, ms, n)
-            e[BASE[f] + j, HX : HX + CX] = lo
-            e[high + j, HX : HX + CX] = hi
-            lo, hi = low_high(c, dr, ds, n)
-            e[BASE[f] + j, 0:HX] = lo[0:HX]
-            e[BASE[f] + j, HX + CX :] = lo[HX:]
-            e[high + j, 0:HX] = hi[0:HX]
-            e[high + j, HX + CX :] = hi[HX:]
-            n += 1
+    c = lax.axis_index("gy")
+
+    row = 0
+    for n, (f, k) in enumerate(SENT):
+        below, above = BASE[f] + HALO[f] - k, BASE[f] + HALO[f] + CZ + k - 1
+        lo, hi = low_high(c, mr[n], ms[n])
+        e[below, HX : HX + CX] = lo
+        e[above, HX : HX + CX] = hi
+        w = CORNER[n]
+        lo, hi = low_high(c, dr[row : row + 2 * w], ds[row : row + 2 * w])
+        for layer, part in ((below, lo), (above, hi)):
+            e[layer, HX - w : HX] = part[:w]
+            e[layer, HX + CX : HX + CX + w] = part[w:]
+        row += 2 * w
 
     def at(field, z):
         return e[BASE[field] + HALO[field] + z]
@@ -205,19 +211,22 @@
 
     loop(4, across)
 
-    inside = pl.ds(NEAR, NARROW)
-    for j in range(4):
-        send[NARROW * j : NARROW * (j + 1)] = b[j, inside]
-    for j in range(2):
-        send[NARROW * (4 + j) : NARROW * (5 + j)] = u[j + 2 * (1 - c), inside]
-    edge = 3 * (1 - c)
-    send[NARROW * 6 : NARROW * 6 + 1] = b[edge, NEAR - 1 : NEAR]
-    send[NARROW * 6 + 1 : NARROW * 6 + 2] = b[edge, ROWS - NEAR : ROWS - NEAR + 1]
-    far[...] = b[0, HX : HX + CX, :CY]
-
-
-def rows_of(a):
+    row = 0
+    for name, k, w in AGAIN:
+        field = b if name == "b" else u
+        rows = CX + 2 * w
+        send[row : row + rows] = field[outgoing(c, k), HX - w : HX + CX + w]
+        row += rows
+    far[...] = b[0, HX : HX + CX]
+
+
+def folded(a):
+    a = a[:, :CY] + a[:, CY:]
     return (a[0:8] + a[8:16]) + (a[16:24] + a[24:32])
+
+
+def middle(a):
+    return a[HX : HX + CX]
 
 
 def weight_kernel(coefs, e, q, pot, lph, g, lv, adj, w, part, edge):
@@ -236,9 +245,9 @@
         w2 = 0.5 * (lv[0, t + 2] - lv[0, t]) + dx(lv[1, t]) + dy(lv[2, t])
         up, dn = lph[t + 2] * g[0, t + 2], lph[t] * g[0, t]
         w3 = 0.5 * (up - dn) + dx(lap * gs[1]) + dy(lap * gs[2])
-        w[0, t] = own(w1)
-        w[1, t] = own(w2)
-        w[2, t] = own(w3)
+        w[0, t] = middle(w1)
+        w[1, t] = middle(w2)
+        w[2, t] = middle(w3)
         lap_pot = lap_of(here, pot[t + 2], pot[t])
         lap_lap = lap_of(lap, lph[t + 2], lph[t])
         flow = at(V0, t) * gs[0] + at(V1, t) * gs[1] + at(V2, t) * gs[2]
@@ -247,8 +256,8 @@
         qs = [q[i, t + 1] for i in range(3)]
         qg = qs[0] * gs[0] + qs[1] * gs[1] + qs[2] * gs[2]
         ql = qs[0] * lv[0, t + 1] + qs[1] * lv[1, t] + qs[2] * lv[2, t]
-        terms = (own(c * lap_pot), own(here * qg), own(ql), own(lap * qg), own(c * lap_lap))
-        sums = [s + rows_of(a) for s, a in zip(sums, terms)]
+        terms = (middle(c * lap_pot), middle(here * qg), middle(ql), middle(lap * qg), middle(c * lap_lap))
+        sums = [s + folded(a) for s, a in zip(sums, terms)]
     for k in range(5):
         part[k] = sums[k]
     for k, z in ((0, CZ - 1), (1, 0)):
@@ -262,27 +271,19 @@
     return (6.0 + SHIFT) * c - ((zu + zd) + (x_up(c) + x_dn(c)) + (y_up(c) + y_dn(c)))
 
 
-def moment_kernel(core, b4, u4, r, s, far, w, part, edge, out, bb, uu, f, af, a2f, ab, au, send, a2b, a2u):
-    c = core[0]
+def moment_kernel(b4, u4, r, s, far, w, part, edge, out, bb, uu, f, af, a2f, ab, au, send, a2b, a2u):
+    c = lax.axis_index("gy")
     near = pl.ds(NEAR, NARROW)
-
-    def got(first, count):
-        mine, theirs = r[first : first + count], other_first(s[first : first + count])
-        return jnp.where(c == 0, mine, theirs), jnp.where(c == 0, theirs, mine)
-
-    for j in range(4):
-        lo, hi = got(NARROW * j, NARROW)
-        bb[j, near] = lo
-        bb[8 + j, near] = hi
-    for j in range(2):
-        lo, hi = got(NARROW * (4 + j), NARROW)
-        uu[j, near] = lo
-        uu[6 + j, near] = hi
-    lo, hi = got(NARROW * 6, 8)
-    for z, rim in ((3, lo), (8, hi)):
-        bb[z, NEAR - 1 : NEAR] = rim[0:1]
-        bb[z, ROWS - NEAR : ROWS - NEAR + 1] = rim[1:2]
-    bb[12, HX : HX + CX, :CY] = far[...]
+    row = 0
+    for name, k, width in AGAIN:
+        rows = CX + 2 * width
+        lo, hi = low_high(c, r[row : row + rows], s[row : row + rows])
+        dst, below = (bb, 4 - k) if name == "b" else (uu, 2 - k)
+        above = 7 + k if name == "b" else 5 + k
+        dst[below, HX - width : HX + CX + width] = lo
+        dst[above, HX - width : HX + CX + width] = hi
+        row += rows
+    bb[12, HX : HX + CX] = far[...]
     bb[4:8] = b4[...]
     uu[2:6] = u4[...]
 
@@ -309,15 +310,14 @@
     apply(au, a2u, 4)
 
     rows = pl.ds(HX, CX)
-    lanes = pl.ds(0, CY)
     acc = [jnp.zeros((8, CY), jnp.float32)] * 40
     for t in range(CZ):
-        vb, vab, va2b = bb[t + 4, rows, lanes], ab[t + 2, rows, lanes], a2b[t, rows, lanes]
-        vu, vau, va2u = uu[t + 2, rows, lanes], au[t + 1, rows, lanes], a2u[t, rows, lanes]
-        vf, vaf, va2f = f[t + 2, rows, lanes], af[t + 1, rows, lanes], a2f[t, rows, lanes]
+        vb, vab, va2b = bb[t + 4, rows], ab[t + 2, rows], a2b[t, rows]
+        vu, vau, va2u = uu[t + 2, rows], au[t + 1, rows], a2u[t, rows]
+        vf, vaf, va2f = f[t + 2, rows], af[t + 1, rows], a2f[t, rows]
         a = a2f[t]
         across = (x_up(a) + x_dn(a)) + (y_up(a) + y_dn(a))
-        va3f = (6.0 + SHIFT) * va2f - (2.0 * a2f[t + 1, rows, lanes] + own(across))
+        va3f = (6.0 + SHIFT) * va2f - (2.0 * a2f[t + 1, rows] + middle(across))
         terms = [
             vb * vb, vb * vab, vab * vab, vab * va2b,
             vu * vu, vu * vau, vau * vau, vau * va2u,
@@ -327,7 +327,7 @@
         for k in range(3):
             wk = w[k, t]
             terms += [a * wk for a in (vu, vau, vf, vaf, va2f, vb, vab)]
-        acc = [x + rows_of(a) for x, a in zip(acc, terms)]
+        acc = [x + folded(a) for x, a in zip(acc, terms)]
     rows_list = [jnp.sum(a, axis=0, keepdims=True) for a in acc]
     rows_list += [jnp.sum(part[k], axis=0, keepdims=True) for k in range(5)]
     rows_list += [jnp.zeros((1, CY), jnp.float32)] * (48 - NUM_SUMS)
@@ -336,7 +336,7 @@
     line = lax.broadcasted_iota(jnp.int32, (48, SLOTS), 1)
     which = lax.broadcasted_iota(jnp.int32, (48, SLOTS), 0)
     row = jnp.sum(jnp.where(line == which, totals, 0.0), axis=0, keepdims=True)
-    out[...] = jnp.broadcast_to(row, (DEVICES, SLOTS))
+    out[...] = jnp.broadcast_to(row, (PARTNERS, SLOTS))
     send[0:4] = edge[c]
     first = 2 * (1 - c)
     send[4] = a2f[first, near]
@@ -356,17 +356,17 @@
 
 
 def last_kernel(
-    coefs, core, gathered, bb, uu, f, af, a2f, ab, au, ri, si, e, q, adj4, pot, g,
+    coefs, gathered, bb, uu, f, af, a2f, ab, au, ri, si, e, q, adj4, pot, g,
     phase_back, velocity_back, params, phi, pr, pa, adj, qe, a2e, afe, aue,
 ):
-    c = core[0]
-    near = pl.ds(NEAR, ROWS - 2 * NEAR)
+    c = lax.axis_index("gy")
+    near = pl.ds(NEAR, NARROW)
     for i in range(2):
-        lo, hi = low_high(c, ri, si, i)
+        lo, hi = low_high(c, ri[i], si[i])
         qe[i, 0, near] = lo
         qe[i, 5, near] = hi
         qe[i, 1:5] = q[i + 1, 1:5]
-        lo, hi = low_high(c, ri, si, 2 + i)
+        lo, hi = low_high(c, ri[2 + i], si[2 + i])
         adj[i, near] = lo
         adj[6 + i, near] = hi
     adj[2:6] = adj4[...]
@@ -409,12 +409,12 @@
     params[...] = (packed * scale)[0, 0:4]
 
     for j in range(2):
-        lo, hi = low_high(c, ri, si, 4 + j)
+        lo, hi = low_high(c, ri[4 + j], si[4 + j])
         a2e[j, near] = lo
         a2e[6 + j, near] = hi
     a2e[2:6] = a2f[0:4]
     for j, (src, dst) in enumerate(((af, afe), (au, aue))):
-        lo, hi = low_high(c, ri, si, 6 + j)
+        lo, hi = low_high(c, ri[6 + j], si[6 + j])
         dst[0, near] = lo
         dst[7, near] = hi
         dst[1:7] = src[0:6]
@@ -529,13 +529,12 @@
 
 
 def local(phase, velocity, phase_obs, velocity_obs, coefs):
-    core = lax.axis_index("gy").astype(jnp.int32).reshape(1)
     mine = (velocity, phase, phase_obs, velocity_obs)
-    stack, edges, coefs = pl.pallas_call(
+    stack, edges, coefs, give = pl.pallas_call(
         load_kernel,
-        out_shape=(f32(8 * CZ, CX, CY), f32(6 * CZ, 2 * HX, CY), f32(4)),
+        out_shape=(f32(8 * CZ, CX, CY), f32(6 * CZ, 2 * HX, CY), f32(4), f32(len(SENT), CX, CY)),
         in_specs=[pl.BlockSpec(memory_space=pltpu.HBM)] * 5,
-        out_specs=(VM, VM, VM),
+        out_specs=(VM,) * 4,
         scratch_shapes=[pltpu.SemaphoreType.DMA((9,))],
         compiler_params=PARAMS,
         name="load",
@@ -544,34 +543,34 @@
     gxr = lax.ppermute(edges, "gx", SWAP)
     main, diag = call(
         pack_kernel,
-        (f32(SENT, CX, LANES), f32(SENT, 2 * HX, LANES)),
-        (core, stack, peer),
+        (f32(len(SENT), CX, LANES), f32(CORNER_ROWS, LANES)),
+        (stack, swap(give)),
         [],
         "pack",
-        1,
+        0,
     )
     mr = role_shift(main, False)
     dr = role_shift(diag, True)
+    gxr, mr, dr = lax.optimization_barrier((gxr, mr, dr))
     gxs = swap(gxr)
     inner = call(inner_kernel, layers(TOTAL), (stack, peer, gxr, gxs), [], "inner", 0)
-    mr, inner = lax.optimization_barrier((mr, inner))
     ms = swap(mr)
     ds = swap(dr)
     e, b, u, q, pot, lph, g, lv, send, far = call(
         first_kernel,
         (layers(TOTAL), layers(4), layers(4), layers(3, 6), layers(6), layers(6), layers(3, 6), layers(3, 6),
-         f32(6 * NARROW + 8, LANES), f32(CX, CY)),
-        (coefs, core, inner, mr, ms, dr, ds),
+         f32(AGAIN_ROWS, LANES), f32(CX, LANES)),
+        (coefs, inner, mr, ms, dr, ds),
         [scratch(6)],
         "first",
-        2,
-        {2: 0},
+        1,
+        {1: 0},
     )
     r2 = role_shift(send, False)
     far = ring(far, -2)
     adj, w, part, edge = call(
         weight_kernel,
-        (layers(4), f32(3, CZ, CX, CY), f32(5, 8, CY), f32(2, 4, NARROW, LANES)),
+        (layers(4), f32(3, CZ, CX, LANES), f32(5, 8, CY), f32(2, 4, NARROW, LANES)),
         (coefs, e, q, pot, lph, g, lv),
         [],
         "weights",
@@ -581,24 +580,24 @@
     s2 = swap(r2)
     sums, bb, uu, f, af, a2f, ab, au, send = call(
         moment_kernel,
-        (f32(DEVICES, SLOTS), layers(13), layers(8), layers(9), layers(7), layers(5), layers(8), layers(6),
+        (f32(PARTNERS, SLOTS), layers(13), layers(8), layers(9), layers(7), layers(5), layers(8), layers(6),
          f32(8, NARROW, LANES)),
-        (core, b, u, r2, s2, far, w, part, edge),
+        (b, u, r2, s2, far, w, part, edge),
         [scratch(4), scratch(4)],
         "moments",
-        1,
+        0,
     )
     ri = role_shift(send, False)
-    gathered = lax.all_to_all(sums.reshape(DEVICES, 1, SLOTS), ("gx", "gy", "gz"), 0, 0).reshape(DEVICES, SLOTS)
+    gathered = lax.all_to_all(sums.reshape(PARTNERS, 1, SLOTS), ("gx", "gz"), 0, 0).reshape(PARTNERS, SLOTS)
     ri, gathered = lax.optimization_barrier((ri, gathered))
     si = swap(ri)
     phase_back, velocity_back, params = call(
         last_kernel,
         (f32(CZ, CX, CY), f32(3, CZ, CX, CY), f32(4)),
-        (coefs, core, gathered, bb, uu, f, af, a2f, ab, au, ri, si, e, q, adj, pot, g),
+        (coefs, gathered, bb, uu, f, af, a2f, ab, au, ri, si, e, q, adj, pot, g),
         [scratch(8), scratch(3, 6), scratch(6), scratch(8), scratch(2, 6), scratch(8), scratch(8), scratch(8)],
         "last",
-        2,
+        1,
     )
     return phase_back, velocity_back, params
 

time: 81.9 us -> 77.1 us (0.941)
  starting transfers between devices: 39.9 us -> 33.7 us
  waiting for transfers between devices: 10.5 us -> 16 us
  blocking collectives: 19.2 us -> 15.7 us
    ppermute x1, waiting for transfers between devices: 0.01 us -> 5.76 us  [local(): gxr = lax.ppermute(edges, 'gx', SWAP)]
    ppermute x4, starting transfers between devices: 27.9 us -> 24.5 us  [role_shift(): return lax.ppermute(value, ('gx', 'gy', 'gz'), pairs)]
    ppermute x6 -> x7, starting transfers between devices: 12 us -> 8.54 us  [swap(): return lax.ppermute(value, 'gy', SWAP)]
    all_to_all x1, blocking collectives: 19.2 us -> 15.7 us  [local(): lax.all_to_all(sums.reshape(PARTNERS, 1, SLOTS), ('gx', 'gz'), 0, 0)]
    ppermute x6 -> x7, waiting for transfers between devices: 4.91 us -> 4.57 us  [swap(): return lax.ppermute(value, 'gy', SWAP)]
  transfers between devices with their start and end apart: 12 -> 13, of which waited for: 5 -> 6; matrix products, arithmetic and copies ran while one was open for 0% -> 0% of each run, Pallas kernels for 1% -> 2%
where the time goes in v4:
time: 77.1 us; the launch traced here: 77 us
  starting transfers between devices  33.7 us (44%)
  waiting for transfers between devices  16 us (21%)
  blocking collectives  15.7 us (20%)
  Pallas kernels  10.8 us (14%)
    ppermute x4, starting transfers between devices, role_shift(): return lax.ppermute(value, ('gx', 'gy', 'gz'), pairs)  24.5 us
    all_to_all x1, blocking collectives, local(): lax.all_to_all(sums.reshape(PARTNERS, 1, SLOTS), ('gx', 'gz'), 0, 0)  15.7 us
    pallas_call x6, Pallas kernels, call(): pl.pallas_call(kernel, out_shape=outs, in_specs=[SM] * smem + [VM] * (len...  9.62 us
    ppermute x7, starting transfers between devices, swap(): return lax.ppermute(value, 'gy', SWAP)  8.54 us
    ppermute x1, waiting for transfers between devices, local(): gxr = lax.ppermute(edges, 'gx', SWAP)  5.76 us
    ppermute x1, waiting for transfers between devices, ring(): lax.ppermute(value, 'gz', [(i, (i + step) % count) for i in range(count)])  5.68 us
    ppermute x7, waiting for transfers between devices, swap(): return lax.ppermute(value, 'gy', SWAP)  4.57 us
  transfers between devices with their start and end apart: 13, of which 6 were waited for; matrix products, arithmetic and copies ran while one was open for 0% of the time, Pallas kernels for 2%

profile of v4, /device:TPU:1, one launch (start us, length us, event | category | flops | bytes accessed | tf_op | source)
XLA Modules:
  0.0 77.0 jit_solution(309675710389605661)
XLA Ops:
  0.6 1.2 %load.1 = (f32[32,32,128]{2,1,0:T(8,128)S(1)}, f32[24,16,128]{2,1,0:T(8,128)S(1)}, f32[4]{0:T(128)S(1)}, f32[7,32,128]{2,1,0:T(8,128)S(1)}) custom-call(f32[3,4,32,128]{3,2,1,0:T(8,128)} %vel.1, f32[4,32,128]{2,1,0:T(8,128)} %ph.1, f32[4,32,128]{2,1,0:T(8,128)} %po.1, f32[3,4,32,128]{3,2,1,0:T(8,128)} %vo.1, f32[4]{0:T(128)} %coefs.1), custom_call_target="tpu_custom_call" | custom-call | tf_op jit(solution)/shard_map/load/pallas_call | solution.py:533
  1.8 3.3 %collective-permute-start.2 = (f32[7,32,128]{2,1,0:T(8,128)S(1)}, f32[7,32,128]{2,1,0:T(8,128)S(1)}, u32[]{:S(2)}, u32[]{:S(2)}) collective-permute-start(f32[7,32,128]{2,1,0:T(8,128)S(1)} %get-tuple-element.45), channel_id=1, source_target_pairs={{0,64},{64,0},{1,65},{65,1},{2,66},{66,2},{3,67},{67,3},{4,68},{68... | collective-permute-start | bytes 344072 | tf_op jit(solution)/shard_map/ppermute | solution.py:515
  5.2 0.1 collective-permute-start
  5.3 0.9 %collective-permute-done.2.got = f32[7,32,128]{2,1,0:T(8,128)S(1)} collective-permute-done((f32[7,32,128]{2,1,0:T(8,128)S(1)}, f32[7,32,128]{2,1,0:T(8,128)S(1)}, u32[]{:S(2)}, u32[]{:S(2)}) %collective-permute-start.2) | collective-permute-done | bytes 114720 | tf_op jit(solution)/shard_map/ppermute | solution.py:515
  6.1 9.0 %collective-permute-start.3 = (f32[7,32,256]{2,1,0:T(8,128)S(1)}, f32[7,32,256]{2,1,0:T(8,128)S(1)}, u32[]{:S(2)}, u32[]{:S(2)}) collective-permute-start(f32[7,32,256]{2,1,0:T(8,128)S(1)} %get-tuple-element.46), channel_id=1, source_target_pairs={{0,1},{1,2},{2,3},{3,4},{4,5},{5,6},{6,7},{7,8},{8,9},{9,10},{10,1... | collective-permute-start | bytes 688136 | tf_op jit(solution)/shard_map/ppermute | solution.py:506
  15.2 0.7 collective-permute-start.1
  15.9 0.1 collective-permute-start.4
  16.0 5.8 %collective-permute-done.1.gxr = f32[24,16,128]{2,1,0:T(8,128)S(1)} collective-permute-done((f32[24,16,128]{2,1,0:T(8,128)S(1)}, f32[24,16,128]{2,1,0:T(8,128)S(1)}, u32[]{:S(2)}, u32[]{:S(2)}) %collective-permute-start.1) | collective-permute-done | bytes 196640 | tf_op jit(solution)/shard_map/ppermute | solution.py:543
  21.8 2.3 %collective-permute-start.6 = (f32[7,32,256]{2,1,0:T(8,128)S(1)}, f32[7,32,256]{2,1,0:T(8,128)S(1)}, u32[]{:S(2)}, u32[]{:S(2)}) collective-permute-start(f32[7,32,256]{2,1,0:T(8,128)S(1)} %collective-permute-done.3.mr), channel_id=1, source_target_pairs={{0,64},{64,0},{1,65},{65,1},{2,66},{66,2},{3,67},{67,3},{4,68},{68... | collective-permute-start | bytes 688136 | tf_op jit(solution)/shard_map/ppermute | solution.py:515
  24.0 0.5 collective-permute-start.7
  24.5 0.9 %collective-permute-done.5.gxs = f32[24,16,128]{2,1,0:T(8,128)S(1)} collective-permute-done((f32[24,16,128]{2,1,0:T(8,128)S(1)}, f32[24,16,128]{2,1,0:T(8,128)S(1)}, u32[]{:S(2)}, u32[]{:S(2)}) %collective-permute-start.5) | collective-permute-done | bytes 196640 | tf_op jit(solution)/shard_map/ppermute | solution.py:515
  25.4 0.1 inner.1
  25.6 0.0 collective-permute-done.7.ds
  25.6 2.6 %first.1 = (f32[46,48,256]{2,1,0:T(8,128)S(1)}, f32[4,48,256]{2,1,0:T(8,128)S(1)}, f32[4,48,256]{2,1,0:T(8,128)S(1)}, f32[3,6,48,256]{3,2,1,0:T(8,128)S(1)}, f32...) custom-call(f32[4]{0:T(128)S(1)} %get-tuple-element.42.coefs, ...), custom_call_target="tpu_custom_call", output_to_operand_aliasing={{0}: (1, {})} | custom-call | tf_op jit(solution)/shard_map/first/pallas_call | solution.py:519
  28.2 7.4 %collective-permute-start.8 = (f32[232,256]{1,0:T(8,128)S(1)}, f32[232,256]{1,0:T(8,128)S(1)}, u32[]{:S(2)}, u32[]{:S(2)}) collective-permute-start(f32[232,256]{1,0:T(8,128)S(1)} %get-tuple-element.53), channel_id=1, source_target_pairs={{0,1},{1,2},{2,3},{3,4},{4,5},{5,6},{6,7},{7,8},{8,9},{9,10},{10,1... | collective-permute-start | bytes 712712 | tf_op jit(solution)/shard_map/ppermute | solution.py:506
  35.6 1.2 %weights.1 = (f32[4,48,256]{2,1,0:T(8,128)S(1)}, f32[3,4,32,256]{3,2,1,0:T(8,128)S(1)}, f32[5,8,128]{2,1,0:T(8,128)S(1)}, f32[2,4,40,256]{3,2,1,0:T(8,128)S(1)}) custom-call(f32[4]{0:T(128)S(1)} %get-tuple-element.42.coefs, f32[46,48,256]{2,1,0:T(8,128)S(1)} %get-tuple-element.55.e, f32[3,6,48,256]{3,2,1,0:T(8,128)S(1)} %get-tuple-element.56.q, ...), custom_call_target="tpu_custom_call" | custom-call | tf_op jit(solution)/shard_map/weights/pallas_call | solution.py:519
  36.8 5.7 %collective-permute-done.9.far = f32[32,256]{1,0:T(8,128)S(1)} collective-permute-done((f32[32,256]{1,0:T(8,128)S(1)}, f32[32,256]{1,0:T(8,128)S(1)}, u32[]{:S(2)}, u32[]{:S(2)}) %collective-permute-start.9) | collective-permute-done | bytes 32800 | tf_op jit(solution)/shard_map/ppermute | solution.py:511
  42.5 1.5 %collective-permute-done.10.s = f32[232,256]{1,0:T(8,128)S(1)} collective-permute-done((f32[232,256]{1,0:T(8,128)S(1)}, f32[232,256]{1,0:T(8,128)S(1)}, u32[]{:S(2)}, u32[]{:S(2)}) %collective-permute-start.10) | collective-permute-done | bytes 237600 | tf_op jit(solution)/shard_map/ppermute | solution.py:515
  44.0 2.7 %moments.1 = (f32[128,64]{1,0:T(8,128)S(1)}, f32[13,48,256]{2,1,0:T(8,128)S(1)}, f32[8,48,256]{2,1,0:T(8,128)S(1)}, f32[9,48,256]{2,1,0:T(8,128)S(1)}, f32[7,48,...) custom-call(f32[4,48,256]{2,1,0:T(8,128)S(1)} %get-tuple-element.51., ...), custom_call_target="tpu_custom_call" | custom-call | tf_op jit(solution)/shard_map/moments/pallas_call | solution.py:519
  46.7 8.0 %collective-permute-start.11 = (f32[8,40,256]{2,1,0:T(8,128)S(1)}, f32[8,40,256]{2,1,0:T(8,128)S(1)}, u32[]{:S(2)}, u32[]{:S(2)}) collective-permute-start(f32[8,40,256]{2,1,0:T(8,128)S(1)} %get-tuple-element.69), channel_id=1, source_target_pairs={{0,1},{1,2},{2,3},{3,4},{4,5},{5,6},{6,7},{7,8},{8,9},{9,10},{10,1... | collective-permute-start | bytes 983048 | tf_op jit(solution)/shard_map/ppermute | solution.py:506
  54.7 15.7 %all_to_all.5 = f32[128,1,64]{2,1,0:T(1,128)S(1)} all-to-all(f32[128,1,64]{2,1,0:T(1,128)S(1)} %bitcast.5), channel_id=1, replica_groups=mesh['gx'=2,'gy'=2,'gz'=64] {'gx','gz'}, dimensions={0} | all-to-all | bytes 65536 | tf_op jit(solution)/shard_map/all_to_all | solution.py:591
  70.4 2.3 %collective-permute-start.12 = (f32[8,40,256]{2,1,0:T(8,128)S(1)}, f32[8,40,256]{2,1,0:T(8,128)S(1)}, u32[]{:S(2)}, u32[]{:S(2)}) collective-permute-start(f32[8,40,256]{2,1,0:T(8,128)S(1)} %collective-permute-done.11.ri), channel_id=1, source_target_pairs={{0,64},{64,0},{1,65},{65,1},{2,66},{66,2},{3,67},{67,3},{4,68},{68... | collective-permute-start | bytes 983048 | tf_op jit(solution)/shard_map/ppermute | solution.py:515
  72.8 1.3 %collective-permute-done.12.si = f32[8,40,256]{2,1,0:T(8,128)S(1)} collective-permute-done((f32[8,40,256]{2,1,0:T(8,128)S(1)}, f32[8,40,256]{2,1,0:T(8,128)S(1)}, u32[]{:S(2)}, u32[]{:S(2)}) %collective-permute-start.12) | collective-permute-done | bytes 327712 | tf_op jit(solution)/shard_map/ppermute | solution.py:515
  74.0 2.9 %last.1 = (f32[4,32,128]{2,1,0:T(8,128)}, f32[3,4,32,128]{3,2,1,0:T(8,128)}, f32[4]{0:T(128)}) custom-call(f32[4]{0:T(128)S(1)} %get-tuple-element.42.coefs, f32[128,64]{1,0:T(8,128)S(1)} %bitcast.4, f32[13,48,256]{2,1,0:T(8,128)S(1)} %get-tuple-element.72.bb, f32[8,48,256]{2,1,0:T(8,128)S(1)} %get-tuple-element.73.uu, ...), custom_call_target="tpu_custom_call" | custom-call | tf_op jit(solution)/shard_map/last/pallas_call | solution.py:519
  (10 shorter events, 0.1 us)
Async XLA Ops:
  1.8 4.3 %collective-permute-start.2 = (f32[7,32,128]{2,1,0:T(8,128)S(1)}, f32[7,32,128]{2,1,0:T(8,128)S(1)}, u32[]{:S(2)}, u32[]{:S(2)}) collective-permute-start(f32[7,32,128]{2,1,0:T(8,128)S(1)} %get-tuple-element.45), channel_id=1, source_target_pairs={{0,64},{64,0},{1,65},{65,1},{2,66},{66,2},{3,67},{67,3},{4,68},{68... | collective-permute-start | bytes 344072 | tf_op jit(solution)/shard_map/ppermute | solution.py:515
  5.2 19.4 %collective-permute-start = (f32[32,32,128]{2,1,0:T(8,128)S(1)}, f32[32,32,128]{2,1,0:T(8,128)S(1)}, u32[]{:S(2)}, u32[]{:S(2)}) collective-permute-start(f32[32,32,128]{2,1,0:T(8,128)S(1)} %get-tuple-element.43.stack), channel_id=1, source_target_pairs={{0,64},{64,0},{1,65},{65,1},{2,66},{66,2},{3,67},{67,3},{4,68},{68... | collective-permute-start | bytes 1572872 | tf_op jit(solution)/shard_map/ppermute | solution.py:515
  6.1 15.6 %collective-permute-start.3 = (f32[7,32,256]{2,1,0:T(8,128)S(1)}, f32[7,32,256]{2,1,0:T(8,128)S(1)}, u32[]{:S(2)}, u32[]{:S(2)}) collective-permute-start(f32[7,32,256]{2,1,0:T(8,128)S(1)} %get-tuple-element.46), channel_id=1, source_target_pairs={{0,1},{1,2},{2,3},{3,4},{4,5},{5,6},{6,7},{7,8},{8,9},{9,10},{10,1... | collective-permute-start | bytes 688136 | tf_op jit(solution)/shard_map/ppermute | solution.py:506
  15.2 6.6 %collective-permute-start.1 = (f32[24,16,128]{2,1,0:T(8,128)S(1)}, f32[24,16,128]{2,1,0:T(8,128)S(1)}, u32[]{:S(2)}, u32[]{:S(2)}) collective-permute-start(f32[24,16,128]{2,1,0:T(8,128)S(1)} %get-tuple-element.44), channel_id=1, source_target_pairs={{0,128},{128,0},{1,129},{129,1},{2,130},{130,2},{3,131},{131,3},{4... | collective-permute-start | bytes 589832 | tf_op jit(solution)/shard_map/ppermute | solution.py:543
  15.9 5.9 %collective-permute-start.4 = (f32[88,256]{1,0:T(8,128)S(1)}, f32[88,256]{1,0:T(8,128)S(1)}, u32[]{:S(2)}, u32[]{:S(2)}) collective-permute-start(f32[88,256]{1,0:T(8,128)S(1)} %get-tuple-element.47), channel_id=1, source_target_pairs={{0,129},{1,130},{2,131},{3,132},{4,133},{5,134},{6,135},{7,136},{8... | collective-permute-start | bytes 270344 | tf_op jit(solution)/shard_map/ppermute | solution.py:506
  21.8 3.8 %collective-permute-start.6 = (f32[7,32,256]{2,1,0:T(8,128)S(1)}, f32[7,32,256]{2,1,0:T(8,128)S(1)}, u32[]{:S(2)}, u32[]{:S(2)}) collective-permute-start(f32[7,32,256]{2,1,0:T(8,128)S(1)} %collective-permute-done.3.mr), channel_id=1, source_target_pairs={{0,64},{64,0},{1,65},{65,1},{2,66},{66,2},{3,67},{67,3},{4,68},{68... | collective-permute-start | bytes 688136 | tf_op jit(solution)/shard_map/ppermute | solution.py:515
  24.0 1.4 %collective-permute-start.5 = (f32[24,16,128]{2,1,0:T(8,128)S(1)}, f32[24,16,128]{2,1,0:T(8,128)S(1)}, u32[]{:S(2)}, u32[]{:S(2)}) collective-permute-start(f32[24,16,128]{2,1,0:T(8,128)S(1)} %collective-permute-done.1.gxr), channel_id=1, source_target_pairs={{0,64},{64,0},{1,65},{65,1},{2,66},{66,2},{3,67},{67,3},{4,68},{68... | collective-permute-start | bytes 589832 | tf_op jit(solution)/shard_map/ppermute | solution.py:515
  24.0 1.6 %collective-permute-start.7 = (f32[88,256]{1,0:T(8,128)S(1)}, f32[88,256]{1,0:T(8,128)S(1)}, u32[]{:S(2)}, u32[]{:S(2)}) collective-permute-start(f32[88,256]{1,0:T(8,128)S(1)} %collective-permute-done.4.dr), channel_id=1, source_target_pairs={{0,64},{64,0},{1,65},{65,1},{2,66},{66,2},{3,67},{67,3},{4,68},{68... | collective-permute-start | bytes 270344 | tf_op jit(solution)/shard_map/ppermute | solution.py:515
  28.2 14.3 %collective-permute-start.8 = (f32[232,256]{1,0:T(8,128)S(1)}, f32[232,256]{1,0:T(8,128)S(1)}, u32[]{:S(2)}, u32[]{:S(2)}) collective-permute-start(f32[232,256]{1,0:T(8,128)S(1)} %get-tuple-element.53), channel_id=1, source_target_pairs={{0,1},{1,2},{2,3},{3,4},{4,5},{5,6},{6,7},{7,8},{8,9},{9,10},{10,1... | collective-permute-start | bytes 712712 | tf_op jit(solution)/shard_map/ppermute | solution.py:506
  35.6 6.9 %collective-permute-start.9 = (f32[32,256]{1,0:T(8,128)S(1)}, f32[32,256]{1,0:T(8,128)S(1)}, u32[]{:S(2)}, u32[]{:S(2)}) collective-permute-start(f32[32,256]{1,0:T(8,128)S(1)} %get-tuple-element.54), channel_id=1, source_target_pairs={{0,62},{1,63},{2,0},{3,1},{4,2},{5,3},{6,4},{7,5},{8,6},{9,7},{10,... | collective-permute-start | bytes 98312 | tf_op jit(solution)/shard_map/ppermute | solution.py:511
  42.5 1.5 %collective-permute-start.10 = (f32[232,256]{1,0:T(8,128)S(1)}, f32[232,256]{1,0:T(8,128)S(1)}, u32[]{:S(2)}, u32[]{:S(2)}) collective-permute-start(f32[232,256]{1,0:T(8,128)S(1)} %collective-permute-done.8.r), channel_id=1, source_target_pairs={{0,64},{64,0},{1,65},{65,1},{2,66},{66,2},{3,67},{67,3},{4,68},{68... | collective-permute-start | bytes 712712 | tf_op jit(solution)/shard_map/ppermute | solution.py:515
  46.7 23.7 %collective-permute-start.11 = (f32[8,40,256]{2,1,0:T(8,128)S(1)}, f32[8,40,256]{2,1,0:T(8,128)S(1)}, u32[]{:S(2)}, u32[]{:S(2)}) collective-permute-start(f32[8,40,256]{2,1,0:T(8,128)S(1)} %get-tuple-element.69), channel_id=1, source_target_pairs={{0,1},{1,2},{2,3},{3,4},{4,5},{5,6},{6,7},{7,8},{8,9},{9,10},{10,1... | collective-permute-start | bytes 983048 | tf_op jit(solution)/shard_map/ppermute | solution.py:506
  70.4 3.6 %collective-permute-start.12 = (f32[8,40,256]{2,1,0:T(8,128)S(1)}, f32[8,40,256]{2,1,0:T(8,128)S(1)}, u32[]{:S(2)}, u32[]{:S(2)}) collective-permute-start(f32[8,40,256]{2,1,0:T(8,128)S(1)} %collective-permute-done.11.ri), channel_id=1, source_target_pairs={{0,64},{64,0},{1,65},{65,1},{2,66},{66,2},{3,67},{67,3},{4,68},{68... | collective-permute-start | bytes 983048 | tf_op jit(solution)/shard_map/ppermute | solution.py:515

commit v5 on v4

--- a/solution.py
+++ b/solution.py
@@ -10,7 +10,6 @@
 CZ, CX, CY = 4, 32, 128
 HX = 8
 NEAR = 4
-UNROLL = 4
 NARROW = (CX + 2 * HX) - 2 * NEAR
 ROWS = CX + 2 * HX
 LANES = 2 * CY
@@ -78,7 +77,7 @@
         body(t)
         return carry
 
-    lax.fori_loop(0, count, step, 0, unroll=UNROLL)
+    lax.fori_loop(0, count, step, 0, unroll=count)
 
 
 def low_high(core, mine, theirs):
@@ -229,7 +228,7 @@
     return a[HX : HX + CX]
 
 
-def weight_kernel(coefs, e, q, pot, lph, g, lv, adj, w, part, edge):
+def weight_kernel(coefs, e, q, pot, lph, g, lv, adj, w, part, edge, gv, base):
     mobility = 0.1 * coefs[0]
 
     def at(field, z):
@@ -253,6 +252,13 @@
         flow = at(V0, t) * gs[0] + at(V1, t) * gs[1] + at(V2, t) * gs[2]
         c = at(PH, t) - DT * flow + (DT * mobility) * lap_pot - at(PO, t)
         adj[t] = c
+        v1, v2 = at(V1, t), at(V2, t)
+        base[t] = own(c + DT * (dx(v1 * c) + dy(v2 * c)))
+        for i, field in enumerate((V0, V1, V2)):
+            a = at(field, t)
+            gv[0, i, t] = own(0.5 * (at(field, t + 1) - at(field, t - 1)))
+            gv[1, i, t] = own(dx(a))
+            gv[2, i, t] = own(dy(a))
         qs = [q[i, t + 1] for i in range(3)]
         qg = qs[0] * gs[0] + qs[1] * gs[1] + qs[2] * gs[2]
         ql = qs[0] * lv[0, t + 1] + qs[1] * lv[1, t] + qs[2] * lv[2, t]
@@ -347,34 +353,12 @@
 
 def steps(m0, m1, m2, m3):
     alpha = m0 / m1
-    norm = m0 * ((m0 * m2) / (m1 * m1) - 1.0)
-    beta = norm / m0
-    one = 1.0 + beta
-    curve = one * one * m1 - 2.0 * one * alpha * m2 + alpha * alpha * m3
-    second = norm / curve
-    return alpha + second * one, -second * alpha
-
-
-def last_kernel(
-    coefs, gathered, bb, uu, f, af, a2f, ab, au, ri, si, e, q, adj4, pot, g,
-    phase_back, velocity_back, params, phi, pr, pa, adj, qe, a2e, afe, aue,
-):
-    c = lax.axis_index("gy")
-    near = pl.ds(NEAR, NARROW)
-    for i in range(2):
-        lo, hi = low_high(c, ri[i], si[i])
-        qe[i, 0, near] = lo
-        qe[i, 5, near] = hi
-        qe[i, 1:5] = q[i + 1, 1:5]
-        lo, hi = low_high(c, ri[2 + i], si[2 + i])
-        adj[i, near] = lo
-        adj[6 + i, near] = hi
-    adj[2:6] = adj4[...]
-    mobility = 0.1 * coefs[0]
-    tension = 0.5 * coefs[1]
-    viscosity = 0.1 * coefs[2]
-    interface = 0.5 * coefs[3]
-
+    second = (m1 / m0) * ((m0 * m2 - m1 * m1) / (m1 * m3 - m2 * m2))
+    second = jnp.clip(second, 1.0 / (12.0 + SHIFT), 1.0 / SHIFT)
+    return alpha + second * ((m0 * m2) / (m1 * m1)), -second * alpha
+
+
+def solve_kernel(gathered, mobility, tension, coef_out, params):
     total = jnp.sum(gathered[...], axis=0, keepdims=True)
     line = lax.broadcasted_iota(jnp.int32, (1, SLOTS), 1)
 
@@ -382,16 +366,18 @@
         return jnp.sum(jnp.where(line == k, total, 0.0), axis=1, keepdims=True)
 
     c0, c1 = steps(s(0), s(1), s(2), s(3))
-    m_uu = [s(4 + k) for k in range(4)]
-    m_uf = [s(8 + k) for k in range(5)]
-    m_ff = [s(13 + k) for k in range(6)]
+    uu = [s(4 + k) for k in range(4)]
+    uf = [s(8 + k) for k in range(5)]
+    ff = [s(13 + k) for k in range(6)]
     moments = [
-        m_uu[k] - 2.0 * (c0 * m_uf[k] + c1 * m_uf[k + 1])
-        + (c0 * c0) * m_ff[k] + (2.0 * c0 * c1) * m_ff[k + 1] + (c1 * c1) * m_ff[k + 2]
+        uu[k] - 2.0 * (c0 * uf[k] + c1 * uf[k + 1])
+        + (c0 * c0) * ff[k] + (2.0 * c0 * c1) * ff[k + 1] + (c1 * c1) * ff[k + 2]
         for k in range(4)
     ]
     e0, e1 = steps(*moments)
     coef = (e0, e1, -e0 * c0, -(e0 * c1 + e1 * c0), -e1 * c1, -c0, -c1)
+    for j in range(7):
+        coef_out[j : j + 1] = jnp.broadcast_to(coef[j], (1, CY))
 
     def meet(k):
         value = coef[0] * s(19 + 7 * k)
@@ -407,26 +393,31 @@
     place = lax.broadcasted_iota(jnp.int32, (1, CY), 1)
     packed = jnp.where(place == 0, g0, jnp.where(place == 1, g1, jnp.where(place == 2, g2, g3)))
     params[...] = (packed * scale)[0, 0:4]
-
-    for j in range(2):
-        lo, hi = low_high(c, ri[4 + j], si[4 + j])
-        a2e[j, near] = lo
-        a2e[6 + j, near] = hi
-    a2e[2:6] = a2f[0:4]
-    for j, (src, dst) in enumerate(((af, afe), (au, aue))):
-        lo, hi = low_high(c, ri[6 + j], si[6 + j])
-        dst[0, near] = lo
-        dst[7, near] = hi
-        dst[1:7] = src[0:6]
-
-    def combine(t):
-        value = coef[0] * uu[t] + coef[1] * aue[t] + coef[2] * f[t] + coef[3] * afe[t]
-        phi[t] = value + coef[4] * a2e[t] + coef[5] * bb[t + 2] + coef[6] * ab[t]
-
-    loop(8, combine)
-
-    def at(field, z):
-        return e[BASE[field] + HALO[field] + z]
+    return coef
+
+
+def half_step(side, halo, coef, consts, basis, state, work, write):
+    mobility, tension, viscosity, interface = consts
+    uu, f, af, a2f, bb, ab, au = basis
+    e, q, adj4, pot, g, gv, base = state
+    phi, pr, pa, adj, qe, new = work
+    near = pl.ds(NEAR, NARROW)
+    for i in range(2):
+        qe[i, 5 * side, near] = halo(i)
+        adj[6 * side + i, near] = halo(2 + i)
+
+    def mixed(terms):
+        value = coef[0] * terms[0]
+        for a, t in zip(coef[1:], terms[1:]):
+            value = value + a * t
+        return value
+
+    i = 1 + 5 * side
+    phi[i, near] = mixed([
+        uu[i, near], au[i - 1, near], f[i, near], af[i - 1, near], halo(5 - side), bb[i + 2, near], ab[i, near],
+    ])
+    i = 7 * side
+    phi[i, near] = mixed([uu[i, near], halo(7), f[i, near], halo(6), halo(4 + side), bb[i + 2, near], ab[i, near]])
 
     def project(t):
         c = phi[t + 1]
@@ -436,45 +427,105 @@
         pr[0, t] = r0
         pr[1, t] = r1
         pr[2, t] = r2
-        d = adj[t + 1]
-        lap = adj[t + 2] + adj[t] + (x_up(d) + x_dn(d)) + (y_up(d) + y_dn(d)) - 6.0 * d
+        lap = lap_of(adj[t + 1], adj[t + 2], adj[t])
         pa[t] = (DT * mobility) * lap + (DT * tension) * (r0 * g[0, t] + r1 * g[1, t] + r2 * g[2, t])
 
-    loop(6, project)
-
-    def finish(t):
-        v0, v1, v2 = at(V0, t), at(V1, t), at(V2, t)
+    for t in new:
+        project(t)
+
+    def at(field, z):
+        return e[BASE[field] + HALO[field] + z]
+
+    for n in range(2):
+        t = 2 * side + n
+        v1, v2 = at(V1, t), at(V2, t)
         v0u, v0d = at(V0, t + 1), at(V0, t - 1)
-        c = adj[t + 2]
         here = pot[t + 1]
-        ph = at(PH, t)
+        ph = own(at(PH, t))
         lam = pa[t + 1]
-        lap = pa[t + 2] + pa[t] + (x_up(lam) + x_dn(lam)) + (y_up(lam) + y_dn(lam)) - 6.0 * lam
         up = v0u * adj[t + 3] - tension * (pot[t + 2] * pr[0, t + 2])
         dn = v0d * adj[t + 1] - tension * (pot[t] * pr[0, t])
-        div = 0.5 * (up - dn)
-        div = div + dx(v1 * c - tension * (here * pr[1, t + 1]))
-        div = div + dy(v2 * c - tension * (here * pr[2, t + 1]))
-        value = c + DT * div + (3.0 * ph * ph - 1.0) * lam - interface * lap
-        phase_back[t] = own(value)
+        div = 0.5 * (up - dn) - tension * (dx(here * pr[1, t + 1]) + dy(here * pr[2, t + 1]))
+        value = base[t] + DT * own(div) + (3.0 * ph * ph - 1.0) * own(lam)
+        write(n, 0, value - interface * own(lap_of(lam, pa[t + 2], pa[t])))
         r = [pr[i, t + 1] for i in range(3)]
-        vel = (v0, v1, v2)
-        grads = [[], [], []]
-        for i, field in enumerate((V0, V1, V2)):
-            grads[0].append(0.5 * (at(field, t + 1) - at(field, t - 1)))
-            grads[1].append(dx(vel[i]))
-            grads[2].append(dy(vel[i]))
+        mine = [own(a) for a in r]
+        c = own(adj[t + 2])
         for k in range(3):
-            mix = r[0] * grads[k][0] + r[1] * grads[k][1] + r[2] * grads[k][2]
-            ru, rd = pr[k, t + 2], pr[k, t]
-            moved = (viscosity + 0.5 * v0u) * ru + (viscosity - 0.5 * v0d) * rd
+            mix = mine[0] * gv[k, 0, t] + mine[1] * gv[k, 1, t] + mine[2] * gv[k, 2, t]
+            moved = (viscosity + 0.5 * v0u) * pr[k, t + 2] + (viscosity - 0.5 * v0d) * pr[k, t]
             moved = moved + x_up((viscosity + 0.5 * v1) * r[k]) + x_dn((viscosity - 0.5 * v1) * r[k])
             moved = moved + y_up((viscosity + 0.5 * v2) * r[k]) + y_dn((viscosity - 0.5 * v2) * r[k])
-            moved = moved - (6.0 * viscosity) * r[k]
-            value = r[k] + DT * (moved - mix - c * g[k, t + 1])
-            velocity_back[k, t] = own(value)
-
-    loop(4, finish)
+            moved = own(moved) - (6.0 * viscosity) * mine[k]
+            write(n, 1 + k, mine[k] + DT * (moved - mix - c * own(g[k, t + 1])))
+
+
+def constants(coefs):
+    return 0.1 * coefs[0], 0.5 * coefs[1], 0.1 * coefs[2], 0.5 * coefs[3]
+
+
+def near_kernel(
+    coefs, gathered, uu, f, af, a2f, bb, ab, au, ri, e, q, adj4, pot, g, gv, base,
+    params, table, phi_own, shared, result, phi, pr, pa, adj, qe,
+):
+    consts = constants(coefs)
+    coef = solve_kernel(gathered, consts[0], consts[1], table, params)
+    side = lax.axis_index("gy")
+    adj[2:6] = adj4[...]
+    for i in range(2):
+        qe[i, 1:5] = q[i + 1, 1:5]
+    for z in range(CZ):
+        value = coef[0] * uu[z + 2] + coef[1] * au[z + 1] + coef[2] * f[z + 2] + coef[3] * af[z + 1]
+        value = value + coef[4] * a2f[z] + coef[5] * bb[z + 4] + coef[6] * ab[z + 2]
+        phi[z + 2] = value
+        phi_own[z] = value
+
+    def write(n, k, value):
+        result[k, n] = value
+
+    new = [2 * side + n for n in range(4)]
+    half_step(
+        side, lambda j: ri[j], coef, consts, (uu, f, af, a2f, bb, ab, au), (e, q, adj4, pot, g, gv, base),
+        (phi, pr, pa, adj, qe, new), write,
+    )
+    for n in range(2):
+        for i in range(3):
+            shared[i, n] = pr[i, 2 + n]
+        shared[3, n] = pa[2 + n]
+
+
+def far_kernel(
+    coefs, table, uu, f, af, a2f, bb, ab, au, si, e, q, adj4, pot, g, gv, base, phi_own, shared, result,
+    phase_back, velocity_back, phi, pr, pa, adj, qe,
+):
+    consts = constants(coefs)
+    coef = [table[j : j + 1, 0:1] for j in range(7)]
+    mine = lax.axis_index("gy")
+    side = 1 - mine
+    adj[2:6] = adj4[...]
+    for i in range(2):
+        qe[i, 1:5] = q[i + 1, 1:5]
+    phi[2:6] = phi_own[...]
+    for n in range(2):
+        for i in range(3):
+            pr[i, 2 + n] = shared[i, n]
+        pa[2 + n] = shared[3, n]
+
+    def write(n, k, value):
+        if k == 0:
+            phase_back[2 * side + n] = value
+        else:
+            velocity_back[k - 1, 2 * side + n] = value
+
+    new = [4 * side + n for n in range(2)]
+    half_step(
+        side, lambda j: other_first(si[j]), coef, consts, (uu, f, af, a2f, bb, ab, au),
+        (e, q, adj4, pot, g, gv, base), (phi, pr, pa, adj, qe, new), write,
+    )
+    for n in range(2):
+        phase_back[2 * mine + n] = result[0, n]
+        for k in range(3):
+            velocity_back[k, 2 * mine + n] = result[1 + k, n]
 
 
 def f32(*shape):
@@ -568,9 +619,9 @@
     )
     r2 = role_shift(send, False)
     far = ring(far, -2)
-    adj, w, part, edge = call(
+    adj, w, part, edge, gv, base = call(
         weight_kernel,
-        (layers(4), f32(3, CZ, CX, LANES), f32(5, 8, CY), f32(2, 4, NARROW, LANES)),
+        (layers(4), f32(3, CZ, CX, LANES), f32(5, 8, CY), f32(2, 4, NARROW, LANES), f32(3, 3, CZ, CX, CY), f32(CZ, CX, CY)),
         (coefs, e, q, pot, lph, g, lv),
         [],
         "weights",
@@ -591,12 +642,23 @@
     gathered = lax.all_to_all(sums.reshape(PARTNERS, 1, SLOTS), ("gx", "gz"), 0, 0).reshape(PARTNERS, SLOTS)
     ri, gathered = lax.optimization_barrier((ri, gathered))
     si = swap(ri)
-    phase_back, velocity_back, params = call(
-        last_kernel,
-        (f32(CZ, CX, CY), f32(3, CZ, CX, CY), f32(4)),
-        (coefs, gathered, bb, uu, f, af, a2f, ab, au, ri, si, e, q, adj, pot, g),
-        [scratch(8), scratch(3, 6), scratch(6), scratch(8), scratch(2, 6), scratch(8), scratch(8), scratch(8)],
-        "last",
+    basis = (uu, f, af, a2f, bb, ab, au)
+    state = (e, q, adj, pot, g, gv, base)
+    room = [scratch(8), scratch(3, 6), scratch(6), scratch(8), scratch(2, 6)]
+    params, table, phi, shared, result = call(
+        near_kernel,
+        (f32(4), f32(8, CY), layers(4), layers(4, 2), f32(4, 2, CX, CY)),
+        (coefs, gathered, *basis, ri, *state),
+        room,
+        "near",
+        1,
+    )
+    phase_back, velocity_back = call(
+        far_kernel,
+        (f32(CZ, CX, CY), f32(3, CZ, CX, CY)),
+        (coefs, table, *basis, si, *state, phi, shared, result),
+        room,
+        "far",
         1,
     )
     return phase_back, velocity_back, params

time: 77.1 us -> 75.4 us (0.978)
  waiting for transfers between devices: 16 us -> 14.4 us
    ppermute x7, waiting for transfers between devices: 4.57 us -> 3.32 us  [swap(): return lax.ppermute(value, 'gy', SWAP)]
    pallas_call x6 -> x7, Pallas kernels: 9.62 us -> 9.54 us  [call(): pl.pallas_call(kernel, out_shape=outs, in_specs=[SM] * smem + [VM] * (len...]
  transfers between devices with their start and end apart: 13 -> 13, of which waited for: 6 -> 5; matrix products, arithmetic and copies ran while one was open for 0% -> 0% of each run, Pallas kernels for 2% -> 5%
where the time goes in v5:
time: 75.4 us; the launch traced here: 75.2 us
  starting transfers between devices  33.9 us (45%)
  blocking collectives  15.6 us (21%)
  waiting for transfers between devices  14.4 us (19%)
  Pallas kernels  10.7 us (14%)
    ppermute x4, starting transfers between devices, role_shift(): return lax.ppermute(value, ('gx', 'gy', 'gz'), pairs)  24.6 us
    all_to_all x1, blocking collectives, local(): lax.all_to_all(sums.reshape(PARTNERS, 1, SLOTS), ('gx', 'gz'), 0, 0)  15.6 us
    pallas_call x7, Pallas kernels, call(): pl.pallas_call(kernel, out_shape=outs, in_specs=[SM] * smem + [VM] * (len...  9.54 us
    ppermute x7, starting transfers between devices, swap(): return lax.ppermute(value, 'gy', SWAP)  8.54 us
    ppermute x1, waiting for transfers between devices, local(): gxr = lax.ppermute(edges, 'gx', SWAP)  5.76 us
    ppermute x1, waiting for transfers between devices, ring(): lax.ppermute(value, 'gz', [(i, (i + step) % count) for i in range(count)])  5.28 us
    ppermute x7, waiting for transfers between devices, swap(): return lax.ppermute(value, 'gy', SWAP)  3.32 us
  transfers between devices with their start and end apart: 13, of which 5 were waited for; matrix products, arithmetic and copies ran while one was open for 0% of the time, Pallas kernels for 5%

profile of v5, /device:TPU:1, one launch (start us, length us, event | category | flops | bytes accessed | tf_op | source)
XLA Modules:
  0.0 75.2 jit_solution(11575698605855009025)
XLA Ops:
  0.6 1.2 %load.1 = (f32[32,32,128]{2,1,0:T(8,128)S(1)}, f32[24,16,128]{2,1,0:T(8,128)S(1)}, f32[4]{0:T(128)S(1)}, f32[7,32,128]{2,1,0:T(8,128)S(1)}) custom-call(f32[3,4,32,128]{3,2,1,0:T(8,128)} %vel.1, f32[4,32,128]{2,1,0:T(8,128)} %ph.1, f32[4,32,128]{2,1,0:T(8,128)} %po.1, f32[3,4,32,128]{3,2,1,0:T(8,128)} %vo.1, f32[4]{0:T(128)} %coefs.1), custom_call_target="tpu_custom_call" | custom-call | tf_op jit(solution)/shard_map/load/pallas_call | solution.py:584
  1.8 3.3 %collective-permute-start.2 = (f32[7,32,128]{2,1,0:T(8,128)S(1)}, f32[7,32,128]{2,1,0:T(8,128)S(1)}, u32[]{:S(2)}, u32[]{:S(2)}) collective-permute-start(f32[7,32,128]{2,1,0:T(8,128)S(1)} %get-tuple-element.54), channel_id=1, source_target_pairs={{0,64},{64,0},{1,65},{65,1},{2,66},{66,2},{3,67},{67,3},{4,68},{68... | collective-permute-start | bytes 344072 | tf_op jit(solution)/shard_map/ppermute | solution.py:566
  5.2 0.1 collective-permute-start
  5.3 0.9 %collective-permute-done.2.got = f32[7,32,128]{2,1,0:T(8,128)S(1)} collective-permute-done((f32[7,32,128]{2,1,0:T(8,128)S(1)}, f32[7,32,128]{2,1,0:T(8,128)S(1)}, u32[]{:S(2)}, u32[]{:S(2)}) %collective-permute-start.2) | collective-permute-done | bytes 114720 | tf_op jit(solution)/shard_map/ppermute | solution.py:566
  6.1 9.0 %collective-permute-start.3 = (f32[7,32,256]{2,1,0:T(8,128)S(1)}, f32[7,32,256]{2,1,0:T(8,128)S(1)}, u32[]{:S(2)}, u32[]{:S(2)}) collective-permute-start(f32[7,32,256]{2,1,0:T(8,128)S(1)} %get-tuple-element.55), channel_id=1, source_target_pairs={{0,1},{1,2},{2,3},{3,4},{4,5},{5,6},{6,7},{7,8},{8,9},{9,10},{10,1... | collective-permute-start | bytes 688136 | tf_op jit(solution)/shard_map/ppermute | solution.py:557
  15.2 0.7 collective-permute-start.1
  15.9 0.1 collective-permute-start.4
  16.0 5.8 %collective-permute-done.1.gxr = f32[24,16,128]{2,1,0:T(8,128)S(1)} collective-permute-done((f32[24,16,128]{2,1,0:T(8,128)S(1)}, f32[24,16,128]{2,1,0:T(8,128)S(1)}, u32[]{:S(2)}, u32[]{:S(2)}) %collective-permute-start.1) | collective-permute-done | bytes 196640 | tf_op jit(solution)/shard_map/ppermute | solution.py:594
  21.8 2.3 %collective-permute-start.6 = (f32[7,32,256]{2,1,0:T(8,128)S(1)}, f32[7,32,256]{2,1,0:T(8,128)S(1)}, u32[]{:S(2)}, u32[]{:S(2)}) collective-permute-start(f32[7,32,256]{2,1,0:T(8,128)S(1)} %collective-permute-done.3.mr), channel_id=1, source_target_pairs={{0,64},{64,0},{1,65},{65,1},{2,66},{66,2},{3,67},{67,3},{4,68},{68... | collective-permute-start | bytes 688136 | tf_op jit(solution)/shard_map/ppermute | solution.py:566
  24.0 0.5 collective-permute-start.7
  24.5 0.9 %collective-permute-done.5.gxs = f32[24,16,128]{2,1,0:T(8,128)S(1)} collective-permute-done((f32[24,16,128]{2,1,0:T(8,128)S(1)}, f32[24,16,128]{2,1,0:T(8,128)S(1)}, u32[]{:S(2)}, u32[]{:S(2)}) %collective-permute-start.5) | collective-permute-done | bytes 196640 | tf_op jit(solution)/shard_map/ppermute | solution.py:566
  25.4 0.1 inner.1
  25.6 0.0 collective-permute-done.7.ds
  25.6 2.1 %first.1 = (f32[46,48,256]{2,1,0:T(8,128)S(1)}, f32[4,48,256]{2,1,0:T(8,128)S(1)}, f32[4,48,256]{2,1,0:T(8,128)S(1)}, f32[3,6,48,256]{3,2,1,0:T(8,128)S(1)}, f32...) custom-call(f32[4]{0:T(128)S(1)} %get-tuple-element.51.coefs, ...), custom_call_target="tpu_custom_call", output_to_operand_aliasing={{0}: (1, {})} | custom-call | tf_op jit(solution)/shard_map/first/pallas_call | solution.py:570
  27.7 7.4 %collective-permute-start.8 = (f32[232,256]{1,0:T(8,128)S(1)}, f32[232,256]{1,0:T(8,128)S(1)}, u32[]{:S(2)}, u32[]{:S(2)}) collective-permute-start(f32[232,256]{1,0:T(8,128)S(1)} %get-tuple-element.62), channel_id=1, source_target_pairs={{0,1},{1,2},{2,3},{3,4},{4,5},{5,6},{6,7},{7,8},{8,9},{9,10},{10,1... | collective-permute-start | bytes 712712 | tf_op jit(solution)/shard_map/ppermute | solution.py:557
  35.1 1.6 %weights.1 = (f32[4,48,256]{2,1,0:T(8,128)S(1)}, f32[3,4,32,256]{3,2,1,0:T(8,128)S(1)}, f32[5,8,128]{2,1,0:T(8,128)S(1)}, f32[2,4,40,256]{3,2,1,0:T(8,128)S(1)},...) custom-call(f32[4]{0:T(128)S(1)} %get-tuple-element.51.coefs, f32[46,48,256]{2,1,0:T(8,128)S(1)} %get-tuple-element.64.e, ...), custom_call_target="tpu_custom_call" | custom-call | tf_op jit(solution)/shard_map/weights/pallas_call | solution.py:570
  36.7 5.3 %collective-permute-done.9.far = f32[32,256]{1,0:T(8,128)S(1)} collective-permute-done((f32[32,256]{1,0:T(8,128)S(1)}, f32[32,256]{1,0:T(8,128)S(1)}, u32[]{:S(2)}, u32[]{:S(2)}) %collective-permute-start.9) | collective-permute-done | bytes 32800 | tf_op jit(solution)/shard_map/ppermute | solution.py:562
  42.0 1.5 %collective-permute-done.10.s = f32[232,256]{1,0:T(8,128)S(1)} collective-permute-done((f32[232,256]{1,0:T(8,128)S(1)}, f32[232,256]{1,0:T(8,128)S(1)}, u32[]{:S(2)}, u32[]{:S(2)}) %collective-permute-start.10) | collective-permute-done | bytes 237600 | tf_op jit(solution)/shard_map/ppermute | solution.py:566
  43.5 1.9 %moments.1 = (f32[128,64]{1,0:T(8,128)S(1)}, f32[13,48,256]{2,1,0:T(8,128)S(1)}, f32[8,48,256]{2,1,0:T(8,128)S(1)}, f32[9,48,256]{2,1,0:T(8,128)S(1)}, f32[7,48,...) custom-call(f32[4,48,256]{2,1,0:T(8,128)S(1)} %get-tuple-element.60., ...), custom_call_target="tpu_custom_call" | custom-call | tf_op jit(solution)/shard_map/moments/pallas_call | solution.py:570
  45.4 8.1 %collective-permute-start.11 = (f32[8,40,256]{2,1,0:T(8,128)S(1)}, f32[8,40,256]{2,1,0:T(8,128)S(1)}, u32[]{:S(2)}, u32[]{:S(2)}) collective-permute-start(f32[8,40,256]{2,1,0:T(8,128)S(1)} %get-tuple-element.78), channel_id=1, source_target_pairs={{0,1},{1,2},{2,3},{3,4},{4,5},{5,6},{6,7},{7,8},{8,9},{9,10},{10,1... | collective-permute-start | bytes 983048 | tf_op jit(solution)/shard_map/ppermute | solution.py:557
  53.6 15.6 %all_to_all.5 = f32[128,1,64]{2,1,0:T(1,128)S(1)} all-to-all(f32[128,1,64]{2,1,0:T(1,128)S(1)} %bitcast.5), channel_id=1, replica_groups=mesh['gx'=2,'gy'=2,'gz'=64] {'gx','gz'}, dimensions={0} | all-to-all | bytes 65536 | tf_op jit(solution)/shard_map/all_to_all | solution.py:642
  69.1 2.3 %collective-permute-start.12 = (f32[8,40,256]{2,1,0:T(8,128)S(1)}, f32[8,40,256]{2,1,0:T(8,128)S(1)}, u32[]{:S(2)}, u32[]{:S(2)}) collective-permute-start(f32[8,40,256]{2,1,0:T(8,128)S(1)} %collective-permute-done.11.ri), channel_id=1, source_target_pairs={{0,64},{64,0},{1,65},{65,1},{2,66},{66,2},{3,67},{67,3},{4,68},{68... | collective-permute-start | bytes 983048 | tf_op jit(solution)/shard_map/ppermute | solution.py:566
  71.5 1.9 %near.1 = (f32[4]{0:T(128)}, f32[8,128]{1,0:T(8,128)S(1)}, f32[4,48,256]{2,1,0:T(8,128)S(1)}, f32[4,2,48,256]{3,2,1,0:T(8,128)S(1)}, f32[4,2,32,128]{3,2,1,0:T(8,128)S(1)}) custom-call(f32[4]{0:T(128)S(1)} %get-tuple-element.51.coefs, f32[128,64]{1,0:T(8,128)S(1)} %bitcast.4, f32[8,48,256]{2,1,0:T(8,128)S(1)} %get-tuple-element.81.uu, ...), custom_call_target="tpu_custom_call" | custom-call | tf_op jit(solution)/shard_map/near/pallas_call | solution.py:570
  73.4 1.8 %far.1 = (f32[4,32,128]{2,1,0:T(8,128)}, f32[3,4,32,128]{3,2,1,0:T(8,128)}) custom-call(f32[4]{0:T(128)S(1)} %get-tuple-element.51.coefs, f32[8,128]{1,0:T(8,128)S(1)} %get-tuple-element.92.table, f32[8,48,256]{2,1,0:T(8,128)S(1)} %get-tuple-element.81.uu, f32[9,48,256]{2,1,0:T(8,128)S(1)} %get-tuple-element.82.f, f32[7,48,256]{2,1,0:T(8,128)S(1)} %get-tuple-element.83.af, ...), custom_call_target="tpu_custom_call" | custom-call | tf_op jit(solution)/shard_map/far/pallas_call | solution.py:570
  (11 shorter events, 0.1 us)
Async XLA Ops:
  1.8 4.3 %collective-permute-start.2 = (f32[7,32,128]{2,1,0:T(8,128)S(1)}, f32[7,32,128]{2,1,0:T(8,128)S(1)}, u32[]{:S(2)}, u32[]{:S(2)}) collective-permute-start(f32[7,32,128]{2,1,0:T(8,128)S(1)} %get-tuple-element.54), channel_id=1, source_target_pairs={{0,64},{64,0},{1,65},{65,1},{2,66},{66,2},{3,67},{67,3},{4,68},{68... | collective-permute-start | bytes 344072 | tf_op jit(solution)/shard_map/ppermute | solution.py:566
  5.2 19.4 %collective-permute-start = (f32[32,32,128]{2,1,0:T(8,128)S(1)}, f32[32,32,128]{2,1,0:T(8,128)S(1)}, u32[]{:S(2)}, u32[]{:S(2)}) collective-permute-start(f32[32,32,128]{2,1,0:T(8,128)S(1)} %get-tuple-element.52.stack), channel_id=1, source_target_pairs={{0,64},{64,0},{1,65},{65,1},{2,66},{66,2},{3,67},{67,3},{4,68},{68... | collective-permute-start | bytes 1572872 | tf_op jit(solution)/shard_map/ppermute | solution.py:566
  6.1 15.6 %collective-permute-start.3 = (f32[7,32,256]{2,1,0:T(8,128)S(1)}, f32[7,32,256]{2,1,0:T(8,128)S(1)}, u32[]{:S(2)}, u32[]{:S(2)}) collective-permute-start(f32[7,32,256]{2,1,0:T(8,128)S(1)} %get-tuple-element.55), channel_id=1, source_target_pairs={{0,1},{1,2},{2,3},{3,4},{4,5},{5,6},{6,7},{7,8},{8,9},{9,10},{10,1... | collective-permute-start | bytes 688136 | tf_op jit(solution)/shard_map/ppermute | solution.py:557
  15.2 6.6 %collective-permute-start.1 = (f32[24,16,128]{2,1,0:T(8,128)S(1)}, f32[24,16,128]{2,1,0:T(8,128)S(1)}, u32[]{:S(2)}, u32[]{:S(2)}) collective-permute-start(f32[24,16,128]{2,1,0:T(8,128)S(1)} %get-tuple-element.53), channel_id=1, source_target_pairs={{0,128},{128,0},{1,129},{129,1},{2,130},{130,2},{3,131},{131,3},{4... | collective-permute-start | bytes 589832 | tf_op jit(solution)/shard_map/ppermute | solution.py:594
  15.9 5.9 %collective-permute-start.4 = (f32[88,256]{1,0:T(8,128)S(1)}, f32[88,256]{1,0:T(8,128)S(1)}, u32[]{:S(2)}, u32[]{:S(2)}) collective-permute-start(f32[88,256]{1,0:T(8,128)S(1)} %get-tuple-element.56), channel_id=1, source_target_pairs={{0,129},{1,130},{2,131},{3,132},{4,133},{5,134},{6,135},{7,136},{8... | collective-permute-start | bytes 270344 | tf_op jit(solution)/shard_map/ppermute | solution.py:557
  21.8 3.8 %collective-permute-start.6 = (f32[7,32,256]{2,1,0:T(8,128)S(1)}, f32[7,32,256]{2,1,0:T(8,128)S(1)}, u32[]{:S(2)}, u32[]{:S(2)}) collective-permute-start(f32[7,32,256]{2,1,0:T(8,128)S(1)} %collective-permute-done.3.mr), channel_id=1, source_target_pairs={{0,64},{64,0},{1,65},{65,1},{2,66},{66,2},{3,67},{67,3},{4,68},{68... | collective-permute-start | bytes 688136 | tf_op jit(solution)/shard_map/ppermute | solution.py:566
  24.0 1.4 %collective-permute-start.5 = (f32[24,16,128]{2,1,0:T(8,128)S(1)}, f32[24,16,128]{2,1,0:T(8,128)S(1)}, u32[]{:S(2)}, u32[]{:S(2)}) collective-permute-start(f32[24,16,128]{2,1,0:T(8,128)S(1)} %collective-permute-done.1.gxr), channel_id=1, source_target_pairs={{0,64},{64,0},{1,65},{65,1},{2,66},{66,2},{3,67},{67,3},{4,68},{68... | collective-permute-start | bytes 589832 | tf_op jit(solution)/shard_map/ppermute | solution.py:566
  24.0 1.6 %collective-permute-start.7 = (f32[88,256]{1,0:T(8,128)S(1)}, f32[88,256]{1,0:T(8,128)S(1)}, u32[]{:S(2)}, u32[]{:S(2)}) collective-permute-start(f32[88,256]{1,0:T(8,128)S(1)} %collective-permute-done.4.dr), channel_id=1, source_target_pairs={{0,64},{64,0},{1,65},{65,1},{2,66},{66,2},{3,67},{67,3},{4,68},{68... | collective-permute-start | bytes 270344 | tf_op jit(solution)/shard_map/ppermute | solution.py:566
  27.7 14.3 %collective-permute-start.8 = (f32[232,256]{1,0:T(8,128)S(1)}, f32[232,256]{1,0:T(8,128)S(1)}, u32[]{:S(2)}, u32[]{:S(2)}) collective-permute-start(f32[232,256]{1,0:T(8,128)S(1)} %get-tuple-element.62), channel_id=1, source_target_pairs={{0,1},{1,2},{2,3},{3,4},{4,5},{5,6},{6,7},{7,8},{8,9},{9,10},{10,1... | collective-permute-start | bytes 712712 | tf_op jit(solution)/shard_map/ppermute | solution.py:557
  35.1 6.9 %collective-permute-start.9 = (f32[32,256]{1,0:T(8,128)S(1)}, f32[32,256]{1,0:T(8,128)S(1)}, u32[]{:S(2)}, u32[]{:S(2)}) collective-permute-start(f32[32,256]{1,0:T(8,128)S(1)} %get-tuple-element.63), channel_id=1, source_target_pairs={{0,62},{1,63},{2,0},{3,1},{4,2},{5,3},{6,4},{7,5},{8,6},{9,7},{10,... | collective-permute-start | bytes 98312 | tf_op jit(solution)/shard_map/ppermute | solution.py:562
  42.0 1.5 %collective-permute-start.10 = (f32[232,256]{1,0:T(8,128)S(1)}, f32[232,256]{1,0:T(8,128)S(1)}, u32[]{:S(2)}, u32[]{:S(2)}) collective-permute-start(f32[232,256]{1,0:T(8,128)S(1)} %collective-permute-done.8.r), channel_id=1, source_target_pairs={{0,64},{64,0},{1,65},{65,1},{2,66},{66,2},{3,67},{67,3},{4,68},{68... | collective-permute-start | bytes 712712 | tf_op jit(solution)/shard_map/ppermute | solution.py:566
  45.4 23.7 %collective-permute-start.11 = (f32[8,40,256]{2,1,0:T(8,128)S(1)}, f32[8,40,256]{2,1,0:T(8,128)S(1)}, u32[]{:S(2)}, u32[]{:S(2)}) collective-permute-start(f32[8,40,256]{2,1,0:T(8,128)S(1)} %get-tuple-element.78), channel_id=1, source_target_pairs={{0,1},{1,2},{2,3},{3,4},{4,5},{5,6},{6,7},{7,8},{8,9},{9,10},{10,1... | collective-permute-start | bytes 983048 | tf_op jit(solution)/shard_map/ppermute | solution.py:557
  69.1 4.3 %collective-permute-start.12 = (f32[8,40,256]{2,1,0:T(8,128)S(1)}, f32[8,40,256]{2,1,0:T(8,128)S(1)}, u32[]{:S(2)}, u32[]{:S(2)}) collective-permute-start(f32[8,40,256]{2,1,0:T(8,128)S(1)} %collective-permute-done.11.ri), channel_id=1, source_target_pairs={{0,64},{64,0},{1,65},{65,1},{2,66},{66,2},{3,67},{67,3},{4,68},{68... | collective-permute-start | bytes 983048 | tf_op jit(solution)/shard_map/ppermute | solution.py:566

commit v6 on v5

--- a/solution.py
+++ b/solution.py
@@ -24,10 +24,14 @@
     _at += CZ + 2 * _h
 TOTAL = _at
 SENT = [(f, k) for f, h in enumerate(HALO) for k in range(1, h + 1)]
-CORNER = [3 if f == O0 else 8 - k for f, k in SENT]
-CORNER_ROWS = -(-2 * sum(CORNER) // 8) * 8
+CORNER = [{(V0, 1): 1, (V1, 1): 1, (V2, 1): 1, (PH, 1): 3, (PH, 2): 2}.get(entry, 0) for entry in SENT]
+CORNER_ROWS = 2 * sum(CORNER)
+EDGE = (2, 2, 2, 4, 2, 1, 1, 1)
+EDGE_ROWS = 2 * CZ * sum(EDGE)
 AGAIN = [("b", k, 6 - k) for k in (1, 2, 3, 4)] + [("u", k, 3 - k) for k in (1, 2)]
-AGAIN_ROWS = -(-sum(CX + 2 * w for _, _, w in AGAIN) // 8) * 8
+AGAIN_ROWS = 2 * sum(w for _, _, w in AGAIN)
+RIM = [("b", z, 6) for z in range(CZ)] + [("u", z, 3) for z in range(CZ)]
+RIM_ROWS = 2 * sum(w for _, _, w in RIM)
 NUM_SUMS = 45
 SLOTS = 64
 
@@ -101,13 +105,12 @@
     other = 1 - lax.axis_index("gy")
     for n, (f, k) in enumerate(SENT):
         give[n] = stack[CZ * f + outgoing(other, k)]
-    wide = CZ * PO
-    out[0:wide, 0:HX] = stack[0:wide, CX - HX :]
-    out[0:wide, HX:] = stack[0:wide, :HX]
-    for n in range(wide):
-        at, row = wide + n // 2, HX * (n % 2)
-        out[at, row : row + NEAR] = stack[wide + n, CX - NEAR :]
-        out[at, row + NEAR : row + HX] = stack[wide + n, :NEAR]
+    row = 0
+    for f, w in enumerate(EDGE):
+        for z in range(CZ):
+            out[row : row + w] = stack[CZ * f + z, CX - w :]
+            out[row + w : row + 2 * w] = stack[CZ * f + z, :w]
+            row += 2 * w
 
 
 def pack_kernel(stack, got, main, diag):
@@ -117,30 +120,26 @@
         src = jnp.concatenate([stack[CZ * f + outgoing(c, k)], got[n]], 1)
         main[n] = src
         w = CORNER[n]
-        diag[row : row + w] = src[CX - w :]
-        diag[row + w : row + 2 * w] = src[:w]
+        if w:
+            diag[row : row + w] = src[CX - w :]
+            diag[row + w : row + 2 * w] = src[:w]
         row += 2 * w
 
 
 def inner_kernel(stack, peer, gxr, gxs, e):
-    for f, h in enumerate(HALO):
-        mid = BASE[f] + h
+    row = 0
+    for f, w in enumerate(EDGE):
+        mid = BASE[f] + HALO[f]
         for z in range(CZ):
             for half, x in enumerate((gxr, gxs)):
-                src = (stack, peer)[half][CZ * f + z]
                 lanes = pl.ds(CY * half, CY)
-                e[mid + z, HX : HX + CX, lanes] = src
-                if f <= PH:
-                    e[mid + z, 0:HX, lanes] = x[CZ * f + z, 0:HX]
-                    e[mid + z, HX + CX :, lanes] = x[CZ * f + z, HX:]
-                else:
-                    k = CZ * (f - PO) + z
-                    pair, row = CZ * PO + k // 2, HX * (k % 2)
-                    e[mid + z, HX - NEAR : HX, lanes] = x[pair, row : row + NEAR]
-                    e[mid + z, HX + CX : HX + CX + NEAR, lanes] = x[pair, row + NEAR : row + HX]
-
-
-def first_kernel(coefs, inner, mr, ms, dr, ds, e, b, u, q, pot, lph, g, lv, send, far, p0):
+                e[mid + z, HX : HX + CX, lanes] = (stack, peer)[half][CZ * f + z]
+                e[mid + z, HX - w : HX, lanes] = x[row : row + w]
+                e[mid + z, HX + CX : HX + CX + w, lanes] = x[row + w : row + 2 * w]
+            row += 2 * w
+
+
+def first_kernel(coefs, inner, mr, ms, dr, ds, e, b, u, q, pot, lph, g, lv, send, corner, rim, far, p0):
     tension = 0.5 * coefs[1]
     viscosity = 0.1 * coefs[2]
     interface = 0.5 * coefs[3]
@@ -153,6 +152,8 @@
         e[below, HX : HX + CX] = lo
         e[above, HX : HX + CX] = hi
         w = CORNER[n]
+        if w == 0:
+            continue
         lo, hi = low_high(c, dr[row : row + 2 * w], ds[row : row + 2 * w])
         for layer, part in ((below, lo), (above, hi)):
             e[layer, HX - w : HX] = part[:w]
@@ -211,11 +212,18 @@
     loop(4, across)
 
     row = 0
-    for name, k, w in AGAIN:
+    for n, (name, k, w) in enumerate(AGAIN):
+        src = (b if name == "b" else u)[outgoing(c, k)]
+        send[CX * n : CX * (n + 1)] = src[HX : HX + CX]
+        corner[row : row + w] = src[HX + CX - w : HX + CX]
+        corner[row + w : row + 2 * w] = src[HX : HX + w]
+        row += 2 * w
+    row = 0
+    for name, z, w in RIM:
         field = b if name == "b" else u
-        rows = CX + 2 * w
-        send[row : row + rows] = field[outgoing(c, k), HX - w : HX + CX + w]
-        row += rows
+        rim[row : row + w] = field[z, HX + CX - w : HX + CX, :CY]
+        rim[row + w : row + 2 * w] = field[z, HX : HX + w, :CY]
+        row += 2 * w
     far[...] = b[0, HX : HX + CX]
 
 
@@ -277,21 +285,32 @@
     return (6.0 + SHIFT) * c - ((zu + zd) + (x_up(c) + x_dn(c)) + (y_up(c) + y_dn(c)))
 
 
-def moment_kernel(b4, u4, r, s, far, w, part, edge, out, bb, uu, f, af, a2f, ab, au, send, a2b, a2u):
+def moment_kernel(b4, u4, r, s, d, ds, x, xs, far, w, part, edge, out, bb, uu, f, af, a2f, ab, au, send, a2b, a2u):
     c = lax.axis_index("gy")
     near = pl.ds(NEAR, NARROW)
+    bb[4:8] = b4[...]
+    uu[2:6] = u4[...]
     row = 0
-    for name, k, width in AGAIN:
-        rows = CX + 2 * width
-        lo, hi = low_high(c, r[row : row + rows], s[row : row + rows])
+    for n, (name, k, width) in enumerate(AGAIN):
         dst, below = (bb, 4 - k) if name == "b" else (uu, 2 - k)
         above = 7 + k if name == "b" else 5 + k
-        dst[below, HX - width : HX + CX + width] = lo
-        dst[above, HX - width : HX + CX + width] = hi
-        row += rows
+        lo, hi = low_high(c, r[CX * n : CX * (n + 1)], s[CX * n : CX * (n + 1)])
+        dst[below, HX : HX + CX] = lo
+        dst[above, HX : HX + CX] = hi
+        lo, hi = low_high(c, d[row : row + 2 * width], ds[row : row + 2 * width])
+        for layer, part_rows in ((below, lo), (above, hi)):
+            dst[layer, HX - width : HX] = part_rows[:width]
+            dst[layer, HX + CX : HX + CX + width] = part_rows[width:]
+        row += 2 * width
+    row = 0
+    for name, z, width in RIM:
+        dst, layer = (bb, 4 + z) if name == "b" else (uu, 2 + z)
+        for half, src in enumerate((x, xs)):
+            lanes = pl.ds(CY * half, CY)
+            dst[layer, HX - width : HX, lanes] = src[row : row + width]
+            dst[layer, HX + CX : HX + CX + width, lanes] = src[row + width : row + 2 * width]
+        row += 2 * width
     bb[12, HX : HX + CX] = far[...]
-    bb[4:8] = b4[...]
-    uu[2:6] = u4[...]
 
     def wide(t):
         a = bb[t + 2]
@@ -583,7 +602,7 @@
     mine = (velocity, phase, phase_obs, velocity_obs)
     stack, edges, coefs, give = pl.pallas_call(
         load_kernel,
-        out_shape=(f32(8 * CZ, CX, CY), f32(6 * CZ, 2 * HX, CY), f32(4), f32(len(SENT), CX, CY)),
+        out_shape=(f32(8 * CZ, CX, CY), f32(EDGE_ROWS, CY), f32(4), f32(len(SENT), CX, CY)),
         in_specs=[pl.BlockSpec(memory_space=pltpu.HBM)] * 5,
         out_specs=(VM,) * 4,
         scratch_shapes=[pltpu.SemaphoreType.DMA((9,))],
@@ -607,10 +626,10 @@
     inner = call(inner_kernel, layers(TOTAL), (stack, peer, gxr, gxs), [], "inner", 0)
     ms = swap(mr)
     ds = swap(dr)
-    e, b, u, q, pot, lph, g, lv, send, far = call(
+    e, b, u, q, pot, lph, g, lv, send, corner, rim, far = call(
         first_kernel,
         (layers(TOTAL), layers(4), layers(4), layers(3, 6), layers(6), layers(6), layers(3, 6), layers(3, 6),
-         f32(AGAIN_ROWS, LANES), f32(CX, LANES)),
+         f32(CX * len(AGAIN), LANES), f32(AGAIN_ROWS, LANES), f32(RIM_ROWS, CY), f32(CX, LANES)),
         (coefs, inner, mr, ms, dr, ds),
         [scratch(6)],
         "first",
@@ -618,6 +637,8 @@
         {1: 0},
     )
     r2 = role_shift(send, False)
+    d2 = role_shift(corner, True)
+    x2 = lax.ppermute(rim, "gx", SWAP)
     far = ring(far, -2)
     adj, w, part, edge, gv, base = call(
         weight_kernel,
@@ -627,13 +648,13 @@
         "weights",
         1,
     )
-    r2, far, w, part, edge = lax.optimization_barrier((r2, far, w, part, edge))
-    s2 = swap(r2)
+    r2, d2, x2, far, w, part, edge = lax.optimization_barrier((r2, d2, x2, far, w, part, edge))
+    s2, ds2, xs2 = swap(r2), swap(d2), swap(x2)
     sums, bb, uu, f, af, a2f, ab, au, send = call(
         moment_kernel,
         (f32(PARTNERS, SLOTS), layers(13), layers(8), layers(9), layers(7), layers(5), layers(8), layers(6),
          f32(8, NARROW, LANES)),
-        (b, u, r2, s2, far, w, part, edge),
+        (b, u, r2, s2, d2, ds2, x2, xs2, far, w, part, edge),
         [scratch(4), scratch(4)],
         "moments",
         0,

time: 75.4 us -> 72.5 us (0.962)
  waiting for transfers between devices: 14.4 us -> 11.7 us
    ppermute x1, waiting for transfers between devices: 5.76 us -> 4.44 us  [local(): gxr = lax.ppermute(edges, 'gx', SWAP)]
    ppermute x1, waiting for transfers between devices: 5.28 us -> 4.21 us  [ring(): lax.ppermute(value, 'gz', [(i, (i + step) % count) for i in range(count)])]
    ppermute x7 -> x9, waiting for transfers between devices: 3.32 us -> 2.49 us  [swap(): return lax.ppermute(value, 'gy', SWAP)]
    ppermute x4 -> x5, starting transfers between devices: 24.6 us -> 24 us  [role_shift(): return lax.ppermute(value, ('gx', 'gy', 'gz'), pairs)]
    ppermute x7 -> x9, starting transfers between devices: 8.54 us -> 8.42 us  [swap(): return lax.ppermute(value, 'gy', SWAP)]
  transfers between devices with their start and end apart: 13 -> 17, of which waited for: 5 -> 6; matrix products, arithmetic and copies ran while one was open for 0% -> 0% of each run, Pallas kernels for 5% -> 5%
where the time goes in v6:
time: 72.5 us; the launch traced here: 72.3 us
  starting transfers between devices  33.7 us (46%)
  blocking collectives  15.5 us (21%)
  waiting for transfers between devices  11.7 us (16%)
  Pallas kernels  10.7 us (15%)
    ppermute x5, starting transfers between devices, role_shift(): return lax.ppermute(value, ('gx', 'gy', 'gz'), pairs)  24 us
    all_to_all x1, blocking collectives, local(): lax.all_to_all(sums.reshape(PARTNERS, 1, SLOTS), ('gx', 'gz'), 0, 0)  15.5 us
    pallas_call x7, Pallas kernels, call(): pl.pallas_call(kernel, out_shape=outs, in_specs=[SM] * smem + [VM] * (len...  9.52 us
    ppermute x9, starting transfers between devices, swap(): return lax.ppermute(value, 'gy', SWAP)  8.42 us
    ppermute x1, waiting for transfers between devices, local(): gxr = lax.ppermute(edges, 'gx', SWAP)  4.44 us
    ppermute x1, waiting for transfers between devices, ring(): lax.ppermute(value, 'gz', [(i, (i + step) % count) for i in range(count)])  4.21 us
    ppermute x9, waiting for transfers between devices, swap(): return lax.ppermute(value, 'gy', SWAP)  2.49 us
  transfers between devices with their start and end apart: 17, of which 6 were waited for; matrix products, arithmetic and copies ran while one was open for 0% of the time, Pallas kernels for 5%

profile of v6, /device:TPU:1, one launch (start us, length us, event | category | flops | bytes accessed | tf_op | source)
XLA Modules:
  0.0 72.3 jit_solution(9356464737090194803)
XLA Ops:
  0.6 1.2 %load.1 = (f32[32,32,128]{2,1,0:T(8,128)S(1)}, f32[120,128]{1,0:T(8,128)S(1)}, f32[4]{0:T(128)S(1)}, f32[7,32,128]{2,1,0:T(8,128)S(1)}) custom-call(f32[3,4,32,128]{3,2,1,0:T(8,128)} %vel.1, f32[4,32,128]{2,1,0:T(8,128)} %ph.1, f32[4,32,128]{2,1,0:T(8,128)} %po.1, f32[3,4,32,128]{3,2,1,0:T(8,128)} %vo.1, f32[4]{0:T(128)} %coefs.1), custom_call_target="tpu_custom_call" | custom-call | tf_op jit(solution)/shard_map/load/pallas_call | solution.py:603
  1.8 3.3 %collective-permute-start.2 = (f32[7,32,128]{2,1,0:T(8,128)S(1)}, f32[7,32,128]{2,1,0:T(8,128)S(1)}, u32[]{:S(2)}, u32[]{:S(2)}) collective-permute-start(f32[7,32,128]{2,1,0:T(8,128)S(1)} %get-tuple-element.58), channel_id=1, source_target_pairs={{0,64},{64,0},{1,65},{65,1},{2,66},{66,2},{3,67},{67,3},{4,68},{68... | collective-permute-start | bytes 344072 | tf_op jit(solution)/shard_map/ppermute | solution.py:585
  5.3 0.9 %collective-permute-done.2.got = f32[7,32,128]{2,1,0:T(8,128)S(1)} collective-permute-done((f32[7,32,128]{2,1,0:T(8,128)S(1)}, f32[7,32,128]{2,1,0:T(8,128)S(1)}, u32[]{:S(2)}, u32[]{:S(2)}) %collective-permute-start.2) | collective-permute-done | bytes 114720 | tf_op jit(solution)/shard_map/ppermute | solution.py:585
  6.1 9.0 %collective-permute-start.3 = (f32[7,32,256]{2,1,0:T(8,128)S(1)}, f32[7,32,256]{2,1,0:T(8,128)S(1)}, u32[]{:S(2)}, u32[]{:S(2)}) collective-permute-start(f32[7,32,256]{2,1,0:T(8,128)S(1)} %get-tuple-element.59), channel_id=1, source_target_pairs={{0,1},{1,2},{2,3},{3,4},{4,5},{5,6},{6,7},{7,8},{8,9},{9,10},{10,1... | collective-permute-start | bytes 688136 | tf_op jit(solution)/shard_map/ppermute | solution.py:576
  15.2 0.7 %collective-permute-start.1 = (f32[120,128]{1,0:T(8,128)S(1)}, f32[120,128]{1,0:T(8,128)S(1)}, u32[]{:S(2)}, u32[]{:S(2)}) collective-permute-start(f32[120,128]{1,0:T(8,128)S(1)} %get-tuple-element.57), channel_id=1, source_target_pairs={{0,128},{128,0},{1,129},{129,1},{2,130},{130,2},{3,131},{131,3},{4... | collective-permute-start | bytes 184328 | tf_op jit(solution)/shard_map/ppermute | solution.py:613
  16.0 4.4 %collective-permute-done.1.gxr = f32[120,128]{1,0:T(8,128)S(1)} collective-permute-done((f32[120,128]{1,0:T(8,128)S(1)}, f32[120,128]{1,0:T(8,128)S(1)}, u32[]{:S(2)}, u32[]{:S(2)}) %collective-permute-start.1) | collective-permute-done | bytes 61472 | tf_op jit(solution)/shard_map/ppermute | solution.py:613
  20.4 0.5 collective-permute-done.4.dr
  20.9 1.1 %collective-permute-start.6 = (f32[7,32,256]{2,1,0:T(8,128)S(1)}, f32[7,32,256]{2,1,0:T(8,128)S(1)}, u32[]{:S(2)}, u32[]{:S(2)}) collective-permute-start(f32[7,32,256]{2,1,0:T(8,128)S(1)} %collective-permute-done.3.mr), channel_id=1, source_target_pairs={{0,64},{64,0},{1,65},{65,1},{2,66},{66,2},{3,67},{67,3},{4,68},{68... | collective-permute-start | bytes 688136 | tf_op jit(solution)/shard_map/ppermute | solution.py:585
  22.0 0.5 collective-permute-start.7
  22.5 0.7 %collective-permute-done.5.gxs = f32[120,128]{1,0:T(8,128)S(1)} collective-permute-done((f32[120,128]{1,0:T(8,128)S(1)}, f32[120,128]{1,0:T(8,128)S(1)}, u32[]{:S(2)}, u32[]{:S(2)}) %collective-permute-start.5) | collective-permute-done | bytes 61472 | tf_op jit(solution)/shard_map/ppermute | solution.py:585
  23.4 2.1 %first.1 = (f32[46,48,256]{2,1,0:T(8,128)S(1)}, f32[4,48,256]{2,1,0:T(8,128)S(1)}, f32[4,48,256]{2,1,0:T(8,128)S(1)}, f32[3,6,48,256]{3,2,1,0:T(8,128)S(1)}, f32...) custom-call(f32[4]{0:T(128)S(1)} %get-tuple-element.55.coefs, ...), custom_call_target="tpu_custom_call", output_to_operand_aliasing={{0}: (1, {})} | custom-call | tf_op jit(solution)/shard_map/first/pallas_call | solution.py:589
  25.4 7.4 %collective-permute-start.8 = (f32[192,256]{1,0:T(8,128)S(1)}, f32[192,256]{1,0:T(8,128)S(1)}, u32[]{:S(2)}, u32[]{:S(2)}) collective-permute-start(f32[192,256]{1,0:T(8,128)S(1)} %get-tuple-element.66), channel_id=1, source_target_pairs={{0,1},{1,2},{2,3},{3,4},{4,5},{5,6},{6,7},{7,8},{8,9},{9,10},{10,1... | collective-permute-start | bytes 589832 | tf_op jit(solution)/shard_map/ppermute | solution.py:576
  32.8 0.5 collective-permute-start.10
  33.3 1.6 %weights.1 = (f32[4,48,256]{2,1,0:T(8,128)S(1)}, f32[3,4,32,256]{3,2,1,0:T(8,128)S(1)}, f32[5,8,128]{2,1,0:T(8,128)S(1)}, f32[2,4,40,256]{3,2,1,0:T(8,128)S(1)},...) custom-call(f32[4]{0:T(128)S(1)} %get-tuple-element.55.coefs, f32[46,48,256]{2,1,0:T(8,128)S(1)} %get-tuple-element.70.e, ...), custom_call_target="tpu_custom_call" | custom-call | tf_op jit(solution)/shard_map/weights/pallas_call | solution.py:589
  34.9 4.2 %collective-permute-done.11.far = f32[32,256]{1,0:T(8,128)S(1)} collective-permute-done((f32[32,256]{1,0:T(8,128)S(1)}, f32[32,256]{1,0:T(8,128)S(1)}, u32[]{:S(2)}, u32[]{:S(2)}) %collective-permute-start.11) | collective-permute-done | bytes 32800 | tf_op jit(solution)/shard_map/ppermute | solution.py:581
  39.1 1.7 %collective-permute-start.12 = (f32[192,256]{1,0:T(8,128)S(1)}, f32[192,256]{1,0:T(8,128)S(1)}, u32[]{:S(2)}, u32[]{:S(2)}) collective-permute-start(f32[192,256]{1,0:T(8,128)S(1)} %collective-permute-done.8.r), channel_id=1, source_target_pairs={{0,64},{64,0},{1,65},{65,1},{2,66},{66,2},{3,67},{67,3},{4,68},{68... | collective-permute-start | bytes 589832 | tf_op jit(solution)/shard_map/ppermute | solution.py:585
  40.9 0.4 collective-permute-start.13
  41.4 0.9 %collective-permute-done.13.ds = f32[34,256]{1,0:T(8,128)S(1)} collective-permute-done((f32[34,256]{1,0:T(8,128)S(1)}, f32[34,256]{1,0:T(8,128)S(1)}, u32[]{:S(2)}, u32[]{:S(2)}) %collective-permute-start.13) | collective-permute-done | bytes 34848 | tf_op jit(solution)/shard_map/ppermute | solution.py:585
  42.2 2.0 %moments.1 = (f32[128,64]{1,0:T(8,128)S(1)}, f32[13,48,256]{2,1,0:T(8,128)S(1)}, f32[8,48,256]{2,1,0:T(8,128)S(1)}, f32[9,48,256]{2,1,0:T(8,128)S(1)}, f32[7,48,...) custom-call(f32[4,48,256]{2,1,0:T(8,128)S(1)} %get-tuple-element.64., ...), custom_call_target="tpu_custom_call" | custom-call | tf_op jit(solution)/shard_map/moments/pallas_call | solution.py:589
  44.2 7.5 %collective-permute-start.15 = (f32[8,40,256]{2,1,0:T(8,128)S(1)}, f32[8,40,256]{2,1,0:T(8,128)S(1)}, u32[]{:S(2)}, u32[]{:S(2)}) collective-permute-start(f32[8,40,256]{2,1,0:T(8,128)S(1)} %get-tuple-element.86), channel_id=1, source_target_pairs={{0,1},{1,2},{2,3},{3,4},{4,5},{5,6},{6,7},{7,8},{8,9},{9,10},{10,1... | collective-permute-start | bytes 983048 | tf_op jit(solution)/shard_map/ppermute | solution.py:576
  51.7 15.5 %all_to_all.5 = f32[128,1,64]{2,1,0:T(1,128)S(1)} all-to-all(f32[128,1,64]{2,1,0:T(1,128)S(1)} %bitcast.5), channel_id=1, replica_groups=mesh['gx'=2,'gy'=2,'gz'=64] {'gx','gz'}, dimensions={0} | all-to-all | bytes 65536 | tf_op jit(solution)/shard_map/all_to_all | solution.py:663
  67.3 1.2 %collective-permute-start.16 = (f32[8,40,256]{2,1,0:T(8,128)S(1)}, f32[8,40,256]{2,1,0:T(8,128)S(1)}, u32[]{:S(2)}, u32[]{:S(2)}) collective-permute-start(f32[8,40,256]{2,1,0:T(8,128)S(1)} %collective-permute-done.15.ri), channel_id=1, source_target_pairs={{0,64},{64,0},{1,65},{65,1},{2,66},{66,2},{3,67},{67,3},{4,68},{68... | collective-permute-start | bytes 983048 | tf_op jit(solution)/shard_map/ppermute | solution.py:585
  68.5 1.9 %near.1 = (f32[4]{0:T(128)}, f32[8,128]{1,0:T(8,128)S(1)}, f32[4,48,256]{2,1,0:T(8,128)S(1)}, f32[4,2,48,256]{3,2,1,0:T(8,128)S(1)}, f32[4,2,32,128]{3,2,1,0:T(8,128)S(1)}) custom-call(f32[4]{0:T(128)S(1)} %get-tuple-element.55.coefs, f32[128,64]{1,0:T(8,128)S(1)} %bitcast.4, f32[8,48,256]{2,1,0:T(8,128)S(1)} %get-tuple-element.89.uu, ...), custom_call_target="tpu_custom_call" | custom-call | tf_op jit(solution)/shard_map/near/pallas_call | solution.py:589
  70.5 1.8 %far.1 = (f32[4,32,128]{2,1,0:T(8,128)}, f32[3,4,32,128]{3,2,1,0:T(8,128)}) custom-call(f32[4]{0:T(128)S(1)} %get-tuple-element.55.coefs, f32[8,128]{1,0:T(8,128)S(1)} %get-tuple-element.100.table, f32[8,48,256]{2,1,0:T(8,128)S(1)} %get-tuple-element.89.uu, f32[9,48,256]{2,1,0:T(8,128)S(1)} %get-tuple-element.90.f, f32[7,48,256]{2,1,0:T(8,128)S(1)} %get-tuple-element.91.af, ...), custom_call_target="tpu_custom_call" | custom-call | tf_op jit(solution)/shard_map/far/pallas_call | solution.py:589
  (19 shorter events, 0.4 us)
Async XLA Ops:
  1.8 4.3 %collective-permute-start.2 = (f32[7,32,128]{2,1,0:T(8,128)S(1)}, f32[7,32,128]{2,1,0:T(8,128)S(1)}, u32[]{:S(2)}, u32[]{:S(2)}) collective-permute-start(f32[7,32,128]{2,1,0:T(8,128)S(1)} %get-tuple-element.58), channel_id=1, source_target_pairs={{0,64},{64,0},{1,65},{65,1},{2,66},{66,2},{3,67},{67,3},{4,68},{68... | collective-permute-start | bytes 344072 | tf_op jit(solution)/shard_map/ppermute | solution.py:585
  5.2 18.1 %collective-permute-start = (f32[32,32,128]{2,1,0:T(8,128)S(1)}, f32[32,32,128]{2,1,0:T(8,128)S(1)}, u32[]{:S(2)}, u32[]{:S(2)}) collective-permute-start(f32[32,32,128]{2,1,0:T(8,128)S(1)} %get-tuple-element.56.stack), channel_id=1, source_target_pairs={{0,64},{64,0},{1,65},{65,1},{2,66},{66,2},{3,67},{67,3},{4,68},{68... | collective-permute-start | bytes 1572872 | tf_op jit(solution)/shard_map/ppermute | solution.py:585
  6.1 14.8 %collective-permute-start.3 = (f32[7,32,256]{2,1,0:T(8,128)S(1)}, f32[7,32,256]{2,1,0:T(8,128)S(1)}, u32[]{:S(2)}, u32[]{:S(2)}) collective-permute-start(f32[7,32,256]{2,1,0:T(8,128)S(1)} %get-tuple-element.59), channel_id=1, source_target_pairs={{0,1},{1,2},{2,3},{3,4},{4,5},{5,6},{6,7},{7,8},{8,9},{9,10},{10,1... | collective-permute-start | bytes 688136 | tf_op jit(solution)/shard_map/ppermute | solution.py:576
  15.2 5.3 %collective-permute-start.1 = (f32[120,128]{1,0:T(8,128)S(1)}, f32[120,128]{1,0:T(8,128)S(1)}, u32[]{:S(2)}, u32[]{:S(2)}) collective-permute-start(f32[120,128]{1,0:T(8,128)S(1)} %get-tuple-element.57), channel_id=1, source_target_pairs={{0,128},{128,0},{1,129},{129,1},{2,130},{130,2},{3,131},{131,3},{4... | collective-permute-start | bytes 184328 | tf_op jit(solution)/shard_map/ppermute | solution.py:613
  15.9 5.0 %collective-permute-start.4 = (f32[16,256]{1,0:T(8,128)S(1)}, f32[16,256]{1,0:T(8,128)S(1)}, u32[]{:S(2)}, u32[]{:S(2)}) collective-permute-start(f32[16,256]{1,0:T(8,128)S(1)} %get-tuple-element.60), channel_id=1, source_target_pairs={{0,129},{1,130},{2,131},{3,132},{4,133},{5,134},{6,135},{7,136},{8... | collective-permute-start | bytes 49160 | tf_op jit(solution)/shard_map/ppermute | solution.py:576
  20.9 2.4 %collective-permute-start.6 = (f32[7,32,256]{2,1,0:T(8,128)S(1)}, f32[7,32,256]{2,1,0:T(8,128)S(1)}, u32[]{:S(2)}, u32[]{:S(2)}) collective-permute-start(f32[7,32,256]{2,1,0:T(8,128)S(1)} %collective-permute-done.3.mr), channel_id=1, source_target_pairs={{0,64},{64,0},{1,65},{65,1},{2,66},{66,2},{3,67},{67,3},{4,68},{68... | collective-permute-start | bytes 688136 | tf_op jit(solution)/shard_map/ppermute | solution.py:585
  22.0 1.2 %collective-permute-start.5 = (f32[120,128]{1,0:T(8,128)S(1)}, f32[120,128]{1,0:T(8,128)S(1)}, u32[]{:S(2)}, u32[]{:S(2)}) collective-permute-start(f32[120,128]{1,0:T(8,128)S(1)} %collective-permute-done.1.gxr), channel_id=1, source_target_pairs={{0,64},{64,0},{1,65},{65,1},{2,66},{66,2},{3,67},{67,3},{4,68},{68... | collective-permute-start | bytes 184328 | tf_op jit(solution)/shard_map/ppermute | solution.py:585
  22.0 1.4 %collective-permute-start.7 = (f32[16,256]{1,0:T(8,128)S(1)}, f32[16,256]{1,0:T(8,128)S(1)}, u32[]{:S(2)}, u32[]{:S(2)}) collective-permute-start(f32[16,256]{1,0:T(8,128)S(1)} %collective-permute-done.4.dr), channel_id=1, source_target_pairs={{0,64},{64,0},{1,65},{65,1},{2,66},{66,2},{3,67},{67,3},{4,68},{68... | collective-permute-start | bytes 49160 | tf_op jit(solution)/shard_map/ppermute | solution.py:585
  25.4 13.7 %collective-permute-start.8 = (f32[192,256]{1,0:T(8,128)S(1)}, f32[192,256]{1,0:T(8,128)S(1)}, u32[]{:S(2)}, u32[]{:S(2)}) collective-permute-start(f32[192,256]{1,0:T(8,128)S(1)} %get-tuple-element.66), channel_id=1, source_target_pairs={{0,1},{1,2},{2,3},{3,4},{4,5},{5,6},{6,7},{7,8},{8,9},{9,10},{10,1... | collective-permute-start | bytes 589832 | tf_op jit(solution)/shard_map/ppermute | solution.py:576
  32.8 6.3 %collective-permute-start.10 = (f32[72,128]{1,0:T(8,128)S(1)}, f32[72,128]{1,0:T(8,128)S(1)}, u32[]{:S(2)}, u32[]{:S(2)}) collective-permute-start(f32[72,128]{1,0:T(8,128)S(1)} %get-tuple-element.68), channel_id=1, source_target_pairs={{0,128},{128,0},{1,129},{129,1},{2,130},{130,2},{3,131},{131,3},{4... | collective-permute-start | bytes 110600 | tf_op jit(solution)/shard_map/ppermute | solution.py:641
  33.3 5.8 %collective-permute-start.9 = (f32[34,256]{1,0:T(8,128)S(1)}, f32[34,256]{1,0:T(8,128)S(1)}, u32[]{:S(2)}, u32[]{:S(2)}) collective-permute-start(f32[34,256]{1,0:T(8,128)S(1)} %get-tuple-element.67), channel_id=1, source_target_pairs={{0,129},{1,130},{2,131},{3,132},{4,133},{5,134},{6,135},{7,136},{8... | collective-permute-start | bytes 104456 | tf_op jit(solution)/shard_map/ppermute | solution.py:576
  33.3 5.8 %collective-permute-start.11 = (f32[32,256]{1,0:T(8,128)S(1)}, f32[32,256]{1,0:T(8,128)S(1)}, u32[]{:S(2)}, u32[]{:S(2)}) collective-permute-start(f32[32,256]{1,0:T(8,128)S(1)} %get-tuple-element.69), channel_id=1, source_target_pairs={{0,62},{1,63},{2,0},{3,1},{4,2},{5,3},{6,4},{7,5},{8,6},{9,7},{10,... | collective-permute-start | bytes 98312 | tf_op jit(solution)/shard_map/ppermute | solution.py:581
  39.1 3.1 %collective-permute-start.12 = (f32[192,256]{1,0:T(8,128)S(1)}, f32[192,256]{1,0:T(8,128)S(1)}, u32[]{:S(2)}, u32[]{:S(2)}) collective-permute-start(f32[192,256]{1,0:T(8,128)S(1)} %collective-permute-done.8.r), channel_id=1, source_target_pairs={{0,64},{64,0},{1,65},{65,1},{2,66},{66,2},{3,67},{67,3},{4,68},{68... | collective-permute-start | bytes 589832 | tf_op jit(solution)/shard_map/ppermute | solution.py:585
  40.8 1.4 %collective-permute-start.14 = (f32[72,128]{1,0:T(8,128)S(1)}, f32[72,128]{1,0:T(8,128)S(1)}, u32[]{:S(2)}, u32[]{:S(2)}) collective-permute-start(f32[72,128]{1,0:T(8,128)S(1)} %collective-permute-done.10.x), channel_id=1, source_target_pairs={{0,64},{64,0},{1,65},{65,1},{2,66},{66,2},{3,67},{67,3},{4,68},{68... | collective-permute-start | bytes 110600 | tf_op jit(solution)/shard_map/ppermute | solution.py:585
  40.9 1.3 %collective-permute-start.13 = (f32[34,256]{1,0:T(8,128)S(1)}, f32[34,256]{1,0:T(8,128)S(1)}, u32[]{:S(2)}, u32[]{:S(2)}) collective-permute-start(f32[34,256]{1,0:T(8,128)S(1)} %collective-permute-done.9.d), channel_id=1, source_target_pairs={{0,64},{64,0},{1,65},{65,1},{2,66},{66,2},{3,67},{67,3},{4,68},{68... | collective-permute-start | bytes 104456 | tf_op jit(solution)/shard_map/ppermute | solution.py:585
  44.2 23.1 %collective-permute-start.15 = (f32[8,40,256]{2,1,0:T(8,128)S(1)}, f32[8,40,256]{2,1,0:T(8,128)S(1)}, u32[]{:S(2)}, u32[]{:S(2)}) collective-permute-start(f32[8,40,256]{2,1,0:T(8,128)S(1)} %get-tuple-element.86), channel_id=1, source_target_pairs={{0,1},{1,2},{2,3},{3,4},{4,5},{5,6},{6,7},{7,8},{8,9},{9,10},{10,1... | collective-permute-start | bytes 983048 | tf_op jit(solution)/shard_map/ppermute | solution.py:576
  67.3 3.2 %collective-permute-start.16 = (f32[8,40,256]{2,1,0:T(8,128)S(1)}, f32[8,40,256]{2,1,0:T(8,128)S(1)}, u32[]{:S(2)}, u32[]{:S(2)}) collective-permute-start(f32[8,40,256]{2,1,0:T(8,128)S(1)} %collective-permute-done.15.ri), channel_id=1, source_target_pairs={{0,64},{64,0},{1,65},{65,1},{2,66},{66,2},{3,67},{67,3},{4,68},{68... | collective-permute-start | bytes 983048 | tf_op jit(solution)/shard_map/ppermute | solution.py:585

commit v7 on v6

--- a/solution.py
+++ b/solution.py
@@ -32,6 +32,9 @@
 AGAIN_ROWS = 2 * sum(w for _, _, w in AGAIN)
 RIM = [("b", z, 6) for z in range(CZ)] + [("u", z, 3) for z in range(CZ)]
 RIM_ROWS = 2 * sum(w for _, _, w in RIM)
+THIRD = (CX, CX, CX + 2, CX, CX + 2, CX, CX, CX)
+THIRD_AT = [sum(THIRD[:n]) for n in range(8)]
+THIRD_ROWS = -(-sum(THIRD) // 8) * 8
 NUM_SUMS = 45
 SLOTS = 64
 
@@ -139,7 +142,25 @@
             row += 2 * w
 
 
-def first_kernel(coefs, inner, mr, ms, dr, ds, e, b, u, q, pot, lph, g, lv, send, corner, rim, far, p0):
+def at(e, field, z):
+    return e[BASE[field] + HALO[field] + z]
+
+
+def middle(a):
+    return a[HX : HX + CX]
+
+
+def provisional(e, field, z, grad, here, tension, viscosity):
+    a = at(e, field, z)
+    zu, zd = at(e, field, z + 1), at(e, field, z - 1)
+    xu, xd, yu, yd = x_up(a), x_dn(a), y_up(a), y_dn(a)
+    lap = (zu + zd) + (xu + xd) + (yu + yd) - 6.0 * a
+    advect = at(e, V0, z) * (zu - zd) + at(e, V1, z) * (xu - xd) + at(e, V2, z) * (yu - yd)
+    value = a - (0.5 * DT) * advect + (DT * viscosity) * lap + (DT * tension) * (here * grad)
+    return value, lap
+
+
+def first_kernel(coefs, inner, mr, ms, dr, ds, e, b, u, send, corner, rim, far, pot, p0):
     tension = 0.5 * coefs[1]
     viscosity = 0.1 * coefs[2]
     interface = 0.5 * coefs[3]
@@ -160,71 +181,46 @@
             e[layer, HX + CX : HX + CX + w] = part[w:]
         row += 2 * w
 
-    def at(field, z):
-        return e[BASE[field] + HALO[field] + z]
-
     def potential(t):
         z = t - 1
-        a = at(PH, z)
-        lap = lap_of(a, at(PH, z + 1), at(PH, z - 1))
-        lph[t] = lap
-        pot[t] = a * a * a - a - interface * lap
+        a = at(e, PH, z)
+        pot[t] = a * a * a - a - interface * lap_of(a, at(e, PH, z + 1), at(e, PH, z - 1))
 
     loop(6, potential)
-
-    def provisional(field, z, grad, here):
-        a = at(field, z)
-        zu, zd = at(field, z + 1), at(field, z - 1)
-        xu, xd, yu, yd = x_up(a), x_dn(a), y_up(a), y_dn(a)
-        lap = (zu + zd) + (xu + xd) + (yu + yd) - 6.0 * a
-        advect = at(V0, z) * (zu - zd) + at(V1, z) * (xu - xd) + at(V2, z) * (yu - yd)
-        value = a - (0.5 * DT) * advect + (DT * viscosity) * lap + (DT * tension) * (here * grad)
-        return value, lap
 
     def along(t):
         z = t - 1
-        grad = 0.5 * (at(PH, z + 1) - at(PH, z - 1))
-        p0[t], lv[0, t] = provisional(V0, z, grad, pot[t])
+        grad = 0.5 * (at(e, PH, z + 1) - at(e, PH, z - 1))
+        value, _ = provisional(e, V0, z, grad, pot[t], tension, viscosity)
+        p0[t] = middle(value)
 
     loop(6, along)
 
-    def slopes(t):
-        z = t - 1
-        a = at(PH, z)
-        g[0, t] = 0.5 * (at(PH, z + 1) - at(PH, z - 1))
-        g[1, t] = dx(a)
-        g[2, t] = dy(a)
-        q[0, t] = p0[t] - at(O0, z)
-
-    loop(6, slopes)
-
     def across(z):
-        here = pot[z + 1]
-        p1, lv[1, z] = provisional(V1, z, g[1, z + 1], here)
-        p2, lv[2, z] = provisional(V2, z, g[2, z + 1], here)
-        b[z] = -(0.5 * (p0[z + 2] - p0[z]) + dx(p1) + dy(p2))
-        q1 = p1 - at(O1, z)
-        q2 = p2 - at(O2, z)
-        q[1, z + 1] = q1
-        q[2, z + 1] = q2
-        u[z] = 0.5 * (q[0, z + 2] - q[0, z]) + dx(q1) + dy(q2)
+        phase = at(e, PH, z)
+        p1, _ = provisional(e, V1, z, dx(phase), pot[z + 1], tension, viscosity)
+        p2, _ = provisional(e, V2, z, dy(phase), pot[z + 1], tension, viscosity)
+        div = 0.5 * (p0[z + 2] - p0[z]) + middle(dx(p1) + dy(p2))
+        b[z] = -div
+        seen = 0.5 * middle(at(e, O0, z + 1) - at(e, O0, z - 1)) + middle(dx(at(e, O1, z)) + dy(at(e, O2, z)))
+        u[z] = div - seen
 
     loop(4, across)
 
     row = 0
     for n, (name, k, w) in enumerate(AGAIN):
         src = (b if name == "b" else u)[outgoing(c, k)]
-        send[CX * n : CX * (n + 1)] = src[HX : HX + CX]
-        corner[row : row + w] = src[HX + CX - w : HX + CX]
-        corner[row + w : row + 2 * w] = src[HX : HX + w]
+        send[CX * n : CX * (n + 1)] = src
+        corner[row : row + w] = src[CX - w :]
+        corner[row + w : row + 2 * w] = src[:w]
         row += 2 * w
     row = 0
     for name, z, w in RIM:
         field = b if name == "b" else u
-        rim[row : row + w] = field[z, HX + CX - w : HX + CX, :CY]
-        rim[row + w : row + 2 * w] = field[z, HX : HX + w, :CY]
+        rim[row : row + w] = field[z, CX - w :, :CY]
+        rim[row + w : row + 2 * w] = field[z, :w, :CY]
         row += 2 * w
-    far[...] = b[0, HX : HX + CX]
+    far[...] = b[0]
 
 
 def folded(a):
@@ -232,16 +228,32 @@
     return (a[0:8] + a[8:16]) + (a[16:24] + a[24:32])
 
 
-def middle(a):
-    return a[HX : HX + CX]
-
-
-def weight_kernel(coefs, e, q, pot, lph, g, lv, adj, w, part, edge, gv, base):
-    mobility = 0.1 * coefs[0]
-
-    def at(field, z):
-        return e[BASE[field] + HALO[field] + z]
-
+def weight_kernel(coefs, e, adj, w, part, edge, gv, base, pot, g, q, lph, lv, p0):
+    mobility, tension, viscosity, interface = constants(coefs)
+
+    def forward(t):
+        z = t - 1
+        a = at(e, PH, z)
+        lap = lap_of(a, at(e, PH, z + 1), at(e, PH, z - 1))
+        lph[t] = lap
+        here = a * a * a - a - interface * lap
+        pot[t] = here
+        g[0, t] = 0.5 * (at(e, PH, z + 1) - at(e, PH, z - 1))
+        g[1, t] = dx(a)
+        g[2, t] = dy(a)
+        value, lv[0, t] = provisional(e, V0, z, g[0, t], here, tension, viscosity)
+        q[0, t] = value - at(e, O0, z)
+
+    loop(6, forward)
+
+    def across(z):
+        here = pot[z + 1]
+        p1, lv[1, z] = provisional(e, V1, z, g[1, z + 1], here, tension, viscosity)
+        p2, lv[2, z] = provisional(e, V2, z, g[2, z + 1], here, tension, viscosity)
+        q[1, z + 1] = p1 - at(e, O1, z)
+        q[2, z + 1] = p2 - at(e, O2, z)
+
+    loop(4, across)
     sums = [jnp.zeros((8, CY), jnp.float32)] * 5
     for t in range(CZ):
         here = pot[t + 1]
@@ -257,14 +269,14 @@
         w[2, t] = middle(w3)
         lap_pot = lap_of(here, pot[t + 2], pot[t])
         lap_lap = lap_of(lap, lph[t + 2], lph[t])
-        flow = at(V0, t) * gs[0] + at(V1, t) * gs[1] + at(V2, t) * gs[2]
-        c = at(PH, t) - DT * flow + (DT * mobility) * lap_pot - at(PO, t)
+        flow = at(e, V0, t) * gs[0] + at(e, V1, t) * gs[1] + at(e, V2, t) * gs[2]
+        c = at(e, PH, t) - DT * flow + (DT * mobility) * lap_pot - at(e, PO, t)
         adj[t] = c
-        v1, v2 = at(V1, t), at(V2, t)
+        v1, v2 = at(e, V1, t), at(e, V2, t)
         base[t] = own(c + DT * (dx(v1 * c) + dy(v2 * c)))
         for i, field in enumerate((V0, V1, V2)):
-            a = at(field, t)
-            gv[0, i, t] = own(0.5 * (at(field, t + 1) - at(field, t - 1)))
+            a = at(e, field, t)
+            gv[0, i, t] = own(0.5 * (at(e, field, t + 1) - at(e, field, t - 1)))
             gv[1, i, t] = own(dx(a))
             gv[2, i, t] = own(dy(a))
         qs = [q[i, t + 1] for i in range(3)]
@@ -274,22 +286,22 @@
         sums = [s + folded(a) for s, a in zip(sums, terms)]
     for k in range(5):
         part[k] = sums[k]
-    for k, z in ((0, CZ - 1), (1, 0)):
-        edge[k, 0] = q[1, z + 1, NEAR : ROWS - NEAR]
-        edge[k, 1] = q[2, z + 1, NEAR : ROWS - NEAR]
-        for j in range(2):
-            edge[k, 2 + j] = adj[2 * (1 - k) + j, NEAR : ROWS - NEAR]
+    c = lax.axis_index("gy")
+    pieces = (q[1, 1 + outgoing(c, 1)], q[2, 1 + outgoing(c, 1)], adj[outgoing(c, 1)], adj[outgoing(c, 2)])
+    for n, src in enumerate(pieces):
+        w = (THIRD[n] - CX) // 2
+        edge[THIRD_AT[n] : THIRD_AT[n] + THIRD[n]] = src[HX - w : HX + CX + w]
 
 
 def shifted(c, zu, zd):
     return (6.0 + SHIFT) * c - ((zu + zd) + (x_up(c) + x_dn(c)) + (y_up(c) + y_dn(c)))
 
 
-def moment_kernel(b4, u4, r, s, d, ds, x, xs, far, w, part, edge, out, bb, uu, f, af, a2f, ab, au, send, a2b, a2u):
+def moment_kernel(b4, u4, r, s, d, ds, x, xs, far, fars, w, part, edge, out, bb, uu, f, af, a2f, ab, au, send, a2b, a2u):
     c = lax.axis_index("gy")
     near = pl.ds(NEAR, NARROW)
-    bb[4:8] = b4[...]
-    uu[2:6] = u4[...]
+    bb[4:8, HX : HX + CX] = b4[...]
+    uu[2:6, HX : HX + CX] = u4[...]
     row = 0
     for n, (name, k, width) in enumerate(AGAIN):
         dst, below = (bb, 4 - k) if name == "b" else (uu, 2 - k)
@@ -310,7 +322,7 @@
             dst[layer, HX - width : HX, lanes] = src[row : row + width]
             dst[layer, HX + CX : HX + CX + width, lanes] = src[row + width : row + 2 * width]
         row += 2 * width
-    bb[12, HX : HX + CX] = far[...]
+    bb[12, HX : HX + CX] = jnp.where(c == 1, far[...], other_first(fars[...]))
 
     def wide(t):
         a = bb[t + 2]
@@ -362,12 +374,11 @@
     which = lax.broadcasted_iota(jnp.int32, (48, SLOTS), 0)
     row = jnp.sum(jnp.where(line == which, totals, 0.0), axis=0, keepdims=True)
     out[...] = jnp.broadcast_to(row, (PARTNERS, SLOTS))
-    send[0:4] = edge[c]
-    first = 2 * (1 - c)
-    send[4] = a2f[first, near]
-    send[5] = a2f[first + 1, near]
-    send[6] = af[3 - c, near]
-    send[7] = au[3 - c, near]
+    send[0 : THIRD_AT[4]] = edge[...]
+    pieces = (a2f[outgoing(c, 1)], a2f[outgoing(c, 2)], af[1 + outgoing(c, 2)], au[1 + outgoing(c, 2)])
+    for n, src in enumerate(pieces, 4):
+        w = (THIRD[n] - CX) // 2
+        send[THIRD_AT[n] : THIRD_AT[n] + THIRD[n]] = src[HX - w : HX + CX + w]
 
 
 def steps(m0, m1, m2, m3):
@@ -420,10 +431,11 @@
     uu, f, af, a2f, bb, ab, au = basis
     e, q, adj4, pot, g, gv, base = state
     phi, pr, pa, adj, qe, new = work
-    near = pl.ds(NEAR, NARROW)
+    inside, wider = pl.ds(HX, CX), pl.ds(HX - 1, CX + 2)
     for i in range(2):
-        qe[i, 5 * side, near] = halo(i)
-        adj[6 * side + i, near] = halo(2 + i)
+        qe[i, 5 * side, inside] = halo(i)
+    adj[1 + 5 * side, wider] = halo(2)
+    adj[7 * side, inside] = halo(3)
 
     def mixed(terms):
         value = coef[0] * terms[0]
@@ -432,11 +444,13 @@
         return value
 
     i = 1 + 5 * side
-    phi[i, near] = mixed([
-        uu[i, near], au[i - 1, near], f[i, near], af[i - 1, near], halo(5 - side), bb[i + 2, near], ab[i, near],
+    phi[i, wider] = mixed([
+        uu[i, wider], au[i - 1, wider], f[i, wider], af[i - 1, wider], halo(4), bb[i + 2, wider], ab[i, wider],
     ])
     i = 7 * side
-    phi[i, near] = mixed([uu[i, near], halo(7), f[i, near], halo(6), halo(4 + side), bb[i + 2, near], ab[i, near]])
+    phi[i, inside] = mixed([
+        uu[i, inside], halo(7), f[i, inside], halo(6), halo(5), bb[i + 2, inside], ab[i, inside],
+    ])
 
     def project(t):
         c = phi[t + 1]
@@ -452,15 +466,12 @@
     for t in new:
         project(t)
 
-    def at(field, z):
-        return e[BASE[field] + HALO[field] + z]
-
     for n in range(2):
         t = 2 * side + n
-        v1, v2 = at(V1, t), at(V2, t)
-        v0u, v0d = at(V0, t + 1), at(V0, t - 1)
+        v1, v2 = at(e, V1, t), at(e, V2, t)
+        v0u, v0d = at(e, V0, t + 1), at(e, V0, t - 1)
         here = pot[t + 1]
-        ph = own(at(PH, t))
+        ph = own(at(e, PH, t))
         lam = pa[t + 1]
         up = v0u * adj[t + 3] - tension * (pot[t + 2] * pr[0, t + 2])
         dn = v0d * adj[t + 1] - tension * (pot[t] * pr[0, t])
@@ -504,7 +515,7 @@
 
     new = [2 * side + n for n in range(4)]
     half_step(
-        side, lambda j: ri[j], coef, consts, (uu, f, af, a2f, bb, ab, au), (e, q, adj4, pot, g, gv, base),
+        side, lambda n: ri[THIRD_AT[n] : THIRD_AT[n] + THIRD[n]], coef, consts, (uu, f, af, a2f, bb, ab, au), (e, q, adj4, pot, g, gv, base),
         (phi, pr, pa, adj, qe, new), write,
     )
     for n in range(2):
@@ -538,7 +549,7 @@
 
     new = [4 * side + n for n in range(2)]
     half_step(
-        side, lambda j: other_first(si[j]), coef, consts, (uu, f, af, a2f, bb, ab, au),
+        side, lambda n: other_first(si[THIRD_AT[n] : THIRD_AT[n] + THIRD[n]]), coef, consts, (uu, f, af, a2f, bb, ab, au),
         (e, q, adj4, pot, g, gv, base), (phi, pr, pa, adj, qe, new), write,
     )
     for n in range(2):
@@ -576,9 +587,10 @@
     return lax.ppermute(value, ("gx", "gy", "gz"), pairs)
 
 
-def ring(value, step):
-    count = lax.axis_size("gz")
-    return lax.ppermute(value, "gz", [(i, (i + step) % count) for i in range(count)])
+def second_down(value):
+    gx, gz = lax.axis_size("gx"), lax.axis_size("gz")
+    pairs = [((2 * x + y) * gz + i, (2 * x + y) * gz + (i - 2 * y) % gz) for x in range(gx) for y in range(2) for i in range(gz)]
+    return lax.ppermute(value, ("gx", "gy", "gz"), pairs)
 
 
 def swap(value):
@@ -626,12 +638,12 @@
     inner = call(inner_kernel, layers(TOTAL), (stack, peer, gxr, gxs), [], "inner", 0)
     ms = swap(mr)
     ds = swap(dr)
-    e, b, u, q, pot, lph, g, lv, send, corner, rim, far = call(
+    e, b, u, send, corner, rim, far = call(
         first_kernel,
-        (layers(TOTAL), layers(4), layers(4), layers(3, 6), layers(6), layers(6), layers(3, 6), layers(3, 6),
-         f32(CX * len(AGAIN), LANES), f32(AGAIN_ROWS, LANES), f32(RIM_ROWS, CY), f32(CX, LANES)),
+        (layers(TOTAL), f32(CZ, CX, LANES), f32(CZ, CX, LANES), f32(CX * len(AGAIN), LANES),
+         f32(AGAIN_ROWS, LANES), f32(RIM_ROWS, CY), f32(CX, LANES)),
         (coefs, inner, mr, ms, dr, ds),
-        [scratch(6)],
+        [scratch(6), pltpu.VMEM((6, CX, LANES), jnp.float32)],
         "first",
         1,
         {1: 0},
@@ -639,22 +651,24 @@
     r2 = role_shift(send, False)
     d2 = role_shift(corner, True)
     x2 = lax.ppermute(rim, "gx", SWAP)
-    far = ring(far, -2)
-    adj, w, part, edge, gv, base = call(
+    far = second_down(far)
+    adj, w, part, edge, gv, base, pot, g, q = call(
         weight_kernel,
-        (layers(4), f32(3, CZ, CX, LANES), f32(5, 8, CY), f32(2, 4, NARROW, LANES), f32(3, 3, CZ, CX, CY), f32(CZ, CX, CY)),
-        (coefs, e, q, pot, lph, g, lv),
-        [],
+        (layers(4), f32(3, CZ, CX, LANES), f32(5, 8, CY), f32(THIRD_AT[4], LANES), f32(3, 3, CZ, CX, CY),
+         f32(CZ, CX, CY), layers(6), layers(3, 6), layers(3, 6)),
+        (coefs, e),
+        [scratch(6), scratch(3, 6), scratch(6)],
         "weights",
         1,
     )
     r2, d2, x2, far, w, part, edge = lax.optimization_barrier((r2, d2, x2, far, w, part, edge))
     s2, ds2, xs2 = swap(r2), swap(d2), swap(x2)
+    fars = swap(far)
     sums, bb, uu, f, af, a2f, ab, au, send = call(
         moment_kernel,
         (f32(PARTNERS, SLOTS), layers(13), layers(8), layers(9), layers(7), layers(5), layers(8), layers(6),
-         f32(8, NARROW, LANES)),
-        (b, u, r2, s2, d2, ds2, x2, xs2, far, w, part, edge),
+         f32(THIRD_ROWS, LANES)),
+        (b, u, r2, s2, d2, ds2, x2, xs2, far, fars, w, part, edge),
         [scratch(4), scratch(4)],
         "moments",
         0,

time: 72.5 us -> 71.6 us (0.988)
  waiting for transfers between devices: 11.7 us -> 9.71 us
    ppermute x1, waiting for transfers between devices: 4.21 us -> 2.02 us  [second_down(): return lax.ppermute(value, ('gx', 'gy', 'gz'), pairs)]
    ppermute x1, starting transfers between devices: 0.01 us -> 1.91 us  [second_down(): return lax.ppermute(value, ('gx', 'gy', 'gz'), pairs)]
    ppermute x5, starting transfers between devices: 24 us -> 22.9 us  [role_shift(): return lax.ppermute(value, ('gx', 'gy', 'gz'), pairs)]
    ppermute x9 -> x10, waiting for transfers between devices: 2.49 us -> 2.73 us  [swap(): return lax.ppermute(value, 'gy', SWAP)]
    ppermute x9 -> x10, starting transfers between devices: 8.42 us -> 8.36 us  [swap(): return lax.ppermute(value, 'gy', SWAP)]
  transfers between devices with their start and end apart: 17 -> 18, of which waited for: 6 -> 6; matrix products, arithmetic and copies ran while one was open for 0% -> 0% of each run, Pallas kernels for 5% -> 6%
where the time goes in v7:
time: 71.6 us; the launch traced here: 71.4 us
  starting transfers between devices  34.4 us (48%)
  blocking collectives  15.5 us (22%)
  Pallas kernels  11.1 us (16%)
  waiting for transfers between devices  9.71 us (14%)
    ppermute x5, starting transfers between devices, role_shift(): return lax.ppermute(value, ('gx', 'gy', 'gz'), pairs)  22.9 us
    all_to_all x1, blocking collectives, local(): lax.all_to_all(sums.reshape(PARTNERS, 1, SLOTS), ('gx', 'gz'), 0, 0)  15.5 us
    pallas_call x7, Pallas kernels, call(): pl.pallas_call(kernel, out_shape=outs, in_specs=[SM] * smem + [VM] * (len...  9.91 us
    ppermute x10, starting transfers between devices, swap(): return lax.ppermute(value, 'gy', SWAP)  8.36 us
    ppermute x1, waiting for transfers between devices, local(): gxr = lax.ppermute(edges, 'gx', SWAP)  4.44 us
    ppermute x10, waiting for transfers between devices, swap(): return lax.ppermute(value, 'gy', SWAP)  2.73 us
    ppermute x1, waiting for transfers between devices, second_down(): return lax.ppermute(value, ('gx', 'gy', 'gz'), pairs)  2.02 us
    ppermute x1, starting transfers between devices, second_down(): return lax.ppermute(value, ('gx', 'gy', 'gz'), pairs)  1.91 us
  transfers between devices with their start and end apart: 18, of which 6 were waited for; matrix products, arithmetic and copies ran while one was open for 0% of the time, Pallas kernels for 6%

profile of v7, /device:TPU:1, one launch (start us, length us, event | category | flops | bytes accessed | tf_op | source)
XLA Modules:
  0.0 71.4 jit_solution(5841747488065087987)
XLA Ops:
  0.6 1.2 %load.1 = (f32[32,32,128]{2,1,0:T(8,128)S(1)}, f32[120,128]{1,0:T(8,128)S(1)}, f32[4]{0:T(128)S(1)}, f32[7,32,128]{2,1,0:T(8,128)S(1)}) custom-call(f32[3,4,32,128]{3,2,1,0:T(8,128)} %vel.1, f32[4,32,128]{2,1,0:T(8,128)} %ph.1, f32[4,32,128]{2,1,0:T(8,128)} %po.1, f32[3,4,32,128]{3,2,1,0:T(8,128)} %vo.1, f32[4]{0:T(128)} %coefs.1), custom_call_target="tpu_custom_call" | custom-call | tf_op jit(solution)/shard_map/load/pallas_call | solution.py:615
  1.8 3.3 %collective-permute-start.2 = (f32[7,32,128]{2,1,0:T(8,128)S(1)}, f32[7,32,128]{2,1,0:T(8,128)S(1)}, u32[]{:S(2)}, u32[]{:S(2)}) collective-permute-start(f32[7,32,128]{2,1,0:T(8,128)S(1)} %get-tuple-element.56), channel_id=1, source_target_pairs={{0,64},{64,0},{1,65},{65,1},{2,66},{66,2},{3,67},{67,3},{4,68},{68... | collective-permute-start | bytes 344072 | tf_op jit(solution)/shard_map/ppermute | solution.py:597
  5.3 0.9 %collective-permute-done.2.got = f32[7,32,128]{2,1,0:T(8,128)S(1)} collective-permute-done((f32[7,32,128]{2,1,0:T(8,128)S(1)}, f32[7,32,128]{2,1,0:T(8,128)S(1)}, u32[]{:S(2)}, u32[]{:S(2)}) %collective-permute-start.2) | collective-permute-done | bytes 114720 | tf_op jit(solution)/shard_map/ppermute | solution.py:597
  6.1 9.0 %collective-permute-start.3 = (f32[7,32,256]{2,1,0:T(8,128)S(1)}, f32[7,32,256]{2,1,0:T(8,128)S(1)}, u32[]{:S(2)}, u32[]{:S(2)}) collective-permute-start(f32[7,32,256]{2,1,0:T(8,128)S(1)} %get-tuple-element.57), channel_id=1, source_target_pairs={{0,1},{1,2},{2,3},{3,4},{4,5},{5,6},{6,7},{7,8},{8,9},{9,10},{10,1... | collective-permute-start | bytes 688136 | tf_op jit(solution)/shard_map/ppermute | solution.py:587
  15.2 0.7 %collective-permute-start.1 = (f32[120,128]{1,0:T(8,128)S(1)}, f32[120,128]{1,0:T(8,128)S(1)}, u32[]{:S(2)}, u32[]{:S(2)}) collective-permute-start(f32[120,128]{1,0:T(8,128)S(1)} %get-tuple-element.55), channel_id=1, source_target_pairs={{0,128},{128,0},{1,129},{129,1},{2,130},{130,2},{3,131},{131,3},{4... | collective-permute-start | bytes 184328 | tf_op jit(solution)/shard_map/ppermute | solution.py:625
  16.0 4.4 %collective-permute-done.1.gxr = f32[120,128]{1,0:T(8,128)S(1)} collective-permute-done((f32[120,128]{1,0:T(8,128)S(1)}, f32[120,128]{1,0:T(8,128)S(1)}, u32[]{:S(2)}, u32[]{:S(2)}) %collective-permute-start.1) | collective-permute-done | bytes 61472 | tf_op jit(solution)/shard_map/ppermute | solution.py:625
  20.4 0.5 collective-permute-done.4.dr
  20.9 1.1 %collective-permute-start.6 = (f32[7,32,256]{2,1,0:T(8,128)S(1)}, f32[7,32,256]{2,1,0:T(8,128)S(1)}, u32[]{:S(2)}, u32[]{:S(2)}) collective-permute-start(f32[7,32,256]{2,1,0:T(8,128)S(1)} %collective-permute-done.3.mr), channel_id=1, source_target_pairs={{0,64},{64,0},{1,65},{65,1},{2,66},{66,2},{3,67},{67,3},{4,68},{68... | collective-permute-start | bytes 688136 | tf_op jit(solution)/shard_map/ppermute | solution.py:597
  22.0 0.5 collective-permute-start.7
  22.5 0.7 %collective-permute-done.5.gxs = f32[120,128]{1,0:T(8,128)S(1)} collective-permute-done((f32[120,128]{1,0:T(8,128)S(1)}, f32[120,128]{1,0:T(8,128)S(1)}, u32[]{:S(2)}, u32[]{:S(2)}) %collective-permute-start.5) | collective-permute-done | bytes 61472 | tf_op jit(solution)/shard_map/ppermute | solution.py:597
  23.4 1.7 %first.1 = (f32[46,48,256]{2,1,0:T(8,128)S(1)}, f32[4,32,256]{2,1,0:T(8,128)S(1)}, f32[4,32,256]{2,1,0:T(8,128)S(1)}, f32[192,256]{1,0:T(8,128)S(1)}, f32[34,256...) custom-call(f32[4]{0:T(128)S(1)} %get-tuple-element.53.coefs, ...), custom_call_target="tpu_custom_call", output_to_operand_aliasing={{0}: (1, {})} | custom-call | tf_op jit(solution)/shard_map/first/pallas_call | solution.py:601
  25.1 7.4 %collective-permute-start.8 = (f32[192,256]{1,0:T(8,128)S(1)}, f32[192,256]{1,0:T(8,128)S(1)}, u32[]{:S(2)}, u32[]{:S(2)}) collective-permute-start(f32[192,256]{1,0:T(8,128)S(1)} %get-tuple-element.64), channel_id=1, source_target_pairs={{0,1},{1,2},{2,3},{3,4},{4,5},{5,6},{6,7},{7,8},{8,9},{9,10},{10,1... | collective-permute-start | bytes 589832 | tf_op jit(solution)/shard_map/ppermute | solution.py:587
  32.5 0.5 collective-permute-start.10
  32.9 1.9 %collective-permute-start.11 = (f32[32,256]{1,0:T(8,128)S(1)}, f32[32,256]{1,0:T(8,128)S(1)}, u32[]{:S(2)}, u32[]{:S(2)}) collective-permute-start(f32[32,256]{1,0:T(8,128)S(1)} %get-tuple-element.67), channel_id=1, source_target_pairs={{0,0},{1,1},{2,2},{3,3},{4,4},{5,5},{6,6},{7,7},{8,8},{9,9},{10,10... | collective-permute-start | bytes 98312 | tf_op jit(solution)/shard_map/ppermute | solution.py:593
  34.8 2.5 %weights.1 = (f32[4,48,256]{2,1,0:T(8,128)S(1)}, f32[3,4,32,256]{3,2,1,0:T(8,128)S(1)}, f32[5,8,128]{2,1,0:T(8,128)S(1)}, f32[130,256]{1,0:T(8,128)S(1)}, f32[3,...) custom-call(f32[4]{0:T(128)S(1)} %get-tuple-element.53.coefs, ...), custom_call_target="tpu_custom_call" | custom-call | tf_op jit(solution)/shard_map/weights/pallas_call | solution.py:601
  37.4 2.0 %collective-permute-done.11.far = f32[32,256]{1,0:T(8,128)S(1)} collective-permute-done((f32[32,256]{1,0:T(8,128)S(1)}, f32[32,256]{1,0:T(8,128)S(1)}, u32[]{:S(2)}, u32[]{:S(2)}) %collective-permute-start.11) | collective-permute-done | bytes 32800 | tf_op jit(solution)/shard_map/ppermute | solution.py:593
  39.4 1.1 %collective-permute-start.12 = (f32[192,256]{1,0:T(8,128)S(1)}, f32[192,256]{1,0:T(8,128)S(1)}, u32[]{:S(2)}, u32[]{:S(2)}) collective-permute-start(f32[192,256]{1,0:T(8,128)S(1)} %collective-permute-done.8.r), channel_id=1, source_target_pairs={{0,64},{64,0},{1,65},{65,1},{2,66},{66,2},{3,67},{67,3},{4,68},{68... | collective-permute-start | bytes 589832 | tf_op jit(solution)/shard_map/ppermute | solution.py:597
  41.1 1.1 %collective-permute-done.15.fars = f32[32,256]{1,0:T(8,128)S(1)} collective-permute-done((f32[32,256]{1,0:T(8,128)S(1)}, f32[32,256]{1,0:T(8,128)S(1)}, u32[]{:S(2)}, u32[]{:S(2)}) %collective-permute-start.15) | collective-permute-done | bytes 32800 | tf_op jit(solution)/shard_map/ppermute | solution.py:597
  42.2 2.0 %moments.1 = (f32[128,64]{1,0:T(8,128)S(1)}, f32[13,48,256]{2,1,0:T(8,128)S(1)}, f32[8,48,256]{2,1,0:T(8,128)S(1)}, f32[9,48,256]{2,1,0:T(8,128)S(1)}, f32[7,48,...) custom-call(f32[4,32,256]{2,1,0:T(8,128)S(1)} %get-tuple-element.62., ...), custom_call_target="tpu_custom_call" | custom-call | tf_op jit(solution)/shard_map/moments/pallas_call | solution.py:601
  44.2 6.4 %collective-permute-start.16 = (f32[264,256]{1,0:T(8,128)S(1)}, f32[264,256]{1,0:T(8,128)S(1)}, u32[]{:S(2)}, u32[]{:S(2)}) collective-permute-start(f32[264,256]{1,0:T(8,128)S(1)} %get-tuple-element.79), channel_id=1, source_target_pairs={{0,1},{1,2},{2,3},{3,4},{4,5},{5,6},{6,7},{7,8},{8,9},{9,10},{10,1... | collective-permute-start | bytes 811016 | tf_op jit(solution)/shard_map/ppermute | solution.py:587
  50.5 15.5 %all_to_all.5 = f32[128,1,64]{2,1,0:T(1,128)S(1)} all-to-all(f32[128,1,64]{2,1,0:T(1,128)S(1)} %bitcast.5), channel_id=1, replica_groups=mesh['gx'=2,'gy'=2,'gz'=64] {'gx','gz'}, dimensions={0} | all-to-all | bytes 65536 | tf_op jit(solution)/shard_map/all_to_all | solution.py:677
  66.1 1.7 %collective-permute-start.17 = (f32[264,256]{1,0:T(8,128)S(1)}, f32[264,256]{1,0:T(8,128)S(1)}, u32[]{:S(2)}, u32[]{:S(2)}) collective-permute-start(f32[264,256]{1,0:T(8,128)S(1)} %collective-permute-done.16.ri), channel_id=1, source_target_pairs={{0,64},{64,0},{1,65},{65,1},{2,66},{66,2},{3,67},{67,3},{4,68},{68... | collective-permute-start | bytes 811016 | tf_op jit(solution)/shard_map/ppermute | solution.py:597
  67.8 1.9 %near.1 = (f32[4]{0:T(128)}, f32[8,128]{1,0:T(8,128)S(1)}, f32[4,48,256]{2,1,0:T(8,128)S(1)}, f32[4,2,48,256]{3,2,1,0:T(8,128)S(1)}, f32[4,2,32,128]{3,2,1,0:T(8,128)S(1)}) custom-call(f32[4]{0:T(128)S(1)} %get-tuple-element.53.coefs, f32[128,64]{1,0:T(8,128)S(1)} %bitcast.4, f32[8,48,256]{2,1,0:T(8,128)S(1)} %get-tuple-element.82.uu, ...), custom_call_target="tpu_custom_call" | custom-call | tf_op jit(solution)/shard_map/near/pallas_call | solution.py:601
  69.6 1.8 %far.1 = (f32[4,32,128]{2,1,0:T(8,128)}, f32[3,4,32,128]{3,2,1,0:T(8,128)}) custom-call(f32[4]{0:T(128)S(1)} %get-tuple-element.53.coefs, f32[8,128]{1,0:T(8,128)S(1)} %get-tuple-element.96.table, f32[8,48,256]{2,1,0:T(8,128)S(1)} %get-tuple-element.82.uu, f32[9,48,256]{2,1,0:T(8,128)S(1)} %get-tuple-element.83.f, f32[7,48,256]{2,1,0:T(8,128)S(1)} %get-tuple-element.84.af, ...), custom_call_target="tpu_custom_call" | custom-call | tf_op jit(solution)/shard_map/far/pallas_call | solution.py:601
  (21 shorter events, 1.0 us)
Async XLA Ops:
  1.8 4.3 %collective-permute-start.2 = (f32[7,32,128]{2,1,0:T(8,128)S(1)}, f32[7,32,128]{2,1,0:T(8,128)S(1)}, u32[]{:S(2)}, u32[]{:S(2)}) collective-permute-start(f32[7,32,128]{2,1,0:T(8,128)S(1)} %get-tuple-element.56), channel_id=1, source_target_pairs={{0,64},{64,0},{1,65},{65,1},{2,66},{66,2},{3,67},{67,3},{4,68},{68... | collective-permute-start | bytes 344072 | tf_op jit(solution)/shard_map/ppermute | solution.py:597
  5.2 18.1 %collective-permute-start = (f32[32,32,128]{2,1,0:T(8,128)S(1)}, f32[32,32,128]{2,1,0:T(8,128)S(1)}, u32[]{:S(2)}, u32[]{:S(2)}) collective-permute-start(f32[32,32,128]{2,1,0:T(8,128)S(1)} %get-tuple-element.54.stack), channel_id=1, source_target_pairs={{0,64},{64,0},{1,65},{65,1},{2,66},{66,2},{3,67},{67,3},{4,68},{68... | collective-permute-start | bytes 1572872 | tf_op jit(solution)/shard_map/ppermute | solution.py:597
  6.1 14.8 %collective-permute-start.3 = (f32[7,32,256]{2,1,0:T(8,128)S(1)}, f32[7,32,256]{2,1,0:T(8,128)S(1)}, u32[]{:S(2)}, u32[]{:S(2)}) collective-permute-start(f32[7,32,256]{2,1,0:T(8,128)S(1)} %get-tuple-element.57), channel_id=1, source_target_pairs={{0,1},{1,2},{2,3},{3,4},{4,5},{5,6},{6,7},{7,8},{8,9},{9,10},{10,1... | collective-permute-start | bytes 688136 | tf_op jit(solution)/shard_map/ppermute | solution.py:587
  15.2 5.3 %collective-permute-start.1 = (f32[120,128]{1,0:T(8,128)S(1)}, f32[120,128]{1,0:T(8,128)S(1)}, u32[]{:S(2)}, u32[]{:S(2)}) collective-permute-start(f32[120,128]{1,0:T(8,128)S(1)} %get-tuple-element.55), channel_id=1, source_target_pairs={{0,128},{128,0},{1,129},{129,1},{2,130},{130,2},{3,131},{131,3},{4... | collective-permute-start | bytes 184328 | tf_op jit(solution)/shard_map/ppermute | solution.py:625
  15.9 5.0 %collective-permute-start.4 = (f32[16,256]{1,0:T(8,128)S(1)}, f32[16,256]{1,0:T(8,128)S(1)}, u32[]{:S(2)}, u32[]{:S(2)}) collective-permute-start(f32[16,256]{1,0:T(8,128)S(1)} %get-tuple-element.58), channel_id=1, source_target_pairs={{0,129},{1,130},{2,131},{3,132},{4,133},{5,134},{6,135},{7,136},{8... | collective-permute-start | bytes 49160 | tf_op jit(solution)/shard_map/ppermute | solution.py:587
  20.9 2.4 %collective-permute-start.6 = (f32[7,32,256]{2,1,0:T(8,128)S(1)}, f32[7,32,256]{2,1,0:T(8,128)S(1)}, u32[]{:S(2)}, u32[]{:S(2)}) collective-permute-start(f32[7,32,256]{2,1,0:T(8,128)S(1)} %collective-permute-done.3.mr), channel_id=1, source_target_pairs={{0,64},{64,0},{1,65},{65,1},{2,66},{66,2},{3,67},{67,3},{4,68},{68... | collective-permute-start | bytes 688136 | tf_op jit(solution)/shard_map/ppermute | solution.py:597
  22.0 1.2 %collective-permute-start.5 = (f32[120,128]{1,0:T(8,128)S(1)}, f32[120,128]{1,0:T(8,128)S(1)}, u32[]{:S(2)}, u32[]{:S(2)}) collective-permute-start(f32[120,128]{1,0:T(8,128)S(1)} %collective-permute-done.1.gxr), channel_id=1, source_target_pairs={{0,64},{64,0},{1,65},{65,1},{2,66},{66,2},{3,67},{67,3},{4,68},{68... | collective-permute-start | bytes 184328 | tf_op jit(solution)/shard_map/ppermute | solution.py:597
  22.0 1.4 %collective-permute-start.7 = (f32[16,256]{1,0:T(8,128)S(1)}, f32[16,256]{1,0:T(8,128)S(1)}, u32[]{:S(2)}, u32[]{:S(2)}) collective-permute-start(f32[16,256]{1,0:T(8,128)S(1)} %collective-permute-done.4.dr), channel_id=1, source_target_pairs={{0,64},{64,0},{1,65},{65,1},{2,66},{66,2},{3,67},{67,3},{4,68},{68... | collective-permute-start | bytes 49160 | tf_op jit(solution)/shard_map/ppermute | solution.py:597
  25.1 14.3 %collective-permute-start.8 = (f32[192,256]{1,0:T(8,128)S(1)}, f32[192,256]{1,0:T(8,128)S(1)}, u32[]{:S(2)}, u32[]{:S(2)}) collective-permute-start(f32[192,256]{1,0:T(8,128)S(1)} %get-tuple-element.64), channel_id=1, source_target_pairs={{0,1},{1,2},{2,3},{3,4},{4,5},{5,6},{6,7},{7,8},{8,9},{9,10},{10,1... | collective-permute-start | bytes 589832 | tf_op jit(solution)/shard_map/ppermute | solution.py:587
  32.5 6.9 %collective-permute-start.10 = (f32[72,128]{1,0:T(8,128)S(1)}, f32[72,128]{1,0:T(8,128)S(1)}, u32[]{:S(2)}, u32[]{:S(2)}) collective-permute-start(f32[72,128]{1,0:T(8,128)S(1)} %get-tuple-element.66), channel_id=1, source_target_pairs={{0,128},{128,0},{1,129},{129,1},{2,130},{130,2},{3,131},{131,3},{4... | collective-permute-start | bytes 110600 | tf_op jit(solution)/shard_map/ppermute | solution.py:653
  32.9 6.5 %collective-permute-start.9 = (f32[34,256]{1,0:T(8,128)S(1)}, f32[34,256]{1,0:T(8,128)S(1)}, u32[]{:S(2)}, u32[]{:S(2)}) collective-permute-start(f32[34,256]{1,0:T(8,128)S(1)} %get-tuple-element.65), channel_id=1, source_target_pairs={{0,129},{1,130},{2,131},{3,132},{4,133},{5,134},{6,135},{7,136},{8... | collective-permute-start | bytes 104456 | tf_op jit(solution)/shard_map/ppermute | solution.py:587
  32.9 6.4 %collective-permute-start.11 = (f32[32,256]{1,0:T(8,128)S(1)}, f32[32,256]{1,0:T(8,128)S(1)}, u32[]{:S(2)}, u32[]{:S(2)}) collective-permute-start(f32[32,256]{1,0:T(8,128)S(1)} %get-tuple-element.67), channel_id=1, source_target_pairs={{0,0},{1,1},{2,2},{3,3},{4,4},{5,5},{6,6},{7,7},{8,8},{9,9},{10,10... | collective-permute-start | bytes 98312 | tf_op jit(solution)/shard_map/ppermute | solution.py:593
  39.4 2.8 %collective-permute-start.12 = (f32[192,256]{1,0:T(8,128)S(1)}, f32[192,256]{1,0:T(8,128)S(1)}, u32[]{:S(2)}, u32[]{:S(2)}) collective-permute-start(f32[192,256]{1,0:T(8,128)S(1)} %collective-permute-done.8.r), channel_id=1, source_target_pairs={{0,64},{64,0},{1,65},{65,1},{2,66},{66,2},{3,67},{67,3},{4,68},{68... | collective-permute-start | bytes 589832 | tf_op jit(solution)/shard_map/ppermute | solution.py:597
  40.5 1.7 %collective-permute-start.14 = (f32[72,128]{1,0:T(8,128)S(1)}, f32[72,128]{1,0:T(8,128)S(1)}, u32[]{:S(2)}, u32[]{:S(2)}) collective-permute-start(f32[72,128]{1,0:T(8,128)S(1)} %collective-permute-done.10.x), channel_id=1, source_target_pairs={{0,64},{64,0},{1,65},{65,1},{2,66},{66,2},{3,67},{67,3},{4,68},{68... | collective-permute-start | bytes 110600 | tf_op jit(solution)/shard_map/ppermute | solution.py:597
  40.6 1.6 %collective-permute-start.13 = (f32[34,256]{1,0:T(8,128)S(1)}, f32[34,256]{1,0:T(8,128)S(1)}, u32[]{:S(2)}, u32[]{:S(2)}) collective-permute-start(f32[34,256]{1,0:T(8,128)S(1)} %collective-permute-done.9.d), channel_id=1, source_target_pairs={{0,64},{64,0},{1,65},{65,1},{2,66},{66,2},{3,67},{67,3},{4,68},{68... | collective-permute-start | bytes 104456 | tf_op jit(solution)/shard_map/ppermute | solution.py:597
  41.0 1.2 %collective-permute-start.15 = (f32[32,256]{1,0:T(8,128)S(1)}, f32[32,256]{1,0:T(8,128)S(1)}, u32[]{:S(2)}, u32[]{:S(2)}) collective-permute-start(f32[32,256]{1,0:T(8,128)S(1)} %collective-permute-done.11.far), channel_id=1, source_target_pairs={{0,64},{64,0},{1,65},{65,1},{2,66},{66,2},{3,67},{67,3},{4,68},{68... | collective-permute-start | bytes 98312 | tf_op jit(solution)/shard_map/ppermute | solution.py:597
  44.2 21.9 %collective-permute-start.16 = (f32[264,256]{1,0:T(8,128)S(1)}, f32[264,256]{1,0:T(8,128)S(1)}, u32[]{:S(2)}, u32[]{:S(2)}) collective-permute-start(f32[264,256]{1,0:T(8,128)S(1)} %get-tuple-element.79), channel_id=1, source_target_pairs={{0,1},{1,2},{2,3},{3,4},{4,5},{5,6},{6,7},{7,8},{8,9},{9,10},{10,1... | collective-permute-start | bytes 811016 | tf_op jit(solution)/shard_map/ppermute | solution.py:587
  66.1 3.5 %collective-permute-start.17 = (f32[264,256]{1,0:T(8,128)S(1)}, f32[264,256]{1,0:T(8,128)S(1)}, u32[]{:S(2)}, u32[]{:S(2)}) collective-permute-start(f32[264,256]{1,0:T(8,128)S(1)} %collective-permute-done.16.ri), channel_id=1, source_target_pairs={{0,64},{64,0},{1,65},{65,1},{2,66},{66,2},{3,67},{67,3},{4,68},{68... | collective-permute-start | bytes 811016 | tf_op jit(solution)/shard_map/ppermute | solution.py:597

commit v8 on v7

--- a/solution.py
+++ b/solution.py
@@ -297,7 +297,16 @@
     return (6.0 + SHIFT) * c - ((zu + zd) + (x_up(c) + x_dn(c)) + (y_up(c) + y_dn(c)))
 
 
-def moment_kernel(b4, u4, r, s, d, ds, x, xs, far, fars, w, part, edge, out, bb, uu, f, af, a2f, ab, au, send, a2b, a2u):
+def gather_kernel(d, x, far, out):
+    out[0:CX] = far[...]
+    half = RIM_ROWS // 2
+    out[CX : CX + half, :CY] = x[:half]
+    out[CX : CX + half, CY:] = x[half:]
+    out[CX + half : CX + half + AGAIN_ROWS] = d[...]
+
+
+def moment_kernel(b4, u4, r, s, d, x, far, swapped, w, part, edge, out, bb, uu, f, af, a2f, ab, au, send, a2b, a2u):
+    corner = CX + RIM_ROWS // 2
     c = lax.axis_index("gy")
     near = pl.ds(NEAR, NARROW)
     bb[4:8, HX : HX + CX] = b4[...]
@@ -309,7 +318,7 @@
         lo, hi = low_high(c, r[CX * n : CX * (n + 1)], s[CX * n : CX * (n + 1)])
         dst[below, HX : HX + CX] = lo
         dst[above, HX : HX + CX] = hi
-        lo, hi = low_high(c, d[row : row + 2 * width], ds[row : row + 2 * width])
+        lo, hi = low_high(c, d[row : row + 2 * width], swapped[corner + row : corner + row + 2 * width])
         for layer, part_rows in ((below, lo), (above, hi)):
             dst[layer, HX - width : HX] = part_rows[:width]
             dst[layer, HX + CX : HX + CX + width] = part_rows[width:]
@@ -317,12 +326,13 @@
     row = 0
     for name, z, width in RIM:
         dst, layer = (bb, 4 + z) if name == "b" else (uu, 2 + z)
-        for half, src in enumerate((x, xs)):
-            lanes = pl.ds(CY * half, CY)
-            dst[layer, HX - width : HX, lanes] = src[row : row + width]
-            dst[layer, HX + CX : HX + CX + width, lanes] = src[row + width : row + 2 * width]
+        place, side = CX + row % (RIM_ROWS // 2), pl.ds(CY * (row // (RIM_ROWS // 2)), CY)
+        dst[layer, HX - width : HX, :CY] = x[row : row + width]
+        dst[layer, HX + CX : HX + CX + width, :CY] = x[row + width : row + 2 * width]
+        dst[layer, HX - width : HX, CY:] = swapped[place : place + width, side]
+        dst[layer, HX + CX : HX + CX + width, CY:] = swapped[place + width : place + 2 * width, side]
         row += 2 * width
-    bb[12, HX : HX + CX] = jnp.where(c == 1, far[...], other_first(fars[...]))
+    bb[12, HX : HX + CX] = jnp.where(c == 1, far[...], other_first(swapped[0:CX]))
 
     def wide(t):
         a = bb[t + 2]
@@ -662,13 +672,13 @@
         1,
     )
     r2, d2, x2, far, w, part, edge = lax.optimization_barrier((r2, d2, x2, far, w, part, edge))
-    s2, ds2, xs2 = swap(r2), swap(d2), swap(x2)
-    fars = swap(far)
+    small = call(gather_kernel, f32(CX + RIM_ROWS // 2 + AGAIN_ROWS, LANES), (d2, x2, far), [], "gather", 0)
+    s2, swapped = swap(r2), swap(small)
     sums, bb, uu, f, af, a2f, ab, au, send = call(
         moment_kernel,
         (f32(PARTNERS, SLOTS), layers(13), layers(8), layers(9), layers(7), layers(5), layers(8), layers(6),
          f32(THIRD_ROWS, LANES)),
-        (b, u, r2, s2, d2, ds2, x2, xs2, far, fars, w, part, edge),
+        (b, u, r2, s2, d2, x2, far, swapped, w, part, edge),
         [scratch(4), scratch(4)],
         "moments",
         0,

time: 71.6 us -> 71.4 us (level)
    ppermute x10 -> x8, starting transfers between devices: 8.36 us -> 8.04 us  [swap(): return lax.ppermute(value, 'gy', SWAP)]
    ppermute x10 -> x8, waiting for transfers between devices: 2.73 us -> 2.91 us  [swap(): return lax.ppermute(value, 'gy', SWAP)]
    pallas_call x7 -> x8, Pallas kernels: 9.91 us -> 9.86 us  [call(): pl.pallas_call(kernel, out_shape=outs, in_specs=[SM] * smem + [VM] * (len...]
  transfers between devices with their start and end apart: 18 -> 16, of which waited for: 6 -> 6; matrix products, arithmetic and copies ran while one was open for 0% -> 0% of each run, Pallas kernels for 6% -> 6%
where the time goes in v8:
time: 71.4 us; the launch traced here: 71.2 us
  starting transfers between devices  34 us (48%)
  blocking collectives  15.5 us (22%)
  Pallas kernels  11.1 us (16%)
  waiting for transfers between devices  9.89 us (14%)
    ppermute x5, starting transfers between devices, role_shift(): return lax.ppermute(value, ('gx', 'gy', 'gz'), pairs)  22.9 us
    all_to_all x1, blocking collectives, local(): lax.all_to_all(sums.reshape(PARTNERS, 1, SLOTS), ('gx', 'gz'), 0, 0)  15.5 us
    pallas_call x8, Pallas kernels, call(): pl.pallas_call(kernel, out_shape=outs, in_specs=[SM] * smem + [VM] * (len...  9.86 us
    ppermute x8, starting transfers between devices, swap(): return lax.ppermute(value, 'gy', SWAP)  8.04 us
    ppermute x1, waiting for transfers between devices, local(): gxr = lax.ppermute(edges, 'gx', SWAP)  4.44 us
    ppermute x8, waiting for transfers between devices, swap(): return lax.ppermute(value, 'gy', SWAP)  2.91 us
    ppermute x1, waiting for transfers between devices, second_down(): return lax.ppermute(value, ('gx', 'gy', 'gz'), pairs)  2.02 us
    ppermute x1, starting transfers between devices, second_down(): return lax.ppermute(value, ('gx', 'gy', 'gz'), pairs)  1.91 us
  transfers between devices with their start and end apart: 16, of which 6 were waited for; matrix products, arithmetic and copies ran while one was open for 0% of the time, Pallas kernels for 6%

profile of v8, /device:TPU:1, one launch (start us, length us, event | category | flops | bytes accessed | tf_op | source)
XLA Modules:
  0.0 71.2 jit_solution(10974400864424325721)
XLA Ops:
  0.6 1.2 %load.1 = (f32[32,32,128]{2,1,0:T(8,128)S(1)}, f32[120,128]{1,0:T(8,128)S(1)}, f32[4]{0:T(128)S(1)}, f32[7,32,128]{2,1,0:T(8,128)S(1)}) custom-call(f32[3,4,32,128]{3,2,1,0:T(8,128)} %vel.1, f32[4,32,128]{2,1,0:T(8,128)} %ph.1, f32[4,32,128]{2,1,0:T(8,128)} %po.1, f32[3,4,32,128]{3,2,1,0:T(8,128)} %vo.1, f32[4]{0:T(128)} %coefs.1), custom_call_target="tpu_custom_call" | custom-call | tf_op jit(solution)/shard_map/load/pallas_call | solution.py:625
  1.8 3.3 %collective-permute-start.2 = (f32[7,32,128]{2,1,0:T(8,128)S(1)}, f32[7,32,128]{2,1,0:T(8,128)S(1)}, u32[]{:S(2)}, u32[]{:S(2)}) collective-permute-start(f32[7,32,128]{2,1,0:T(8,128)S(1)} %get-tuple-element.56), channel_id=1, source_target_pairs={{0,64},{64,0},{1,65},{65,1},{2,66},{66,2},{3,67},{67,3},{4,68},{68... | collective-permute-start | bytes 344072 | tf_op jit(solution)/shard_map/ppermute | solution.py:607
  5.3 0.9 %collective-permute-done.2.got = f32[7,32,128]{2,1,0:T(8,128)S(1)} collective-permute-done((f32[7,32,128]{2,1,0:T(8,128)S(1)}, f32[7,32,128]{2,1,0:T(8,128)S(1)}, u32[]{:S(2)}, u32[]{:S(2)}) %collective-permute-start.2) | collective-permute-done | bytes 114720 | tf_op jit(solution)/shard_map/ppermute | solution.py:607
  6.1 9.0 %collective-permute-start.3 = (f32[7,32,256]{2,1,0:T(8,128)S(1)}, f32[7,32,256]{2,1,0:T(8,128)S(1)}, u32[]{:S(2)}, u32[]{:S(2)}) collective-permute-start(f32[7,32,256]{2,1,0:T(8,128)S(1)} %get-tuple-element.57), channel_id=1, source_target_pairs={{0,1},{1,2},{2,3},{3,4},{4,5},{5,6},{6,7},{7,8},{8,9},{9,10},{10,1... | collective-permute-start | bytes 688136 | tf_op jit(solution)/shard_map/ppermute | solution.py:597
  15.2 0.7 %collective-permute-start.1 = (f32[120,128]{1,0:T(8,128)S(1)}, f32[120,128]{1,0:T(8,128)S(1)}, u32[]{:S(2)}, u32[]{:S(2)}) collective-permute-start(f32[120,128]{1,0:T(8,128)S(1)} %get-tuple-element.55), channel_id=1, source_target_pairs={{0,128},{128,0},{1,129},{129,1},{2,130},{130,2},{3,131},{131,3},{4... | collective-permute-start | bytes 184328 | tf_op jit(solution)/shard_map/ppermute | solution.py:635
  16.0 4.4 %collective-permute-done.1.gxr = f32[120,128]{1,0:T(8,128)S(1)} collective-permute-done((f32[120,128]{1,0:T(8,128)S(1)}, f32[120,128]{1,0:T(8,128)S(1)}, u32[]{:S(2)}, u32[]{:S(2)}) %collective-permute-start.1) | collective-permute-done | bytes 61472 | tf_op jit(solution)/shard_map/ppermute | solution.py:635
  20.4 0.5 collective-permute-done.4.dr
  20.9 1.1 %collective-permute-start.6 = (f32[7,32,256]{2,1,0:T(8,128)S(1)}, f32[7,32,256]{2,1,0:T(8,128)S(1)}, u32[]{:S(2)}, u32[]{:S(2)}) collective-permute-start(f32[7,32,256]{2,1,0:T(8,128)S(1)} %collective-permute-done.3.mr), channel_id=1, source_target_pairs={{0,64},{64,0},{1,65},{65,1},{2,66},{66,2},{3,67},{67,3},{4,68},{68... | collective-permute-start | bytes 688136 | tf_op jit(solution)/shard_map/ppermute | solution.py:607
  22.0 0.5 collective-permute-start.7
  22.5 0.7 %collective-permute-done.5.gxs = f32[120,128]{1,0:T(8,128)S(1)} collective-permute-done((f32[120,128]{1,0:T(8,128)S(1)}, f32[120,128]{1,0:T(8,128)S(1)}, u32[]{:S(2)}, u32[]{:S(2)}) %collective-permute-start.5) | collective-permute-done | bytes 61472 | tf_op jit(solution)/shard_map/ppermute | solution.py:607
  23.4 1.7 %first.1 = (f32[46,48,256]{2,1,0:T(8,128)S(1)}, f32[4,32,256]{2,1,0:T(8,128)S(1)}, f32[4,32,256]{2,1,0:T(8,128)S(1)}, f32[192,256]{1,0:T(8,128)S(1)}, f32[34,256...) custom-call(f32[4]{0:T(128)S(1)} %get-tuple-element.53.coefs, ...), custom_call_target="tpu_custom_call", output_to_operand_aliasing={{0}: (1, {})} | custom-call | tf_op jit(solution)/shard_map/first/pallas_call | solution.py:611
  25.1 7.4 %collective-permute-start.8 = (f32[192,256]{1,0:T(8,128)S(1)}, f32[192,256]{1,0:T(8,128)S(1)}, u32[]{:S(2)}, u32[]{:S(2)}) collective-permute-start(f32[192,256]{1,0:T(8,128)S(1)} %get-tuple-element.64), channel_id=1, source_target_pairs={{0,1},{1,2},{2,3},{3,4},{4,5},{5,6},{6,7},{7,8},{8,9},{9,10},{10,1... | collective-permute-start | bytes 589832 | tf_op jit(solution)/shard_map/ppermute | solution.py:597
  32.5 0.5 collective-permute-start.10
  32.9 1.9 %collective-permute-start.11 = (f32[32,256]{1,0:T(8,128)S(1)}, f32[32,256]{1,0:T(8,128)S(1)}, u32[]{:S(2)}, u32[]{:S(2)}) collective-permute-start(f32[32,256]{1,0:T(8,128)S(1)} %get-tuple-element.67), channel_id=1, source_target_pairs={{0,0},{1,1},{2,2},{3,3},{4,4},{5,5},{6,6},{7,7},{8,8},{9,9},{10,10... | collective-permute-start | bytes 98312 | tf_op jit(solution)/shard_map/ppermute | solution.py:603
  34.8 2.5 %weights.1 = (f32[4,48,256]{2,1,0:T(8,128)S(1)}, f32[3,4,32,256]{3,2,1,0:T(8,128)S(1)}, f32[5,8,128]{2,1,0:T(8,128)S(1)}, f32[130,256]{1,0:T(8,128)S(1)}, f32[3,...) custom-call(f32[4]{0:T(128)S(1)} %get-tuple-element.53.coefs, ...), custom_call_target="tpu_custom_call" | custom-call | tf_op jit(solution)/shard_map/weights/pallas_call | solution.py:611
  37.4 2.0 %collective-permute-done.11.far = f32[32,256]{1,0:T(8,128)S(1)} collective-permute-done((f32[32,256]{1,0:T(8,128)S(1)}, f32[32,256]{1,0:T(8,128)S(1)}, u32[]{:S(2)}, u32[]{:S(2)}) %collective-permute-start.11) | collective-permute-done | bytes 32800 | tf_op jit(solution)/shard_map/ppermute | solution.py:603
  39.4 1.1 %collective-permute-start.12 = (f32[192,256]{1,0:T(8,128)S(1)}, f32[192,256]{1,0:T(8,128)S(1)}, u32[]{:S(2)}, u32[]{:S(2)}) collective-permute-start(f32[192,256]{1,0:T(8,128)S(1)} %collective-permute-done.8.r), channel_id=1, source_target_pairs={{0,64},{64,0},{1,65},{65,1},{2,66},{66,2},{3,67},{67,3},{4,68},{68... | collective-permute-start | bytes 589832 | tf_op jit(solution)/shard_map/ppermute | solution.py:607
  40.8 1.3 %collective-permute-done.13.swapped = f32[102,256]{1,0:T(8,128)S(1)} collective-permute-done((f32[102,256]{1,0:T(8,128)S(1)}, f32[102,256]{1,0:T(8,128)S(1)}, u32[]{:S(2)}, u32[]{:S(2)}) %collective-permute-start.13) | collective-permute-done | bytes 104480 | tf_op jit(solution)/shard_map/ppermute | solution.py:607
  42.1 1.9 %moments.1 = (f32[128,64]{1,0:T(8,128)S(1)}, f32[13,48,256]{2,1,0:T(8,128)S(1)}, f32[8,48,256]{2,1,0:T(8,128)S(1)}, f32[9,48,256]{2,1,0:T(8,128)S(1)}, f32[7,48,...) custom-call(f32[4,32,256]{2,1,0:T(8,128)S(1)} %get-tuple-element.62., ...), custom_call_target="tpu_custom_call" | custom-call | tf_op jit(solution)/shard_map/moments/pallas_call | solution.py:611
  44.0 6.4 %collective-permute-start.14 = (f32[264,256]{1,0:T(8,128)S(1)}, f32[264,256]{1,0:T(8,128)S(1)}, u32[]{:S(2)}, u32[]{:S(2)}) collective-permute-start(f32[264,256]{1,0:T(8,128)S(1)} %get-tuple-element.79), channel_id=1, source_target_pairs={{0,1},{1,2},{2,3},{3,4},{4,5},{5,6},{6,7},{7,8},{8,9},{9,10},{10,1... | collective-permute-start | bytes 811016 | tf_op jit(solution)/shard_map/ppermute | solution.py:597
  50.4 15.5 %all_to_all.5 = f32[128,1,64]{2,1,0:T(1,128)S(1)} all-to-all(f32[128,1,64]{2,1,0:T(1,128)S(1)} %bitcast.5), channel_id=1, replica_groups=mesh['gx'=2,'gy'=2,'gz'=64] {'gx','gz'}, dimensions={0} | all-to-all | bytes 65536 | tf_op jit(solution)/shard_map/all_to_all | solution.py:687
  65.9 1.7 %collective-permute-start.15 = (f32[264,256]{1,0:T(8,128)S(1)}, f32[264,256]{1,0:T(8,128)S(1)}, u32[]{:S(2)}, u32[]{:S(2)}) collective-permute-start(f32[264,256]{1,0:T(8,128)S(1)} %collective-permute-done.14.ri), channel_id=1, source_target_pairs={{0,64},{64,0},{1,65},{65,1},{2,66},{66,2},{3,67},{67,3},{4,68},{68... | collective-permute-start | bytes 811016 | tf_op jit(solution)/shard_map/ppermute | solution.py:607
  67.6 1.9 %near.1 = (f32[4]{0:T(128)}, f32[8,128]{1,0:T(8,128)S(1)}, f32[4,48,256]{2,1,0:T(8,128)S(1)}, f32[4,2,48,256]{3,2,1,0:T(8,128)S(1)}, f32[4,2,32,128]{3,2,1,0:T(8,128)S(1)}) custom-call(f32[4]{0:T(128)S(1)} %get-tuple-element.53.coefs, f32[128,64]{1,0:T(8,128)S(1)} %bitcast.4, f32[8,48,256]{2,1,0:T(8,128)S(1)} %get-tuple-element.82.uu, ...), custom_call_target="tpu_custom_call" | custom-call | tf_op jit(solution)/shard_map/near/pallas_call | solution.py:611
  69.4 1.8 %far.1 = (f32[4,32,128]{2,1,0:T(8,128)}, f32[3,4,32,128]{3,2,1,0:T(8,128)}) custom-call(f32[4]{0:T(128)S(1)} %get-tuple-element.53.coefs, f32[8,128]{1,0:T(8,128)S(1)} %get-tuple-element.96.table, f32[8,48,256]{2,1,0:T(8,128)S(1)} %get-tuple-element.82.uu, f32[9,48,256]{2,1,0:T(8,128)S(1)} %get-tuple-element.83.f, f32[7,48,256]{2,1,0:T(8,128)S(1)} %get-tuple-element.84.af, ...), custom_call_target="tpu_custom_call" | custom-call | tf_op jit(solution)/shard_map/far/pallas_call | solution.py:611
  (18 shorter events, 0.6 us)
Async XLA Ops:
  1.8 4.3 %collective-permute-start.2 = (f32[7,32,128]{2,1,0:T(8,128)S(1)}, f32[7,32,128]{2,1,0:T(8,128)S(1)}, u32[]{:S(2)}, u32[]{:S(2)}) collective-permute-start(f32[7,32,128]{2,1,0:T(8,128)S(1)} %get-tuple-element.56), channel_id=1, source_target_pairs={{0,64},{64,0},{1,65},{65,1},{2,66},{66,2},{3,67},{67,3},{4,68},{68... | collective-permute-start | bytes 344072 | tf_op jit(solution)/shard_map/ppermute | solution.py:607
  5.2 18.1 %collective-permute-start = (f32[32,32,128]{2,1,0:T(8,128)S(1)}, f32[32,32,128]{2,1,0:T(8,128)S(1)}, u32[]{:S(2)}, u32[]{:S(2)}) collective-permute-start(f32[32,32,128]{2,1,0:T(8,128)S(1)} %get-tuple-element.54.stack), channel_id=1, source_target_pairs={{0,64},{64,0},{1,65},{65,1},{2,66},{66,2},{3,67},{67,3},{4,68},{68... | collective-permute-start | bytes 1572872 | tf_op jit(solution)/shard_map/ppermute | solution.py:607
  6.1 14.8 %collective-permute-start.3 = (f32[7,32,256]{2,1,0:T(8,128)S(1)}, f32[7,32,256]{2,1,0:T(8,128)S(1)}, u32[]{:S(2)}, u32[]{:S(2)}) collective-permute-start(f32[7,32,256]{2,1,0:T(8,128)S(1)} %get-tuple-element.57), channel_id=1, source_target_pairs={{0,1},{1,2},{2,3},{3,4},{4,5},{5,6},{6,7},{7,8},{8,9},{9,10},{10,1... | collective-permute-start | bytes 688136 | tf_op jit(solution)/shard_map/ppermute | solution.py:597
  15.2 5.3 %collective-permute-start.1 = (f32[120,128]{1,0:T(8,128)S(1)}, f32[120,128]{1,0:T(8,128)S(1)}, u32[]{:S(2)}, u32[]{:S(2)}) collective-permute-start(f32[120,128]{1,0:T(8,128)S(1)} %get-tuple-element.55), channel_id=1, source_target_pairs={{0,128},{128,0},{1,129},{129,1},{2,130},{130,2},{3,131},{131,3},{4... | collective-permute-start | bytes 184328 | tf_op jit(solution)/shard_map/ppermute | solution.py:635
  15.9 5.0 %collective-permute-start.4 = (f32[16,256]{1,0:T(8,128)S(1)}, f32[16,256]{1,0:T(8,128)S(1)}, u32[]{:S(2)}, u32[]{:S(2)}) collective-permute-start(f32[16,256]{1,0:T(8,128)S(1)} %get-tuple-element.58), channel_id=1, source_target_pairs={{0,129},{1,130},{2,131},{3,132},{4,133},{5,134},{6,135},{7,136},{8... | collective-permute-start | bytes 49160 | tf_op jit(solution)/shard_map/ppermute | solution.py:597
  20.9 2.4 %collective-permute-start.6 = (f32[7,32,256]{2,1,0:T(8,128)S(1)}, f32[7,32,256]{2,1,0:T(8,128)S(1)}, u32[]{:S(2)}, u32[]{:S(2)}) collective-permute-start(f32[7,32,256]{2,1,0:T(8,128)S(1)} %collective-permute-done.3.mr), channel_id=1, source_target_pairs={{0,64},{64,0},{1,65},{65,1},{2,66},{66,2},{3,67},{67,3},{4,68},{68... | collective-permute-start | bytes 688136 | tf_op jit(solution)/shard_map/ppermute | solution.py:607
  22.0 1.2 %collective-permute-start.5 = (f32[120,128]{1,0:T(8,128)S(1)}, f32[120,128]{1,0:T(8,128)S(1)}, u32[]{:S(2)}, u32[]{:S(2)}) collective-permute-start(f32[120,128]{1,0:T(8,128)S(1)} %collective-permute-done.1.gxr), channel_id=1, source_target_pairs={{0,64},{64,0},{1,65},{65,1},{2,66},{66,2},{3,67},{67,3},{4,68},{68... | collective-permute-start | bytes 184328 | tf_op jit(solution)/shard_map/ppermute | solution.py:607
  22.0 1.4 %collective-permute-start.7 = (f32[16,256]{1,0:T(8,128)S(1)}, f32[16,256]{1,0:T(8,128)S(1)}, u32[]{:S(2)}, u32[]{:S(2)}) collective-permute-start(f32[16,256]{1,0:T(8,128)S(1)} %collective-permute-done.4.dr), channel_id=1, source_target_pairs={{0,64},{64,0},{1,65},{65,1},{2,66},{66,2},{3,67},{67,3},{4,68},{68... | collective-permute-start | bytes 49160 | tf_op jit(solution)/shard_map/ppermute | solution.py:607
  25.1 14.3 %collective-permute-start.8 = (f32[192,256]{1,0:T(8,128)S(1)}, f32[192,256]{1,0:T(8,128)S(1)}, u32[]{:S(2)}, u32[]{:S(2)}) collective-permute-start(f32[192,256]{1,0:T(8,128)S(1)} %get-tuple-element.64), channel_id=1, source_target_pairs={{0,1},{1,2},{2,3},{3,4},{4,5},{5,6},{6,7},{7,8},{8,9},{9,10},{10,1... | collective-permute-start | bytes 589832 | tf_op jit(solution)/shard_map/ppermute | solution.py:597
  32.5 6.9 %collective-permute-start.10 = (f32[72,128]{1,0:T(8,128)S(1)}, f32[72,128]{1,0:T(8,128)S(1)}, u32[]{:S(2)}, u32[]{:S(2)}) collective-permute-start(f32[72,128]{1,0:T(8,128)S(1)} %get-tuple-element.66), channel_id=1, source_target_pairs={{0,128},{128,0},{1,129},{129,1},{2,130},{130,2},{3,131},{131,3},{4... | collective-permute-start | bytes 110600 | tf_op jit(solution)/shard_map/ppermute | solution.py:663
  32.9 6.5 %collective-permute-start.9 = (f32[34,256]{1,0:T(8,128)S(1)}, f32[34,256]{1,0:T(8,128)S(1)}, u32[]{:S(2)}, u32[]{:S(2)}) collective-permute-start(f32[34,256]{1,0:T(8,128)S(1)} %get-tuple-element.65), channel_id=1, source_target_pairs={{0,129},{1,130},{2,131},{3,132},{4,133},{5,134},{6,135},{7,136},{8... | collective-permute-start | bytes 104456 | tf_op jit(solution)/shard_map/ppermute | solution.py:597
  32.9 6.4 %collective-permute-start.11 = (f32[32,256]{1,0:T(8,128)S(1)}, f32[32,256]{1,0:T(8,128)S(1)}, u32[]{:S(2)}, u32[]{:S(2)}) collective-permute-start(f32[32,256]{1,0:T(8,128)S(1)} %get-tuple-element.67), channel_id=1, source_target_pairs={{0,0},{1,1},{2,2},{3,3},{4,4},{5,5},{6,6},{7,7},{8,8},{9,9},{10,10... | collective-permute-start | bytes 98312 | tf_op jit(solution)/shard_map/ppermute | solution.py:603
  39.4 2.7 %collective-permute-start.12 = (f32[192,256]{1,0:T(8,128)S(1)}, f32[192,256]{1,0:T(8,128)S(1)}, u32[]{:S(2)}, u32[]{:S(2)}) collective-permute-start(f32[192,256]{1,0:T(8,128)S(1)} %collective-permute-done.8.r), channel_id=1, source_target_pairs={{0,64},{64,0},{1,65},{65,1},{2,66},{66,2},{3,67},{67,3},{4,68},{68... | collective-permute-start | bytes 589832 | tf_op jit(solution)/shard_map/ppermute | solution.py:607
  40.5 1.6 %collective-permute-start.13 = (f32[102,256]{1,0:T(8,128)S(1)}, f32[102,256]{1,0:T(8,128)S(1)}, u32[]{:S(2)}, u32[]{:S(2)}) collective-permute-start(f32[102,256]{1,0:T(8,128)S(1)} %gather.1), channel_id=1, source_target_pairs={{0,64},{64,0},{1,65},{65,1},{2,66},{66,2},{3,67},{67,3},{4,68},{68... | collective-permute-start | bytes 313352 | tf_op jit(solution)/shard_map/ppermute | solution.py:607
  44.0 21.9 %collective-permute-start.14 = (f32[264,256]{1,0:T(8,128)S(1)}, f32[264,256]{1,0:T(8,128)S(1)}, u32[]{:S(2)}, u32[]{:S(2)}) collective-permute-start(f32[264,256]{1,0:T(8,128)S(1)} %get-tuple-element.79), channel_id=1, source_target_pairs={{0,1},{1,2},{2,3},{3,4},{4,5},{5,6},{6,7},{7,8},{8,9},{9,10},{10,1... | collective-permute-start | bytes 811016 | tf_op jit(solution)/shard_map/ppermute | solution.py:597
  65.9 3.5 %collective-permute-start.15 = (f32[264,256]{1,0:T(8,128)S(1)}, f32[264,256]{1,0:T(8,128)S(1)}, u32[]{:S(2)}, u32[]{:S(2)}) collective-permute-start(f32[264,256]{1,0:T(8,128)S(1)} %collective-permute-done.14.ri), channel_id=1, source_target_pairs={{0,64},{64,0},{1,65},{65,1},{2,66},{66,2},{3,67},{67,3},{4,68},{68... | collective-permute-start | bytes 811016 | tf_op jit(solution)/shard_map/ppermute | solution.py:607

commit v9 on v7

--- a/solution.py
+++ b/solution.py
@@ -94,25 +94,24 @@
 
 def load_kernel(vel, ph, po, vo, coefs, stack, out, coefs_out, give, sems):
     copies = [
-        pltpu.make_async_copy(ph, stack.at[pl.ds(CZ * PH, CZ)], sems.at[6]),
-        pltpu.make_async_copy(po, stack.at[pl.ds(CZ * PO, CZ)], sems.at[7]),
-        pltpu.make_async_copy(coefs, coefs_out, sems.at[8]),
+        pltpu.make_async_copy(vel, stack.at[pl.ds(V0, 3)], sems.at[0]),
+        pltpu.make_async_copy(ph, stack.at[PH], sems.at[1]),
+        pltpu.make_async_copy(vo, stack.at[pl.ds(O0, 3)], sems.at[2]),
+        pltpu.make_async_copy(po, stack.at[PO], sems.at[3]),
+        pltpu.make_async_copy(coefs, coefs_out, sems.at[4]),
     ]
-    for i in range(3):
-        copies.append(pltpu.make_async_copy(vel.at[i], stack.at[pl.ds(CZ * (V0 + i), CZ)], sems.at[i]))
-        copies.append(pltpu.make_async_copy(vo.at[i], stack.at[pl.ds(CZ * (O0 + i), CZ)], sems.at[3 + i]))
     for copy in copies:
         copy.start()
     for copy in copies:
         copy.wait()
     other = 1 - lax.axis_index("gy")
     for n, (f, k) in enumerate(SENT):
-        give[n] = stack[CZ * f + outgoing(other, k)]
+        give[n] = stack[f, outgoing(other, k)]
     row = 0
     for f, w in enumerate(EDGE):
         for z in range(CZ):
-            out[row : row + w] = stack[CZ * f + z, CX - w :]
-            out[row + w : row + 2 * w] = stack[CZ * f + z, :w]
+            out[row : row + w] = stack[f, z, CX - w :]
+            out[row + w : row + 2 * w] = stack[f, z, :w]
             row += 2 * w
 
 
@@ -120,7 +119,7 @@
     c = lax.axis_index("gy")
     row = 0
     for n, (f, k) in enumerate(SENT):
-        src = jnp.concatenate([stack[CZ * f + outgoing(c, k)], got[n]], 1)
+        src = jnp.concatenate([stack[f, outgoing(c, k)], got[n]], 1)
         main[n] = src
         w = CORNER[n]
         if w:
@@ -136,7 +135,7 @@
         for z in range(CZ):
             for half, x in enumerate((gxr, gxs)):
                 lanes = pl.ds(CY * half, CY)
-                e[mid + z, HX : HX + CX, lanes] = (stack, peer)[half][CZ * f + z]
+                e[mid + z, HX : HX + CX, lanes] = (stack, peer)[half][f, z]
                 e[mid + z, HX - w : HX, lanes] = x[row : row + w]
                 e[mid + z, HX + CX : HX + CX + w, lanes] = x[row + w : row + 2 * w]
             row += 2 * w
@@ -614,10 +613,10 @@
     mine = (velocity, phase, phase_obs, velocity_obs)
     stack, edges, coefs, give = pl.pallas_call(
         load_kernel,
-        out_shape=(f32(8 * CZ, CX, CY), f32(EDGE_ROWS, CY), f32(4), f32(len(SENT), CX, CY)),
+        out_shape=(f32(8, CZ, CX, CY), f32(EDGE_ROWS, CY), f32(4), f32(len(SENT), CX, CY)),
         in_specs=[pl.BlockSpec(memory_space=pltpu.HBM)] * 5,
         out_specs=(VM,) * 4,
-        scratch_shapes=[pltpu.SemaphoreType.DMA((9,))],
+        scratch_shapes=[pltpu.SemaphoreType.DMA((5,))],
         compiler_params=PARAMS,
         name="load",
     )(*(pltpu.with_memory_space_constraint(a, pltpu.HBM) for a in (*mine, coefs)))

time: 71.6 us -> 71.5 us (level)
  no operation moved by 1% of the time
where the time goes in v9:
time: 71.5 us; the launch traced here: 71.4 us
  starting transfers between devices  34.4 us (48%)
  blocking collectives  15.5 us (22%)
  Pallas kernels  11.1 us (16%)
  waiting for transfers between devices  9.71 us (14%)
    ppermute x5, starting transfers between devices, role_shift(): return lax.ppermute(value, ('gx', 'gy', 'gz'), pairs)  22.9 us
    all_to_all x1, blocking collectives, local(): lax.all_to_all(sums.reshape(PARTNERS, 1, SLOTS), ('gx', 'gz'), 0, 0)  15.5 us
    pallas_call x7, Pallas kernels, call(): pl.pallas_call(kernel, out_shape=outs, in_specs=[SM] * smem + [VM] * (len...  9.91 us
    ppermute x10, starting transfers between devices, swap(): return lax.ppermute(value, 'gy', SWAP)  8.36 us
    ppermute x1, waiting for transfers between devices, local(): gxr = lax.ppermute(edges, 'gx', SWAP)  4.44 us
    ppermute x10, waiting for transfers between devices, swap(): return lax.ppermute(value, 'gy', SWAP)  2.73 us
    ppermute x1, waiting for transfers between devices, second_down(): return lax.ppermute(value, ('gx', 'gy', 'gz'), pairs)  2.02 us
    ppermute x1, starting transfers between devices, second_down(): return lax.ppermute(value, ('gx', 'gy', 'gz'), pairs)  1.91 us
  transfers between devices with their start and end apart: 18, of which 6 were waited for; matrix products, arithmetic and copies ran while one was open for 0% of the time, Pallas kernels for 6%

profile of v9, /device:TPU:1, one launch (start us, length us, event | category | flops | bytes accessed | tf_op | source)
XLA Modules:
  0.0 71.4 jit_solution(12012134860983417850)
XLA Ops:
  0.6 1.1 %load.1 = (f32[8,4,32,128]{3,2,1,0:T(8,128)S(1)}, f32[120,128]{1,0:T(8,128)S(1)}, f32[4]{0:T(128)S(1)}, f32[7,32,128]{2,1,0:T(8,128)S(1)}) custom-call(f32[3,4,32,128]{3,2,1,0:T(8,128)} %vel.1, f32[4,32,128]{2,1,0:T(8,128)} %ph.1, f32[4,32,128]{2,1,0:T(8,128)} %po.1, f32[3,4,32,128]{3,2,1,0:T(8,128)} %vo.1, f32[4]{0:T(128)} %coefs.1), custom_call_target="tpu_custom_call" | custom-call | tf_op jit(solution)/shard_map/load/pallas_call | solution.py:614
  1.8 3.3 %collective-permute-start.2 = (f32[7,32,128]{2,1,0:T(8,128)S(1)}, f32[7,32,128]{2,1,0:T(8,128)S(1)}, u32[]{:S(2)}, u32[]{:S(2)}) collective-permute-start(f32[7,32,128]{2,1,0:T(8,128)S(1)} %get-tuple-element.56), channel_id=1, source_target_pairs={{0,64},{64,0},{1,65},{65,1},{2,66},{66,2},{3,67},{67,3},{4,68},{68... | collective-permute-start | bytes 344072 | tf_op jit(solution)/shard_map/ppermute | solution.py:596
  5.2 0.9 %collective-permute-done.2.got = f32[7,32,128]{2,1,0:T(8,128)S(1)} collective-permute-done((f32[7,32,128]{2,1,0:T(8,128)S(1)}, f32[7,32,128]{2,1,0:T(8,128)S(1)}, u32[]{:S(2)}, u32[]{:S(2)}) %collective-permute-start.2) | collective-permute-done | bytes 114720 | tf_op jit(solution)/shard_map/ppermute | solution.py:596
  6.1 9.0 %collective-permute-start.3 = (f32[7,32,256]{2,1,0:T(8,128)S(1)}, f32[7,32,256]{2,1,0:T(8,128)S(1)}, u32[]{:S(2)}, u32[]{:S(2)}) collective-permute-start(f32[7,32,256]{2,1,0:T(8,128)S(1)} %get-tuple-element.57), channel_id=1, source_target_pairs={{0,1},{1,2},{2,3},{3,4},{4,5},{5,6},{6,7},{7,8},{8,9},{9,10},{10,1... | collective-permute-start | bytes 688136 | tf_op jit(solution)/shard_map/ppermute | solution.py:586
  15.1 0.7 %collective-permute-start.1 = (f32[120,128]{1,0:T(8,128)S(1)}, f32[120,128]{1,0:T(8,128)S(1)}, u32[]{:S(2)}, u32[]{:S(2)}) collective-permute-start(f32[120,128]{1,0:T(8,128)S(1)} %get-tuple-element.55), channel_id=1, source_target_pairs={{0,128},{128,0},{1,129},{129,1},{2,130},{130,2},{3,131},{131,3},{4... | collective-permute-start | bytes 184328 | tf_op jit(solution)/shard_map/ppermute | solution.py:624
  15.9 4.4 %collective-permute-done.1.gxr = f32[120,128]{1,0:T(8,128)S(1)} collective-permute-done((f32[120,128]{1,0:T(8,128)S(1)}, f32[120,128]{1,0:T(8,128)S(1)}, u32[]{:S(2)}, u32[]{:S(2)}) %collective-permute-start.1) | collective-permute-done | bytes 61472 | tf_op jit(solution)/shard_map/ppermute | solution.py:624
  20.4 0.5 collective-permute-done.4.dr
  20.9 1.1 %collective-permute-start.6 = (f32[7,32,256]{2,1,0:T(8,128)S(1)}, f32[7,32,256]{2,1,0:T(8,128)S(1)}, u32[]{:S(2)}, u32[]{:S(2)}) collective-permute-start(f32[7,32,256]{2,1,0:T(8,128)S(1)} %collective-permute-done.3.mr), channel_id=1, source_target_pairs={{0,64},{64,0},{1,65},{65,1},{2,66},{66,2},{3,67},{67,3},{4,68},{68... | collective-permute-start | bytes 688136 | tf_op jit(solution)/shard_map/ppermute | solution.py:596
  21.9 0.5 collective-permute-start.7
  22.4 0.7 %collective-permute-done.5.gxs = f32[120,128]{1,0:T(8,128)S(1)} collective-permute-done((f32[120,128]{1,0:T(8,128)S(1)}, f32[120,128]{1,0:T(8,128)S(1)}, u32[]{:S(2)}, u32[]{:S(2)}) %collective-permute-start.5) | collective-permute-done | bytes 61472 | tf_op jit(solution)/shard_map/ppermute | solution.py:596
  23.3 1.7 %first.1 = (f32[46,48,256]{2,1,0:T(8,128)S(1)}, f32[4,32,256]{2,1,0:T(8,128)S(1)}, f32[4,32,256]{2,1,0:T(8,128)S(1)}, f32[192,256]{1,0:T(8,128)S(1)}, f32[34,256...) custom-call(f32[4]{0:T(128)S(1)} %get-tuple-element.53.coefs, ...), custom_call_target="tpu_custom_call", output_to_operand_aliasing={{0}: (1, {})} | custom-call | tf_op jit(solution)/shard_map/first/pallas_call | solution.py:600
  25.0 7.4 %collective-permute-start.8 = (f32[192,256]{1,0:T(8,128)S(1)}, f32[192,256]{1,0:T(8,128)S(1)}, u32[]{:S(2)}, u32[]{:S(2)}) collective-permute-start(f32[192,256]{1,0:T(8,128)S(1)} %get-tuple-element.64), channel_id=1, source_target_pairs={{0,1},{1,2},{2,3},{3,4},{4,5},{5,6},{6,7},{7,8},{8,9},{9,10},{10,1... | collective-permute-start | bytes 589832 | tf_op jit(solution)/shard_map/ppermute | solution.py:586
  32.4 0.5 collective-permute-start.10
  32.9 1.9 %collective-permute-start.11 = (f32[32,256]{1,0:T(8,128)S(1)}, f32[32,256]{1,0:T(8,128)S(1)}, u32[]{:S(2)}, u32[]{:S(2)}) collective-permute-start(f32[32,256]{1,0:T(8,128)S(1)} %get-tuple-element.67), channel_id=1, source_target_pairs={{0,0},{1,1},{2,2},{3,3},{4,4},{5,5},{6,6},{7,7},{8,8},{9,9},{10,10... | collective-permute-start | bytes 98312 | tf_op jit(solution)/shard_map/ppermute | solution.py:592
  34.8 2.5 %weights.1 = (f32[4,48,256]{2,1,0:T(8,128)S(1)}, f32[3,4,32,256]{3,2,1,0:T(8,128)S(1)}, f32[5,8,128]{2,1,0:T(8,128)S(1)}, f32[130,256]{1,0:T(8,128)S(1)}, f32[3,...) custom-call(f32[4]{0:T(128)S(1)} %get-tuple-element.53.coefs, ...), custom_call_target="tpu_custom_call" | custom-call | tf_op jit(solution)/shard_map/weights/pallas_call | solution.py:600
  37.3 2.0 %collective-permute-done.11.far = f32[32,256]{1,0:T(8,128)S(1)} collective-permute-done((f32[32,256]{1,0:T(8,128)S(1)}, f32[32,256]{1,0:T(8,128)S(1)}, u32[]{:S(2)}, u32[]{:S(2)}) %collective-permute-start.11) | collective-permute-done | bytes 32800 | tf_op jit(solution)/shard_map/ppermute | solution.py:592
  39.3 1.1 %collective-permute-start.12 = (f32[192,256]{1,0:T(8,128)S(1)}, f32[192,256]{1,0:T(8,128)S(1)}, u32[]{:S(2)}, u32[]{:S(2)}) collective-permute-start(f32[192,256]{1,0:T(8,128)S(1)} %collective-permute-done.8.r), channel_id=1, source_target_pairs={{0,64},{64,0},{1,65},{65,1},{2,66},{66,2},{3,67},{67,3},{4,68},{68... | collective-permute-start | bytes 589832 | tf_op jit(solution)/shard_map/ppermute | solution.py:596
  41.0 1.1 %collective-permute-done.15.fars = f32[32,256]{1,0:T(8,128)S(1)} collective-permute-done((f32[32,256]{1,0:T(8,128)S(1)}, f32[32,256]{1,0:T(8,128)S(1)}, u32[]{:S(2)}, u32[]{:S(2)}) %collective-permute-start.15) | collective-permute-done | bytes 32800 | tf_op jit(solution)/shard_map/ppermute | solution.py:596
  42.2 2.0 %moments.1 = (f32[128,64]{1,0:T(8,128)S(1)}, f32[13,48,256]{2,1,0:T(8,128)S(1)}, f32[8,48,256]{2,1,0:T(8,128)S(1)}, f32[9,48,256]{2,1,0:T(8,128)S(1)}, f32[7,48,...) custom-call(f32[4,32,256]{2,1,0:T(8,128)S(1)} %get-tuple-element.62., ...), custom_call_target="tpu_custom_call" | custom-call | tf_op jit(solution)/shard_map/moments/pallas_call | solution.py:600
  44.1 6.4 %collective-permute-start.16 = (f32[264,256]{1,0:T(8,128)S(1)}, f32[264,256]{1,0:T(8,128)S(1)}, u32[]{:S(2)}, u32[]{:S(2)}) collective-permute-start(f32[264,256]{1,0:T(8,128)S(1)} %get-tuple-element.79), channel_id=1, source_target_pairs={{0,1},{1,2},{2,3},{3,4},{4,5},{5,6},{6,7},{7,8},{8,9},{9,10},{10,1... | collective-permute-start | bytes 811016 | tf_op jit(solution)/shard_map/ppermute | solution.py:586
  50.5 15.5 %all_to_all.5 = f32[128,1,64]{2,1,0:T(1,128)S(1)} all-to-all(f32[128,1,64]{2,1,0:T(1,128)S(1)} %bitcast.5), channel_id=1, replica_groups=mesh['gx'=2,'gy'=2,'gz'=64] {'gx','gz'}, dimensions={0} | all-to-all | bytes 65536 | tf_op jit(solution)/shard_map/all_to_all | solution.py:676
  66.0 1.7 %collective-permute-start.17 = (f32[264,256]{1,0:T(8,128)S(1)}, f32[264,256]{1,0:T(8,128)S(1)}, u32[]{:S(2)}, u32[]{:S(2)}) collective-permute-start(f32[264,256]{1,0:T(8,128)S(1)} %collective-permute-done.16.ri), channel_id=1, source_target_pairs={{0,64},{64,0},{1,65},{65,1},{2,66},{66,2},{3,67},{67,3},{4,68},{68... | collective-permute-start | bytes 811016 | tf_op jit(solution)/shard_map/ppermute | solution.py:596
  67.7 1.9 %near.1 = (f32[4]{0:T(128)}, f32[8,128]{1,0:T(8,128)S(1)}, f32[4,48,256]{2,1,0:T(8,128)S(1)}, f32[4,2,48,256]{3,2,1,0:T(8,128)S(1)}, f32[4,2,32,128]{3,2,1,0:T(8,128)S(1)}) custom-call(f32[4]{0:T(128)S(1)} %get-tuple-element.53.coefs, f32[128,64]{1,0:T(8,128)S(1)} %bitcast.4, f32[8,48,256]{2,1,0:T(8,128)S(1)} %get-tuple-element.82.uu, ...), custom_call_target="tpu_custom_call" | custom-call | tf_op jit(solution)/shard_map/near/pallas_call | solution.py:600
  69.6 1.8 %far.1 = (f32[4,32,128]{2,1,0:T(8,128)}, f32[3,4,32,128]{3,2,1,0:T(8,128)}) custom-call(f32[4]{0:T(128)S(1)} %get-tuple-element.53.coefs, f32[8,128]{1,0:T(8,128)S(1)} %get-tuple-element.96.table, f32[8,48,256]{2,1,0:T(8,128)S(1)} %get-tuple-element.82.uu, f32[9,48,256]{2,1,0:T(8,128)S(1)} %get-tuple-element.83.f, f32[7,48,256]{2,1,0:T(8,128)S(1)} %get-tuple-element.84.af, ...), custom_call_target="tpu_custom_call" | custom-call | tf_op jit(solution)/shard_map/far/pallas_call | solution.py:600
  (21 shorter events, 1.0 us)
Async XLA Ops:
  1.8 4.3 %collective-permute-start.2 = (f32[7,32,128]{2,1,0:T(8,128)S(1)}, f32[7,32,128]{2,1,0:T(8,128)S(1)}, u32[]{:S(2)}, u32[]{:S(2)}) collective-permute-start(f32[7,32,128]{2,1,0:T(8,128)S(1)} %get-tuple-element.56), channel_id=1, source_target_pairs={{0,64},{64,0},{1,65},{65,1},{2,66},{66,2},{3,67},{67,3},{4,68},{68... | collective-permute-start | bytes 344072 | tf_op jit(solution)/shard_map/ppermute | solution.py:596
  5.1 18.1 %collective-permute-start = (f32[8,4,32,128]{3,2,1,0:T(8,128)S(1)}, f32[8,4,32,128]{3,2,1,0:T(8,128)S(1)}, u32[]{:S(2)}, u32[]{:S(2)}) collective-permute-start(f32[8,4,32,128]{3,2,1,0:T(8,128)S(1)} %get-tuple-element.54.stack), channel_id=1, source_target_pairs={{0,64},{64,0},{1,65},{65,1},{2,66},{66,2},{3,67},{67,3},{4,68},{68... | collective-permute-start | bytes 1572872 | tf_op jit(solution)/shard_map/ppermute | solution.py:596
  6.1 14.8 %collective-permute-start.3 = (f32[7,32,256]{2,1,0:T(8,128)S(1)}, f32[7,32,256]{2,1,0:T(8,128)S(1)}, u32[]{:S(2)}, u32[]{:S(2)}) collective-permute-start(f32[7,32,256]{2,1,0:T(8,128)S(1)} %get-tuple-element.57), channel_id=1, source_target_pairs={{0,1},{1,2},{2,3},{3,4},{4,5},{5,6},{6,7},{7,8},{8,9},{9,10},{10,1... | collective-permute-start | bytes 688136 | tf_op jit(solution)/shard_map/ppermute | solution.py:586
  15.1 5.3 %collective-permute-start.1 = (f32[120,128]{1,0:T(8,128)S(1)}, f32[120,128]{1,0:T(8,128)S(1)}, u32[]{:S(2)}, u32[]{:S(2)}) collective-permute-start(f32[120,128]{1,0:T(8,128)S(1)} %get-tuple-element.55), channel_id=1, source_target_pairs={{0,128},{128,0},{1,129},{129,1},{2,130},{130,2},{3,131},{131,3},{4... | collective-permute-start | bytes 184328 | tf_op jit(solution)/shard_map/ppermute | solution.py:624
  15.8 5.0 %collective-permute-start.4 = (f32[16,256]{1,0:T(8,128)S(1)}, f32[16,256]{1,0:T(8,128)S(1)}, u32[]{:S(2)}, u32[]{:S(2)}) collective-permute-start(f32[16,256]{1,0:T(8,128)S(1)} %get-tuple-element.58), channel_id=1, source_target_pairs={{0,129},{1,130},{2,131},{3,132},{4,133},{5,134},{6,135},{7,136},{8... | collective-permute-start | bytes 49160 | tf_op jit(solution)/shard_map/ppermute | solution.py:586
  20.9 2.4 %collective-permute-start.6 = (f32[7,32,256]{2,1,0:T(8,128)S(1)}, f32[7,32,256]{2,1,0:T(8,128)S(1)}, u32[]{:S(2)}, u32[]{:S(2)}) collective-permute-start(f32[7,32,256]{2,1,0:T(8,128)S(1)} %collective-permute-done.3.mr), channel_id=1, source_target_pairs={{0,64},{64,0},{1,65},{65,1},{2,66},{66,2},{3,67},{67,3},{4,68},{68... | collective-permute-start | bytes 688136 | tf_op jit(solution)/shard_map/ppermute | solution.py:596
  21.9 1.2 %collective-permute-start.5 = (f32[120,128]{1,0:T(8,128)S(1)}, f32[120,128]{1,0:T(8,128)S(1)}, u32[]{:S(2)}, u32[]{:S(2)}) collective-permute-start(f32[120,128]{1,0:T(8,128)S(1)} %collective-permute-done.1.gxr), channel_id=1, source_target_pairs={{0,64},{64,0},{1,65},{65,1},{2,66},{66,2},{3,67},{67,3},{4,68},{68... | collective-permute-start | bytes 184328 | tf_op jit(solution)/shard_map/ppermute | solution.py:596
  21.9 1.4 %collective-permute-start.7 = (f32[16,256]{1,0:T(8,128)S(1)}, f32[16,256]{1,0:T(8,128)S(1)}, u32[]{:S(2)}, u32[]{:S(2)}) collective-permute-start(f32[16,256]{1,0:T(8,128)S(1)} %collective-permute-done.4.dr), channel_id=1, source_target_pairs={{0,64},{64,0},{1,65},{65,1},{2,66},{66,2},{3,67},{67,3},{4,68},{68... | collective-permute-start | bytes 49160 | tf_op jit(solution)/shard_map/ppermute | solution.py:596
  25.0 14.3 %collective-permute-start.8 = (f32[192,256]{1,0:T(8,128)S(1)}, f32[192,256]{1,0:T(8,128)S(1)}, u32[]{:S(2)}, u32[]{:S(2)}) collective-permute-start(f32[192,256]{1,0:T(8,128)S(1)} %get-tuple-element.64), channel_id=1, source_target_pairs={{0,1},{1,2},{2,3},{3,4},{4,5},{5,6},{6,7},{7,8},{8,9},{9,10},{10,1... | collective-permute-start | bytes 589832 | tf_op jit(solution)/shard_map/ppermute | solution.py:586
  32.4 6.9 %collective-permute-start.10 = (f32[72,128]{1,0:T(8,128)S(1)}, f32[72,128]{1,0:T(8,128)S(1)}, u32[]{:S(2)}, u32[]{:S(2)}) collective-permute-start(f32[72,128]{1,0:T(8,128)S(1)} %get-tuple-element.66), channel_id=1, source_target_pairs={{0,128},{128,0},{1,129},{129,1},{2,130},{130,2},{3,131},{131,3},{4... | collective-permute-start | bytes 110600 | tf_op jit(solution)/shard_map/ppermute | solution.py:652
  32.9 6.5 %collective-permute-start.9 = (f32[34,256]{1,0:T(8,128)S(1)}, f32[34,256]{1,0:T(8,128)S(1)}, u32[]{:S(2)}, u32[]{:S(2)}) collective-permute-start(f32[34,256]{1,0:T(8,128)S(1)} %get-tuple-element.65), channel_id=1, source_target_pairs={{0,129},{1,130},{2,131},{3,132},{4,133},{5,134},{6,135},{7,136},{8... | collective-permute-start | bytes 104456 | tf_op jit(solution)/shard_map/ppermute | solution.py:586
  32.9 6.4 %collective-permute-start.11 = (f32[32,256]{1,0:T(8,128)S(1)}, f32[32,256]{1,0:T(8,128)S(1)}, u32[]{:S(2)}, u32[]{:S(2)}) collective-permute-start(f32[32,256]{1,0:T(8,128)S(1)} %get-tuple-element.67), channel_id=1, source_target_pairs={{0,0},{1,1},{2,2},{3,3},{4,4},{5,5},{6,6},{7,7},{8,8},{9,9},{10,10... | collective-permute-start | bytes 98312 | tf_op jit(solution)/shard_map/ppermute | solution.py:592
  39.3 2.8 %collective-permute-start.12 = (f32[192,256]{1,0:T(8,128)S(1)}, f32[192,256]{1,0:T(8,128)S(1)}, u32[]{:S(2)}, u32[]{:S(2)}) collective-permute-start(f32[192,256]{1,0:T(8,128)S(1)} %collective-permute-done.8.r), channel_id=1, source_target_pairs={{0,64},{64,0},{1,65},{65,1},{2,66},{66,2},{3,67},{67,3},{4,68},{68... | collective-permute-start | bytes 589832 | tf_op jit(solution)/shard_map/ppermute | solution.py:596
  40.4 1.7 %collective-permute-start.14 = (f32[72,128]{1,0:T(8,128)S(1)}, f32[72,128]{1,0:T(8,128)S(1)}, u32[]{:S(2)}, u32[]{:S(2)}) collective-permute-start(f32[72,128]{1,0:T(8,128)S(1)} %collective-permute-done.10.x), channel_id=1, source_target_pairs={{0,64},{64,0},{1,65},{65,1},{2,66},{66,2},{3,67},{67,3},{4,68},{68... | collective-permute-start | bytes 110600 | tf_op jit(solution)/shard_map/ppermute | solution.py:596
  40.5 1.6 %collective-permute-start.13 = (f32[34,256]{1,0:T(8,128)S(1)}, f32[34,256]{1,0:T(8,128)S(1)}, u32[]{:S(2)}, u32[]{:S(2)}) collective-permute-start(f32[34,256]{1,0:T(8,128)S(1)} %collective-permute-done.9.d), channel_id=1, source_target_pairs={{0,64},{64,0},{1,65},{65,1},{2,66},{66,2},{3,67},{67,3},{4,68},{68... | collective-permute-start | bytes 104456 | tf_op jit(solution)/shard_map/ppermute | solution.py:596
  40.9 1.2 %collective-permute-start.15 = (f32[32,256]{1,0:T(8,128)S(1)}, f32[32,256]{1,0:T(8,128)S(1)}, u32[]{:S(2)}, u32[]{:S(2)}) collective-permute-start(f32[32,256]{1,0:T(8,128)S(1)} %collective-permute-done.11.far), channel_id=1, source_target_pairs={{0,64},{64,0},{1,65},{65,1},{2,66},{66,2},{3,67},{67,3},{4,68},{68... | collective-permute-start | bytes 98312 | tf_op jit(solution)/shard_map/ppermute | solution.py:596
  44.1 21.9 %collective-permute-start.16 = (f32[264,256]{1,0:T(8,128)S(1)}, f32[264,256]{1,0:T(8,128)S(1)}, u32[]{:S(2)}, u32[]{:S(2)}) collective-permute-start(f32[264,256]{1,0:T(8,128)S(1)} %get-tuple-element.79), channel_id=1, source_target_pairs={{0,1},{1,2},{2,3},{3,4},{4,5},{5,6},{6,7},{7,8},{8,9},{9,10},{10,1... | collective-permute-start | bytes 811016 | tf_op jit(solution)/shard_map/ppermute | solution.py:586
  66.0 3.5 %collective-permute-start.17 = (f32[264,256]{1,0:T(8,128)S(1)}, f32[264,256]{1,0:T(8,128)S(1)}, u32[]{:S(2)}, u32[]{:S(2)}) collective-permute-start(f32[264,256]{1,0:T(8,128)S(1)} %collective-permute-done.16.ri), channel_id=1, source_target_pairs={{0,64},{64,0},{1,65},{65,1},{2,66},{66,2},{3,67},{67,3},{4,68},{68... | collective-permute-start | bytes 811016 | tf_op jit(solution)/shard_map/ppermute | solution.py:596
